TPU v7x, 128 devices: a whole 4x4x4 slice. The times are simulated.
128 devices in a mesh: grp: 4 (over y), fsdp: 32 (over x, z, core).
Axes of the slice: x: 4, y: 4, z: 4, core: 2. Of those that a mesh axis runs over, the one named last changes fastest.
Arguments:
- tokens: bfloat16 [65536, 8192], P(('grp', 'fsdp')), may hold values from -6 to 6
- frozen_key_weight: bfloat16 [8192, 1024], P('fsdp'), may hold values from -0.0625 to 0.0625
- adapter_down: bfloat16 [8192, 512], replicated, may hold values from -0.0625 to 0.0625
- adapter_up: bfloat16 [1024, 512], replicated, may hold values from -0.75 to 0.75
- key_cotangent: bfloat16 [65536, 1024], P(('grp', 'fsdp')), may hold values from -24 to 24
- token_tasks: int32 [65536], P(('grp', 'fsdp')), may hold values from 0 to 7, never falling along the last dimension, each value on 1 to 16384 neighbouring positions
- owned: int32 [8], replicated, may hold values from 0 to 7, each once
- counts: int32 [8], replicated, may hold values from 32 to 128
Outputs:
- keys: bfloat16 [65536, 1024], P(('grp', 'fsdp'))
- grad_down: float32 [4, 8192, 128], P('grp', 'fsdp')
- grad_up: float32 [4, 1024, 128], P('grp', 'fsdp')
Inputs may be any that keep to these rules, and one draw needn't show every extreme that they name: `token_tasks`: task ids never decrease along the tokens; every task has one token or more, and one task has exactly 16384. `owned`: every adapter appears once.
All inputs are finite; a program needn't handle non-finite values.
Results may differ from a plain program's by a relative error of at most 0.013.
Values may be sent and summed in bfloat16 or wider, within the bound.
No kernel may reach another device: no remote copies, remote signals or barrier semaphores. Data moves between devices by JAX's collectives and lax.ppermute only.
A program may use at most 192 MiB of HBM per device.

v0:
```python
import jax
import jax.numpy as jnp
from jax import lax
from jax.sharding import PartitionSpec as P

ADAPTER_RANK = 64


ADAPTER_SCALE = 0.5


def owner_columns(owned, rank):
    return (owned[:, None] * rank + jnp.arange(rank, dtype=jnp.int32)[None, :]).reshape(-1)


def token_masks(token_tasks, owned, counts, rank):
    adapters = owned.shape[0]
    owner_hit = (token_tasks[:, None] == owned[None, :]).astype(jnp.float32)
    column_mask = jnp.repeat(owner_hit, rank, axis=1)
    task_hot = (token_tasks[:, None] == jnp.arange(adapters, dtype=jnp.int32)[None, :]).astype(
        jnp.float32
    )
    token_adapter_mask = jnp.sum(task_hot * counts.astype(jnp.float32)[None, :], axis=1)
    return (column_mask, ADAPTER_SCALE / token_adapter_mask)


def per_device(
    tokens, frozen_key_weight, adapter_down, adapter_up, key_cotangent, token_tasks, owned, counts
):
    tok_rows, width = tokens.shape
    kv_width = frozen_key_weight.shape[1]
    column_position = owner_columns(owned, ADAPTER_RANK)
    down_selected = jnp.take(adapter_down, column_position, axis=1)
    up_selected = jnp.take(adapter_up, column_position, axis=1)
    column_mask, token_weight = token_masks(token_tasks, owned, counts, ADAPTER_RANK)
    frozen_keys = jnp.dot(
        tokens,
        lax.all_gather(frozen_key_weight, "fsdp", axis=0, tiled=True),
        preferred_element_type=jnp.float32,
    )
    hidden = (
        jnp.dot(tokens, down_selected, preferred_element_type=jnp.float32) * column_mask
    ).astype(jnp.bfloat16)
    adapted_keys = lax.dot_general(
        hidden, up_selected, (((1,), (1,)), ((), ())), preferred_element_type=jnp.float32
    )
    keys = (frozen_keys + ADAPTER_SCALE * adapted_keys).astype(jnp.bfloat16)
    scaled = (key_cotangent.astype(jnp.float32) * token_weight[:, None]).astype(jnp.bfloat16)
    low_grad = (
        jnp.dot(scaled, up_selected, preferred_element_type=jnp.float32) * column_mask
    ).astype(jnp.bfloat16)
    groups = lax.axis_size("grp")
    slot_width = column_position.shape[0] // groups
    down_term = jnp.einsum(
        "td,tgk->gdk",
        tokens,
        low_grad.reshape(tok_rows, groups, slot_width),
        preferred_element_type=jnp.float32,
    )
    up_term = jnp.einsum(
        "tv,tgk->gvk",
        scaled,
        hidden.reshape(tok_rows, groups, slot_width),
        preferred_element_type=jnp.float32,
    )
    down_part, up_part = (
        lax.psum_scatter(
            down_term.reshape(groups * width, slot_width),
            ("grp", "fsdp"),
            scatter_dimension=0,
            tiled=True,
        ),
        lax.psum_scatter(
            up_term.reshape(groups * kv_width, slot_width),
            ("grp", "fsdp"),
            scatter_dimension=0,
            tiled=True,
        ),
    )
    return (keys, down_part.reshape(1, -1, slot_width), up_part.reshape(1, -1, slot_width))


def solution(mesh):
    in_specs = (
        P(("grp", "fsdp"), None),
        P("fsdp", None),
        P(),
        P(),
        P(("grp", "fsdp"), None),
        P(("grp", "fsdp")),
        P(),
        P(),
    )
    out_specs = (P(("grp", "fsdp"), None), P("grp", "fsdp", None), P("grp", "fsdp", None))
    return jax.shard_map(
        per_device, mesh=mesh, in_specs=in_specs, out_specs=out_specs, check_vma=False
    )
```

profile of v0, /device:TPU:0, one launch (start us, length us, event | category | flops | bytes accessed | tf_op | source)
XLA Modules:
  0.0 1381.9 jit_solution(1392401250796098492)
XLA Ops:
  8.0 0.0 all-gather.2.cloned.1.call-start
  8.0 0.7 all-gather.2.cloned.1.call-update
  8.7 0.0 reduce-scatter.5.cloned.1.call-start
  8.8 0.7 broadcast_multiply_fusion
  9.4 0.1 iota_add_fusion
  9.5 0.1 add.64
  9.6 0.1 add.67
  9.7 0.0 copy-start.3
  9.7 11.8 copy.13
  21.5 0.0 copy-done.3
  21.5 0.0 copy-start.1
  21.6 0.0 copy-start.2
  21.6 20.4 %gather_fusion = bf16[512,8192]{1,0:T(8,128)(2,1)} fusion(bf16[8192,512]{0,1:T(8,128)(2,1)} %copy.13, s32[1024]{0:T(1024)S(1)} %pad_clamp_fusion), kind=kCustom, calls=%fused_computation | custom fusion | bytes 16779264 | tf_op jit(solution)/shard_map/jit(_take)/gather | solution.py:33
  42.0 0.0 copy-done.1
  42.0 0.0 copy-done.2
  42.0 0.1 compare_convert_fusion
  42.1 0.0 copy-start
  42.1 11.2 fusion.11
  53.3 0.1 select_reduce_fusion
  53.3 0.0 copy-done
  53.4 0.8 convolution_bitcast_fusion.1
  54.2 1.9 copy.16
  56.0 0.0 reduce-scatter.5.cloned.1.call-update
  56.1 0.0 reduce-scatter.3.cloned.1.call-start
  56.1 1.5 copy.14
  57.6 2.1 gather_fusion.1
  59.7 2.1 fusion.10
  61.8 12.3 convolution_bitcast_fusion
  74.0 17.6 %copy.15 = f32[4,8192,128]{2,1,0:T(8,128)} copy(f32[4,8192,128]{1,2,0:T(8,128)} %convolution_bitcast_fusion) | data formatting | bytes 33554432 | tf_op jit(solution)/shard_map/td,tgk->gdk/transpose | solution.py:54
  91.6 0.0 reduce-scatter.3.cloned.1.call-update
  91.6 2.1 fusion.15
  93.7 0.0 all-gather.2.cloned.1.call-done
  93.8 15.9 %add_convert_fusion = bf16[512,1024]{1,0:T(8,128)(2,1)} fusion(f32[512,1024]{1,0:T(8,128)} %fusion.15, bf16[512,8192]{1,0:T(8,128)(2,1)} %param.8, bf16[8192,1024]{1,0:T(8,128)(2,1)} %all-gather.2.cloned.1.call-done), kind=kOutput, calls=%fused_computation.9 | convolution fusion | flops 8591507456 | bytes 28311552 | tf_op jit(solution)/shard_map/dot_general | solution.py:36
  109.6 597.1 %reduce-scatter.5.cloned.1.call-done = f32[32,128]{1,0:T(8,128)} async-done(((f32[4096,128]{1,0:T(8,128)}), f32[32,128]{1,0:T(8,128)}) %reduce-scatter.5.cloned.1.call-update) | async-done | bytes 16400 | tf_op jit(solution)/shard_map/reduce_scatter | solution.py:73
  706.7 667.7 %reduce-scatter.3.cloned.1.call-done = f32[256,128]{1,0:T(8,128)} async-done(((f32[32768,128]{1,0:T(8,128)}), f32[256,128]{1,0:T(8,128)}) %reduce-scatter.3.cloned.1.call-update) | async-done | bytes 131088 | tf_op jit(solution)/shard_map/reduce_scatter | solution.py:67
  (5 shorter events, 0.0 us)
Async XLA Ops:
  8.0 85.8 %all-gather.2.cloned.1.call-start = ((), (), s32[]{:S(2)}) async-start(), calls=%async_computation.2 | async-start | bytes 17301504 | tf_op jit(solution)/shard_map/all_gather | solution.py:38
  8.7 698.0 %reduce-scatter.5.cloned.1.call-start = ((), (), s32[]{:S(2)}) async-start(), calls=%async_computation.4 | async-start | bytes 2113536 | tf_op jit(solution)/shard_map/reduce_scatter | solution.py:73
  9.7 11.8 copy-start.3
  21.5 20.4 %copy-start.1 = (s32[512]{0:T(512)S(1)}, s32[512]{0:T(512)}, u32[]{:S(2)}) copy-start(s32[512]{0:T(512)} %param.13) | copy-start | bytes 6148
  21.6 20.4 %copy-start.2 = (s32[8]{0:T(128)S(1)}, s32[8]{0:T(128)}, u32[]{:S(2)}) copy-start(s32[8]{0:T(128)} %param.14) | copy-start | bytes 100
  42.1 11.3 copy-start
  56.1 1318.4 %reduce-scatter.3.cloned.1.call-start = ((), (), s32[]{:S(2)}) async-start(), calls=%async_computation.3 | async-start | bytes 16908288 | tf_op jit(solution)/shard_map/reduce_scatter | solution.py:67
Sparse Core Ops, SparseCore 0:
  11.1 75.1 all-gather.1
Sparse Core Ops, SparseCore 1:
  56.1 650.5 reduce-scatter.4
  709.7 664.7 reduce-scatter.2
where the time goes:
time: 1380 us
  waiting for transfers between devices  1270 us (92%)
  local copies, waits for them, and re-layouts  55.4 us (4%)
  matrix products  44.3 us (3%)
  between operations  15.6 us (1%)
    reduce_scatter x1, waiting for transfers between devices, per_device(): lax.psum_scatter(down_term.reshape(groups * width, slot_width), ('grp', '...  668 us
    reduce_scatter x1, waiting for transfers between devices, per_device(): lax.psum_scatter(up_term.reshape(groups * kv_width, slot_width), ('grp',...  597 us
  transfers between devices with their start and end apart: 3, of which 2 were waited for; matrix products, arithmetic and copies ran while one was open for 7% of the time, Pallas kernels for 0%

commit v1 on v0

v1 whole, which is shorter than its diff:
```python
import jax
import jax.numpy as jnp
from jax import lax
from jax.sharding import Mesh, PartitionSpec as P

RANK = 64
SCALE = 0.5
BF = jnp.bfloat16
F32 = jnp.float32
SLOTS = 4
INFO = 16


def dot(a, b, dims=((1,), (0,))):
    return lax.dot_general(a, b, (dims, ((), ())), preferred_element_type=F32)


def exchange(a, axis):
    return lax.all_to_all(a, axis, 0, 0, tiled=True)


def info_rows(rows, width, flag):
    row = lax.broadcasted_iota(jnp.int32, (INFO, width), 0)
    return jnp.where(row == 0, rows[None, :], jnp.where(row == 1, flag, 0.0)).astype(BF)


def per_device(tokens, weight, down, up, cotangent, tasks, owned, counts):
    n_tok, width = tokens.shape
    kv = weight.shape[1]
    adapters = owned.shape[0]
    cols = adapters * RANK
    ny, nx, nz = lax.axis_size("y"), lax.axis_size("x"), lax.axis_size("z")
    me_c = lax.axis_index("c")
    d_rows, v_rows = width // (nx * nz * 2), kv // (nx * nz * 2)
    b_rows = d_rows + v_rows
    sc = SLOTS * RANK
    swap = [(0, 1), (1, 0)]

    full_weight = lax.all_gather(weight, ("x", "z", "c"), axis=0, tiled=True)

    ids = jnp.arange(adapters, dtype=jnp.int32)
    partner_tasks = lax.ppermute(tasks, "c", swap)
    hit = tasks[:, None] == ids[None, :]
    present = jnp.any(hit | (partner_tasks[:, None] == ids[None, :]), axis=0)
    rank_of = jnp.sum((ids[None, :] < ids[:, None]) & present[None, :], axis=1)
    col_slot = jnp.arange(sc, dtype=jnp.int32) // RANK
    col_rank = jnp.arange(sc, dtype=jnp.int32) % RANK
    chosen = present[None, :] & (rank_of[None, :] == col_slot[:, None])
    col_task = jnp.sum(jnp.where(chosen, ids[None, :] + 1, 0), axis=1) - 1
    overflow = (jnp.sum(present.astype(jnp.int32)) > SLOTS).astype(F32)

    row = jnp.arange(cols, dtype=jnp.int32)
    pick = ((row // RANK)[:, None] == col_task[None, :]) & ((row % RANK)[:, None] == col_rank[None, :])
    pick = pick.astype(BF)
    mask_full = (tasks[:, None] == (row // RANK)[None, :]).astype(F32)
    mask_slot = (tasks[:, None] == col_task[None, :]).astype(F32)

    token_count = jnp.sum(jnp.where(hit, counts.astype(F32)[None, :], 0.0), axis=1)
    scaled = (cotangent.astype(F32) * (SCALE / token_count)[:, None]).astype(BF)

    up_slot = dot(up, pick).astype(BF)
    low = (dot(scaled, up_slot) * mask_slot).astype(BF)
    hidden = (dot(tokens, down) * mask_full).astype(BF)
    hidden_slot = dot(hidden, pick).astype(BF)

    down_term = dot(tokens, low, ((0,), (0,))).reshape(nx, nz, 2, d_rows, sc)
    up_term = dot(scaled, hidden_slot, ((0,), (0,))).reshape(nx, nz, 2, v_rows, sc)
    term = jnp.concatenate([down_term, up_term], axis=3)
    theirs = lax.dynamic_index_in_dim(term, 1 - me_c, 2, keepdims=False).astype(BF)
    mine = lax.dynamic_index_in_dim(term, me_c, 2, keepdims=False)
    chip = (mine + lax.ppermute(theirs, "c", swap).astype(F32)).astype(BF)

    chip = jnp.transpose(chip, (1, 0, 2, 3)).reshape(nz, nx * b_rows, sc)
    note = jnp.broadcast_to(info_rows(col_task.astype(F32), sc, overflow)[None], (nz, INFO, sc))
    got = exchange(jnp.concatenate([chip, note], axis=1), "z")
    flag = jnp.max(got[:, nx * b_rows + 1, 0].astype(F32))
    sent_task = got[:, nx * b_rows, :].astype(F32)
    place = (sent_task[:, :, None] == owned[row // RANK].astype(F32)[None, None, :]) & (
        col_rank[None, :, None] == (row % RANK)[None, None, :]
    )
    spread = lax.dot_general(
        got[:, : nx * b_rows], place.astype(BF), (((2,), (1,)), ((0,), (0,))), preferred_element_type=F32
    ).sum(axis=0)

    own = cols // ny
    spread = jnp.transpose(spread.reshape(nx * b_rows, ny, own).astype(BF), (1, 0, 2))
    note = jnp.broadcast_to(info_rows(jnp.zeros((own,), F32), own, flag)[None], (ny, INFO, own))
    got = exchange(jnp.concatenate([spread, note], axis=1), "y").astype(F32)
    flag = jnp.max(got[:, nx * b_rows + 1, 0])
    part = got[:, : nx * b_rows].sum(axis=0).astype(BF).reshape(nx, b_rows, own)

    note = jnp.broadcast_to(info_rows(jnp.zeros((own,), F32), own, flag)[None], (nx, INFO, own))
    got = exchange(jnp.concatenate([part, note], axis=1), "x").astype(F32)
    flag = jnp.max(got[:, b_rows + 1, 0])
    total = got[:, :b_rows].sum(axis=0)
    grad_down, grad_up = total[:d_rows], total[d_rows:]

    keys = (dot(tokens, full_weight) + SCALE * dot(hidden, up, ((1,), (1,)))).astype(BF)

    flag, keys = lax.optimization_barrier((flag, keys))

    def rest(grads):
        left = (1.0 - jnp.sum(mask_slot, axis=1) / RANK)[:, None]
        order = ((row // RANK)[:, None] == owned[row // RANK][None, :]) & (
            (row % RANK)[:, None] == (row % RANK)[None, :]
        )
        order = order.astype(BF)
        low_left = (dot(scaled, up) * (mask_full * left)).astype(BF)
        low_left = dot(low_left, order).astype(BF)
        hid_left = dot((hidden * left).astype(BF), order).astype(BF)

        def summed(a, b):
            rows = a.shape[1]
            t = lax.dot_general(
                a, b.reshape(n_tok, ny, own), (((0,), (0,)), ((), ())), preferred_element_type=F32
            )
            t = jnp.transpose(t, (1, 0, 2)).reshape(ny * rows, own)
            for axis in ("y", "x", "z", "c"):
                t = lax.psum_scatter(t, axis, scatter_dimension=0, tiled=True)
            return t

        return grads[0] + summed(tokens, low_left), grads[1] + summed(scaled, hid_left)

    grad_down, grad_up = lax.cond(flag > 0.5, rest, lambda g: g, (grad_down, grad_up))
    return keys, grad_down[None], grad_up[None]


def solution(mesh):
    sizes = dict(mesh.shape)
    ny = sizes["grp"]
    nx = nz = int((sizes["fsdp"] // 2) ** 0.5)
    fine = Mesh(mesh.devices.reshape(ny, nx, nz, 2), ("y", "x", "z", "c"))
    fsdp = ("x", "z", "c")
    every = ("y", "x", "z", "c")
    in_specs = (P(every, None), P(fsdp, None), P(), P(), P(every, None), P(every), P(), P())
    out_specs = (P(every, None), P("y", fsdp, None), P("y", fsdp, None))
    return jax.shard_map(per_device, mesh=fine, in_specs=in_specs, out_specs=out_specs, check_vma=False)
```

time: 1380 us -> 186 us (0.13)
  waiting for transfers between devices: 1270 us -> 46.7 us
  other arithmetic: 0.92 us -> 31.7 us
  local copies, waits for them, and re-layouts: 55.4 us -> 32.1 us
  starting transfers between devices: 0.13 us -> 15.9 us
    reduce_scatter x2 -> x0, waiting for transfers between devices: 1260 us -> none  [the longest x1 668 us: per_device(): lax.psum_scatter(down_term.reshape(groups * width, slot_width), ('grp', '...]
    all_to_all x0 -> x3, waiting for transfers between devices: none -> 42.8 us  [exchange(): return lax.all_to_all(a, axis, 0, 0, tiled=True)]
    reshape x0 -> x2, local copies, waits for them, and re-layouts: none -> 25.1 us  [per_device(): down_term = dot(tokens, low, ((0,), (0,))).reshape(nx, nz, 2, d_rows, sc)]
    gather x2 -> x1, local copies, waits for them, and re-layouts: 22.5 us -> 0.69 us  [per_device(): owned[row // RANK].astype(F32)[None, None, :]]
    transpose x2 -> x1, local copies, waits for them, and re-layouts: 19.4 us -> 0.16 us  [per_device(): chip = jnp.transpose(chip, (1, 0, 2, 3)).reshape(nz, nx * b_rows, sc)]
    all_to_all x0 -> x3, starting transfers between devices: none -> 15.4 us  [exchange(): return lax.all_to_all(a, axis, 0, 0, tiled=True)]
    dot_general x6 -> x7, matrix products: 44.3 us -> 43 us  [the longest x6 39.3 us: dot(): return lax.dot_general(a, b, (dims, ((), ())), preferred_element_type=F32)]
  transfers between devices with their start and end apart: 3 -> 6, of which waited for: 2 -> 4; matrix products, arithmetic and copies ran while one was open for 7% -> 49% of each run, Pallas kernels for 0% -> 0%
where the time goes in v1:
time: 186 us; the launch traced here: 185 us
  waiting for transfers between devices  46.7 us (25%)
  matrix products  43 us (23%)
  local copies, waits for them, and re-layouts  32.1 us (17%)
  other arithmetic  31.7 us (17%)
  starting transfers between devices  15.9 us (9%)
  between operations  15.6 us (8%)
    all_to_all x3, waiting for transfers between devices, exchange(): return lax.all_to_all(a, axis, 0, 0, tiled=True)  42.8 us
    dot_general x6, matrix products, dot(): return lax.dot_general(a, b, (dims, ((), ())), preferred_element_type=F32)  39.3 us
    reshape x2, local copies, waits for them, and re-layouts, per_device(): down_term = dot(tokens, low, ((0,), (0,))).reshape(nx, nz, 2, d_rows, sc)  25.1 us
    all_to_all x3, starting transfers between devices, exchange(): return lax.all_to_all(a, axis, 0, 0, tiled=True)  15.4 us
    gather x2, other arithmetic, per_device(): owned[row // RANK].astype(F32)[None, None, :]  4.47 us
    convert_element_type x1, other arithmetic, per_device(): lax.dynamic_index_in_dim(term, 1 - me_c, 2, keepdims=False).astype(BF)  4.23 us
  transfers between devices with their start and end apart: 6, of which 4 were waited for; matrix products, arithmetic and copies ran while one was open for 49% of the time, Pallas kernels for 0%

profile of v1, /device:TPU:0, one launch (start us, length us, event | category | flops | bytes accessed | tf_op | source)
XLA Modules:
  0.0 184.9 jit_solution(1983182839077782648)
XLA Ops:
  7.2 0.7 all-gather.2.cloned.1.call-update
  8.0 0.7 convert_element_type.140
  8.7 0.8 select_reduce_fusion
  9.4 1.5 multiply_convert_fusion.2
  10.9 10.3 %fusion.31 = bf16[512,512]{1,0:T(8,128)(2,1)S(1)} fusion(bf16[512,8192]{1,0:T(8,128)(2,1)} %param.10, bf16[8192,512]{1,0:T(8,128)(2,1)} %param.12, s32[512]{0:T(512)S(1)} %get-tuple-element.86, s32[512]{0:T(512)S(1)} %copy-done.9), kind=kOutput, calls=%fused_computation.69 | convolution fusion | flops 4295753728 | bytes 17305600 | tf_op jit(solution)/shard_map/dot_general | solution.py:15
  21.3 0.1 fusion.59
  21.4 0.1 convert_reduce_fusion
  21.7 1.1 fusion.34
  22.8 9.2 %convolution_bitcast_fusion.2 = f32[8192,256]{0,1:T(8,128)} fusion(bf16[512,256]{1,0:T(8,128)(2,1)S(1)} %fusion.34, bf16[512,8192]{1,0:T(8,128)(2,1)} %param.10), kind=kOutput, calls=%fused_computation.46 | convolution fusion | flops 2147483648 | bytes 17039360 | tf_op jit(solution)/shard_map/dot_general | solution.py:15
  32.0 11.8 %reshape.289 = f32[4,4,2,256,256]{3,2,1,0,4:T(2,128)} reshape(f32[8192,256]{0,1:T(8,128)} %convolution_bitcast_fusion.2) | data formatting | bytes 16777216 | tf_op jit(solution)/shard_map/reshape | solution.py:66
  43.7 13.4 %copy.38 = f32[4,4,2,256,256]{4,3,1,0,2:T(8,128)} copy(f32[4,4,2,256,256]{3,2,1,0,4:T(2,128)} %reshape.289) | data formatting | bytes 16777216 | tf_op jit(solution)/shard_map/reshape | solution.py:66
  57.1 1.0 fusion.35
  58.1 4.2 %fusion.27 = bf16[4,4,288,256]{3,2,1,0:T(8,128)(2,1)} fusion(s32[]{:T(128)S(6)} %select_n.153, f32[4,4,2,256,256]{4,3,1,0,2:T(8,128)} %copy.38, f32[4,4,2,32,256]{4,3,2,1,0:T(8,128)S(1)} %bitcast.85), kind=kLoop, calls=%fused_computation.59 | loop fusion | flops 4718592 | bytes 11796484 | tf_op jit(solution)/shard_map/convert_element_type | solution.py:69
  62.3 0.3 collective-permute-start.1
  62.6 0.6 convert_reduce_fusion.1
  64.0 3.2 %collective-permute-done.1 = bf16[4,4,288,256]{3,2,1,0:T(8,128)(2,1)} collective-permute-done((bf16[4,4,288,256]{3,2,1,0:T(8,128)(2,1)}, bf16[4,4,288,256]{3,2,1,0:T(8,128)(2,1)}, u32[]{:S(2)}, u32[]{:S(2)}) %collective-permute-start.1) | collective-permute-done | bytes 2359328 | tf_op jit(solution)/shard_map/ppermute | solution.py:71
  67.2 3.7 %fusion.26 = bf16[4,4,288,256]{3,2,0,1:T(8,128)(2,1)S(1)} fusion(bf16[4,4,288,256]{3,2,1,0:T(8,128)(2,1)} %collective-permute-done.1, s32[]{:T(128)S(6)} %select_n.152, f32[4,4,2,256,256]{4,3,1,0,2:T(8,128)} %copy.38, f32[4,4,2,32,256]{4,3,2,1,0:T(8,128)S(1)} %bitcast.86), kind=kLoop, calls=%fused_computation.58 | loop fusion | flops 4718592 | bytes 14155780 | tf_op jit(solution)/shard_map/transpose | solution.py:73
  70.9 0.2 copy.40
  71.0 1.6 pad_maximum_fusion
  72.6 6.3 %all-to-all-start = ((bf16[4,1168,256]{2,1,0:T(8,128)(2,1)}), bf16[4,1168,256]{2,1,0:T(8,128)(2,1)S(1)}, u32[]{:S(2)}, u32[]{:S(2)}) async-start(bf16[4,1168,256]{2,1,0:T(8,128)(2,1)} %pad_maximum_fusion), calls=%async_computation.8 | async-start | bytes 4784128 | tf_op jit(solution)/shard_map/all_to_all | solution.py:19
  78.9 0.7 fusion.75
  79.6 4.4 %compare_select_fusion.3 = s32[512,1]{0,1:T(1,128)S(1)} fusion(s32[]{:T(128)} %bitcast.27, s32[]{:T(128)} %bitcast.28, s32[]{:T(128)} %bitcast.29, s32[]{:T(128)} %bitcast.30, s32[]{:T(128)} %bitcast.31, s32[]{:T(128)} %bitcast.33, s32[]{:T(128)} %bitcast.32), kind=kLoop, calls=%fused_computation.104 | loop fusion | flops 11776 | bytes 2076 | tf_op jit(solution)/shard_map/gather | solution.py:78
  84.1 0.7 select_convert_fusion.3
  84.7 0.8 broadcast_compare_fusion
  85.5 23.5 %all-to-all-done = bf16[4,1168,256]{2,1,0:T(8,128)(2,1)S(1)} async-done(((bf16[4,1168,256]{2,1,0:T(8,128)(2,1)}), bf16[4,1168,256]{2,1,0:T(8,128)(2,1)S(1)}, u32[]{:S(2)}, u32[]{:S(2)}) %all-to-all-start) | async-done | bytes 2392096 | tf_op jit(solution)/shard_map/all_to_all | solution.py:19
  109.0 3.7 %fusion.25 = bf16[1152,512]{0,1:T(8,128)(2,1)} fusion(bf16[4,1168,256]{2,1,0:T(8,128)(2,1)S(1)} %all-to-all-done, f32[4,256]{1,0:T(4,128)S(1)} %bitcast.94, f32[512]{0:T(512)S(1)} %select_convert_fusion.3, pred[256,512]{0,1:T(8,128)(4,1)} %broadcast_compare_fusion), kind=kOutput, calls=%fused_computation.56 | convolution fusion | flops 1209597952 | bytes 3676160 | tf_op jit(solution)/shard_map/dot_general | solution.py:81
  112.7 1.7 copy.41
  114.4 1.3 slice_reduce_fusion.4
  115.7 0.6 fusion.71
  116.5 1.1 pad_maximum_fusion.1
  117.6 4.4 %all-to-all-start.1 = ((bf16[4,1168,128]{2,1,0:T(8,128)(2,1)}), bf16[4,1168,128]{2,1,0:T(8,128)(2,1)}, u32[]{:S(2)}, u32[]{:S(2)}) async-start(bf16[4,1168,128]{2,1,0:T(8,128)(2,1)} %pad_maximum_fusion.1), calls=%async_computation.9 | async-start | bytes 2392064 | tf_op jit(solution)/shard_map/all_to_all | solution.py:19
  122.0 1.1 compare_convert_fusion
  123.1 2.1 %fusion.76 = f32[512,1024]{1,0:T(8,128)} fusion(bf16[512,512]{1,0:T(8,128)(2,1)S(1)} %copy-done.5, bf16[1024,512]{1,0:T(8,128)(2,1)S(1)} %copy-done.3), kind=kOutput, calls=%fused_computation.153 | convolution fusion | flops 536870912 | bytes 3670016 | tf_op jit(solution)/shard_map/dot_general | solution.py:15
  125.2 13.3 %all-to-all-done.1 = bf16[4,1168,128]{2,1,0:T(8,128)(2,1)} async-done(((bf16[4,1168,128]{2,1,0:T(8,128)(2,1)}), bf16[4,1168,128]{2,1,0:T(8,128)(2,1)}, u32[]{:S(2)}, u32[]{:S(2)}) %all-to-all-start.1) | async-done | bytes 1196064 | tf_op jit(solution)/shard_map/all_to_all | solution.py:19
  138.5 1.4 convert_element_type.160
  140.0 0.8 slice_reduce_fusion
  140.8 1.9 %copy.45 = bf16[1152,128]{0,1:T(8,128)(2,1)} copy(bf16[1152,128]{1,0:T(8,128)(2,1)} %slice_reduce_fusion) | data formatting | bytes 589824
  142.6 1.8 copy.43
  144.5 0.6 slice_reduce_fusion.3
  145.1 0.8 fusion.70
  146.0 1.7 pad_maximum_fusion.2
  147.7 4.8 %all-to-all-start.2 = ((bf16[4,304,128]{2,1,0:T(8,128)(2,1)}), bf16[4,304,128]{2,1,0:T(8,128)(2,1)}, u32[]{:S(2)}, u32[]{:S(2)}) async-start(bf16[4,304,128]{2,1,0:T(8,128)(2,1)} %pad_maximum_fusion.2), calls=%async_computation.10 | async-start | bytes 622592 | tf_op jit(solution)/shard_map/all_to_all | solution.py:19
  152.4 0.9 compare_convert_fusion.1
  153.4 6.1 %all-to-all-done.2 = bf16[4,304,128]{2,1,0:T(8,128)(2,1)} async-done(((bf16[4,304,128]{2,1,0:T(8,128)(2,1)}), bf16[4,304,128]{2,1,0:T(8,128)(2,1)}, u32[]{:S(2)}, u32[]{:S(2)}) %all-to-all-start.2) | async-done | bytes 311328 | tf_op jit(solution)/shard_map/all_to_all | solution.py:19
  159.5 1.0 convert_element_type.164
  160.6 0.6 slice_reduce_fusion.2
  161.2 15.6 %add_convert_fusion = bf16[512,1024]{1,0:T(8,128)(2,1)} fusion(f32[512,1024]{1,0:T(8,128)S(1)} %copy-done.1, bf16[512,8192]{1,0:T(8,128)(2,1)} %param.10, bf16[8192,1024]{1,0:T(8,128)(2,1)} %all-gather.2.cloned.1.call-done), kind=kOutput, calls=%fused_computation.62 | convolution fusion | flops 8591507456 | bytes 28311552 | tf_op jit(solution)/shard_map/dot_general | solution.py:15
  177.5 0.6 copy-done.6
  (45 shorter events, 0.6 us)
Async XLA Ops:
  7.2 3.8 %copy-start.9 = (s32[512]{0:T(512)S(1)}, s32[512]{0:T(512)}, u32[]{:S(2)}) copy-start(s32[512]{0:T(512)} %param.15) | copy-start | bytes 6148
  7.2 154.0 %all-gather.2.cloned.1.call-start = ((), (), s32[]{:S(2)}) async-start(), calls=%async_computation.19 | async-start | bytes 17301504 | tf_op jit(solution)/shard_map/all_gather | solution.py:39
  7.9 13.4 %collective-permute-start = (s32[512]{0:T(512)}, s32[512]{0:T(512)S(1)}, u32[]{:S(2)}, u32[]{:S(2)}) collective-permute-start(s32[512]{0:T(512)} %param.15), channel_id=1, source_target_pairs={{0,1},{1,0},{2,3},{3,2},{4,5},{5,4},{6,7},{7,6},{8,9},{9,8},{10,11... | collective-permute-start | bytes 6152 | tf_op jit(solution)/shard_map/ppermute | solution.py:42
  10.9 10.7 %copy-start.2 = (bf16[1024,512]{1,0:T(8,128)(2,1)S(1)}, bf16[1024,512]{1,0:T(8,128)(2,1)}, u32[]{:S(2)}) copy-start(bf16[1024,512]{1,0:T(8,128)(2,1)} %param.13) | copy-start | bytes 3145732
  21.3 35.8 %copy-start.4 = (bf16[512,512]{1,0:T(8,128)(2,1)}, bf16[512,512]{1,0:T(8,128)(2,1)S(1)}, u32[]{:S(2)}) copy-start(bf16[512,512]{1,0:T(8,128)(2,1)S(1)} %fusion.31) | copy-start | bytes 1572868
  62.3 4.9 %collective-permute-start.1 = (bf16[4,4,288,256]{3,2,1,0:T(8,128)(2,1)}, bf16[4,4,288,256]{3,2,1,0:T(8,128)(2,1)}, u32[]{:S(2)}, u32[]{:S(2)}) collective-permute-start(bf16[4,4,288,256]{3,2,1,0:T(8,128)(2,1)} %fusion.27), channel_id=1, source_target_pairs={{0,1},{1,0},{2,3},{3,2},{4,5},{5,4},{6,7},{7,6},{8,9},{9,8},{10,11... | collective-permute-start | bytes 7077896 | tf_op jit(solution)/shard_map/ppermute | solution.py:71
  72.6 6.3 %copy-start.7 = (s32[8]{0:T(128)S(1)}, s32[8]{0:T(128)}, u32[]{:S(2)}) copy-start(s32[8]{0:T(128)} %param.16) | copy-start | bytes 100
  72.6 36.4 %all-to-all-start = ((bf16[4,1168,256]{2,1,0:T(8,128)(2,1)}), bf16[4,1168,256]{2,1,0:T(8,128)(2,1)S(1)}, u32[]{:S(2)}, u32[]{:S(2)}) async-start(bf16[4,1168,256]{2,1,0:T(8,128)(2,1)} %pad_maximum_fusion), calls=%async_computation.8 | async-start | bytes 4784128 | tf_op jit(solution)/shard_map/all_to_all | solution.py:19
  109.0 3.7 %copy-start = (bf16[4,1168,256]{2,1,0:T(8,128)(2,1)}, bf16[4,1168,256]{2,1,0:T(8,128)(2,1)S(1)}, u32[]{:S(2)}) copy-start(bf16[4,1168,256]{2,1,0:T(8,128)(2,1)S(1)} %all-to-all-done) | copy-start | bytes 7176196
  116.5 6.7 %copy-start.3 = (bf16[1024,512]{1,0:T(8,128)(2,1)S(1)}, bf16[1024,512]{1,0:T(8,128)(2,1)}, u32[]{:S(2)}) copy-start(bf16[1024,512]{1,0:T(8,128)(2,1)} %param.13) | copy-start | bytes 3145732
  117.6 5.6 %copy-start.5 = (bf16[512,512]{1,0:T(8,128)(2,1)S(1)}, bf16[512,512]{1,0:T(8,128)(2,1)}, u32[]{:S(2)}) copy-start(bf16[512,512]{1,0:T(8,128)(2,1)} %copy-done.4) | copy-start | bytes 1572868
  117.6 20.9 %all-to-all-start.1 = ((bf16[4,1168,128]{2,1,0:T(8,128)(2,1)}), bf16[4,1168,128]{2,1,0:T(8,128)(2,1)}, u32[]{:S(2)}, u32[]{:S(2)}) async-start(bf16[4,1168,128]{2,1,0:T(8,128)(2,1)} %pad_maximum_fusion.1), calls=%async_computation.9 | async-start | bytes 2392064 | tf_op jit(solution)/shard_map/all_to_all | solution.py:19
  145.1 16.1 %copy-start.1 = (f32[512,1024]{1,0:T(8,128)S(1)}, f32[512,1024]{1,0:T(8,128)}, u32[]{:S(2)}) copy-start(f32[512,1024]{1,0:T(8,128)} %fusion.76) | copy-start | bytes 6291460
  147.7 11.8 %all-to-all-start.2 = ((bf16[4,304,128]{2,1,0:T(8,128)(2,1)}), bf16[4,304,128]{2,1,0:T(8,128)(2,1)}, u32[]{:S(2)}, u32[]{:S(2)}) async-start(bf16[4,304,128]{2,1,0:T(8,128)(2,1)} %pad_maximum_fusion.2), calls=%async_computation.10 | async-start | bytes 622592 | tf_op jit(solution)/shard_map/all_to_all | solution.py:19
  177.4 0.7 copy-start.6
  177.4 0.6 copy-start.8
Sparse Core Ops, SparseCore 0:
  10.3 75.2 all-gather.1

commit v2 on v1

v2 whole, which is shorter than its diff:
```python
import jax
import jax.numpy as jnp
from jax import lax
from jax.experimental import pallas as pl
from jax.experimental.pallas import tpu as pltpu
from jax.sharding import Mesh, PartitionSpec as P

RANK = 64
SCALE = 0.5
BF = jnp.bfloat16
F32 = jnp.float32
SLOTS = 4
INFO = 16
MIB = 1 << 20
SWAP = [(0, 1), (1, 0)]


def dot(a, b, dims=((1,), (0,))):
    return lax.dot_general(a, b, (dims, ((), ())), preferred_element_type=F32)


def exchange(a, axis):
    return lax.all_to_all(a, axis, 0, 0, tiled=True)


def call(body, out, grid, in_specs, out_specs, scratch=(), flops=0, data=0, vmem=40):
    return pl.pallas_call(
        body,
        out_shape=out,
        grid=grid,
        in_specs=in_specs,
        out_specs=out_specs,
        scratch_shapes=list(scratch),
        compiler_params=pltpu.CompilerParams(vmem_limit_bytes=vmem * MIB),
        cost_estimate=pl.CostEstimate(flops=flops, bytes_accessed=data, transcendentals=0),
    )


def whole(shape):
    return pl.BlockSpec(shape, lambda *i: (0,) * len(shape))


def terms(tokens, down, low_t, scaled, tasks_col, pick_t, me_c, nx, nz):
    n_tok, width = tokens.shape
    cols = down.shape[1]
    sc = low_t.shape[0]
    kv = scaled.shape[1]
    steps = nx * nz
    blk = width // steps
    d = blk // 2
    half = kv // 2
    u = half // nz
    lanes = nx * d + u

    def body(me, tok, dn, low, sca, task, pick, hidden, theirs, mine, acc):
        i = pl.program_id(0)
        x, z = i // nz, i % nz
        first = me[0] == 0

        @pl.when(i == 0)
        def _():
            acc[...] = jnp.zeros_like(acc)

        t = tok[...]
        acc[...] += dot(t, dn[...])
        r = dot(low[...], t)
        at = pl.ds(pl.multiple_of(x * d, d), d)
        mine[z, :, at] = jnp.where(first, r[:, :d], r[:, d:])
        theirs[z, :, at] = jnp.where(first, r[:, d:], r[:, :d]).astype(BF)

        @pl.when(i == steps - 1)
        def _():
            adapter = lax.broadcasted_iota(jnp.int32, (n_tok, cols), 1) // RANK
            h = jnp.where(task[...] == adapter, acc[...], 0.0).astype(BF)
            hidden[...] = h
            h_t = dot(pick[...], h, ((1,), (1,))).astype(BF)
            g = dot(h_t, sca[...])
            for k in range(nz):
                a, b = g[:, k * u : (k + 1) * u], g[:, half + k * u : half + (k + 1) * u]
                mine[k, :, nx * d :] = jnp.where(first, a, b)
                theirs[k, :, nx * d :] = jnp.where(first, b, a).astype(BF)

    return call(
        body,
        (
            jax.ShapeDtypeStruct((n_tok, cols), BF),
            jax.ShapeDtypeStruct((nz, sc, lanes), BF),
            jax.ShapeDtypeStruct((nz, sc, lanes), F32),
        ),
        (steps,),
        [
            pl.BlockSpec(memory_space=pltpu.SMEM),
            pl.BlockSpec((n_tok, blk), lambda i: (0, i)),
            pl.BlockSpec((blk, cols), lambda i: (i, 0)),
            whole((sc, n_tok)),
            whole((n_tok, kv)),
            whole((n_tok, 1)),
            whole((sc, cols)),
        ],
        (whole((n_tok, cols)), whole((nz, sc, lanes)), whole((nz, sc, lanes))),
        [pltpu.VMEM((n_tok, cols), F32)],
        flops=2 * n_tok * width * (cols + sc),
        data=28 * MIB,
        vmem=48,
    )(me_c, tokens, down, low_t, scaled, tasks_col, pick_t)


def pack(mine, theirs, note):
    n, sc, lanes = mine.shape

    def body(a, b, c, out):
        out[0, :sc] = (a[0] + b[0].astype(F32)).astype(BF)
        out[0, sc:] = c[...]

    block = pl.BlockSpec((1, sc, lanes), lambda i: (i, 0, 0))
    return call(
        body,
        jax.ShapeDtypeStruct((n, sc + INFO, lanes), BF),
        (n,),
        [block, block, whole((INFO, lanes))],
        pl.BlockSpec((1, sc + INFO, lanes), lambda i: (i, 0, 0)),
        data=10 * MIB,
    )(mine, theirs, note)


def spread(got, owned_col, ny):
    n, rows, lanes = got.shape
    sc = rows - INFO
    cols = owned_col.shape[0]
    own = cols // ny

    def body(g, ow, out):
        total = jnp.zeros((own, lanes), F32)
        flag = jnp.zeros((1, lanes), BF)
        same = (
            lax.broadcasted_iota(jnp.int32, (own, sc), 0) % RANK
            == lax.broadcasted_iota(jnp.int32, (own, sc), 1) % RANK
        )
        for p in range(n):
            note = g[p, sc:, :]
            sent = note[0:1, :sc].astype(F32)
            place = jnp.where(same & (ow[...] == sent), 1.0, 0.0).astype(BF)
            total += dot(place, g[p, :sc, :])
            flag = jnp.maximum(flag, note[1:2, :])
        out[0, :own] = total.astype(BF)
        out[0, own:] = jnp.broadcast_to(flag, (INFO, lanes))

    return call(
        body,
        jax.ShapeDtypeStruct((ny, own + INFO, lanes), BF),
        (ny,),
        [whole((n, rows, lanes)), pl.BlockSpec((own, 1), lambda i: (i, 0))],
        pl.BlockSpec((1, own + INFO, lanes), lambda i: (i, 0, 0)),
        flops=2 * cols * n * sc * lanes,
        data=5 * MIB,
    )(got, owned_col)


def turn(got, nx, d):
    n, rows, lanes = got.shape
    own = rows - INFO
    v = (lanes - nx * d) // nx

    def body(g, out):
        total = g[0, :own].astype(F32)
        flag = g[0, own : own + INFO, :own]
        for p in range(1, n):
            total += g[p, :own].astype(F32)
            flag = jnp.maximum(flag, g[p, own : own + INFO, :own])
        t = total.T.astype(BF)
        for x in range(nx):
            out[x, :d] = t[x * d : (x + 1) * d]
            out[x, d : d + v] = t[nx * d + x * v : nx * d + (x + 1) * v]
            out[x, d + v :] = flag

    return call(
        body,
        jax.ShapeDtypeStruct((nx, d + v + INFO, own), BF),
        (1,),
        [whole(got.shape)],
        whole((nx, d + v + INFO, own)),
        data=2 * MIB,
    )(got)


def finish(got, d):
    n, rows, own = got.shape
    v = rows - INFO - d

    def body(g, down, up, flag):
        total = g[0].astype(F32)
        most = g[0, d + v :].astype(F32)
        for p in range(1, n):
            total += g[p].astype(F32)
            most = jnp.maximum(most, g[p, d + v :].astype(F32))
        down[...] = total[:d]
        up[...] = total[d : d + v]
        flag[...] = most

    shapes = (d, own), (v, own), (INFO, own)
    return call(
        body,
        tuple(jax.ShapeDtypeStruct(s, F32) for s in shapes),
        (1,),
        [whole(got.shape)],
        tuple(whole(s) for s in shapes),
        data=MIB // 2,
    )(got)


def project(tokens, weight, hidden, up):
    n_tok, width = tokens.shape
    kv, cols = up.shape
    blk = 512
    steps = width // blk

    def body(t, w, h, u, out, acc):
        i = pl.program_id(0)

        @pl.when(i == 0)
        def _():
            acc[...] = SCALE * dot(h[...], u[...], ((1,), (1,)))

        acc[...] += dot(t[...], w[...])

        @pl.when(i == steps - 1)
        def _():
            out[...] = acc[...].astype(BF)

    return call(
        body,
        jax.ShapeDtypeStruct((n_tok, kv), BF),
        (steps,),
        [
            pl.BlockSpec((n_tok, blk), lambda i: (0, i)),
            pl.BlockSpec((blk, kv), lambda i: (i, 0)),
            whole((n_tok, cols)),
            whole((kv, cols)),
        ],
        whole((n_tok, kv)),
        [pltpu.VMEM((n_tok, kv), F32)],
        flops=2 * n_tok * kv * (width + cols),
        data=26 * MIB,
    )(tokens, weight, hidden, up)


def per_device(tokens, weight, down, up, cotangent, tasks, owned, counts):
    n_tok, width = tokens.shape
    kv = weight.shape[1]
    adapters = owned.shape[0]
    cols = adapters * RANK
    ny, nx, nz = lax.axis_size("y"), lax.axis_size("x"), lax.axis_size("z")
    me_c = lax.axis_index("c")
    d_rows, v_rows = width // (nx * nz * 2), kv // (nx * nz * 2)
    sc = SLOTS * RANK
    lanes = nx * (d_rows + v_rows)

    full_weight = lax.all_gather(weight, ("x", "z", "c"), axis=0, tiled=True)

    ids = jnp.arange(adapters, dtype=jnp.int32)
    partner_tasks = lax.ppermute(tasks, "c", SWAP)
    hit = tasks[:, None] == ids[None, :]
    present = jnp.any(hit | (partner_tasks[:, None] == ids[None, :]), axis=0)
    rank_of = jnp.sum((ids[None, :] < ids[:, None]) & present[None, :], axis=1)
    col_slot = jnp.arange(sc, dtype=jnp.int32) // RANK
    col_rank = jnp.arange(sc, dtype=jnp.int32) % RANK
    chosen = present[None, :] & (rank_of[None, :] == col_slot[:, None])
    col_task = jnp.sum(jnp.where(chosen, ids[None, :] + 1, 0), axis=1) - 1
    overflow = (jnp.sum(present.astype(jnp.int32)) > SLOTS).astype(F32)

    row = jnp.arange(cols, dtype=jnp.int32)
    pick_t = ((row // RANK)[None, :] == col_task[:, None]) & ((row % RANK)[None, :] == col_rank[:, None])
    pick_t = pick_t.astype(BF)
    mask_slot_t = (tasks[None, :] == col_task[:, None]).astype(F32)

    token_count = jnp.sum(jnp.where(hit, counts.astype(F32)[None, :], 0.0), axis=1)
    scaled = (cotangent.astype(F32) * (SCALE / token_count)[:, None]).astype(BF)
    v_in = jnp.arange(kv, dtype=jnp.int32)
    v_from = (
        (v_in // v_rows % nx) * (nz * 2 * v_rows)
        + (v_in // (v_rows * nx) % nz) * (2 * v_rows)
        + v_in // (v_rows * nx * nz) * v_rows
        + v_in % v_rows
    )
    scaled_by_core = dot(scaled, (v_in[:, None] == v_from[None, :]).astype(BF)).astype(BF)

    up_slot_t = dot(pick_t, up, ((1,), (1,))).astype(BF)
    low_t = (dot(up_slot_t, scaled, ((1,), (1,))) * mask_slot_t).astype(BF)

    hidden, theirs, mine = terms(
        tokens, down, low_t, scaled_by_core, tasks[:, None], pick_t, me_c.astype(jnp.int32)[None], nx, nz
    )

    note_row = lax.broadcasted_iota(jnp.int32, (INFO, lanes), 0)
    note = jnp.where(note_row == 0, jnp.pad(col_task.astype(F32), (0, lanes - sc))[None, :], overflow)
    chip = pack(mine, lax.ppermute(theirs, "c", SWAP), note.astype(BF))

    owned_col = jnp.repeat(owned.astype(F32), RANK)[:, None]
    by_owner = spread(exchange(chip, "z"), owned_col, ny)
    by_x = turn(exchange(by_owner, "y"), nx, d_rows)
    grad_down, grad_up, flags = finish(exchange(by_x, "x"), d_rows)

    keys = project(tokens, full_weight, hidden, up)

    flag, keys = lax.optimization_barrier((flags[0, 0], keys))

    def rest(grads):
        own = cols // ny
        left = jnp.all(tasks[:, None] != col_task[None, :], axis=1)[:, None]
        mask = (tasks[:, None] == (row // RANK)[None, :]) & left
        order = ((row // RANK)[:, None] == owned[row // RANK][None, :]) & (
            (row % RANK)[:, None] == (row % RANK)[None, :]
        )
        order = order.astype(BF)
        low_left = jnp.where(mask, dot(scaled, up), 0.0).astype(BF)
        low_left = dot(low_left, order).astype(BF)
        hid_left = dot(jnp.where(left, hidden, 0.0).astype(BF), order).astype(BF)

        def summed(a, b):
            t = lax.dot_general(
                a, b.reshape(n_tok, ny, own), (((0,), (0,)), ((), ())), preferred_element_type=F32
            )
            t = jnp.transpose(t, (1, 0, 2)).reshape(-1, own)
            for axis in ("y", "x", "z", "c"):
                t = lax.psum_scatter(t, axis, scatter_dimension=0, tiled=True)
            return t

        return grads[0] + summed(tokens, low_left), grads[1] + summed(scaled, hid_left)

    grad_down, grad_up = lax.cond(flag > 0.5, rest, lambda g: g, (grad_down, grad_up))
    return keys, grad_down[None], grad_up[None]


def solution(mesh):
    sizes = dict(mesh.shape)
    ny = sizes["grp"]
    nx = nz = int((sizes["fsdp"] // 2) ** 0.5)
    fine = Mesh(mesh.devices.reshape(ny, nx, nz, 2), ("y", "x", "z", "c"))
    fsdp = ("x", "z", "c")
    every = ("y", "x", "z", "c")
    in_specs = (P(every, None), P(fsdp, None), P(), P(), P(every, None), P(every), P(), P())
    out_specs = (P(every, None), P("y", fsdp, None), P("y", fsdp, None))
    return jax.shard_map(per_device, mesh=fine, in_specs=in_specs, out_specs=out_specs, check_vma=False)
```

time: 186 us -> 174 us (0.935)
  Pallas kernels: 0 us -> 44.8 us
  matrix products: 43 us -> 3.3 us
  blocking collectives: 0 us -> 32.9 us
  local copies, waits for them, and re-layouts: 32.1 us -> 3.96 us
  other arithmetic: 31.7 us -> 4.14 us
  waiting for transfers between devices: 46.7 us -> 62 us
  starting transfers between devices: 15.9 us -> 6.11 us
    pallas_call x0 -> x6, Pallas kernels: none -> 44.8 us  [the longest x1 20.6 us: project(): call(body, jax.ShapeDtypeStruct((n_tok, kv), BF), (steps,), [pl.BlockSpec...]
    dot_general x6 -> x2, matrix products: 39.3 us -> 3.3 us  [dot(): return lax.dot_general(a, b, (dims, ((), ())), preferred_element_type=F32)]
    all_to_all x0 -> x2, blocking collectives: none -> 32.9 us  [exchange(): return lax.all_to_all(a, axis, 0, 0, tiled=True)]
    reshape x2 -> x0, local copies, waits for them, and re-layouts: 25.1 us -> none  [per_device(): down_term = dot(tokens, low, ((0,), (0,))).reshape(nx, nz, 2, d_rows, sc)]
    all_to_all x3 -> x1, waiting for transfers between devices: 42.8 us -> 58.4 us  [exchange(): return lax.all_to_all(a, axis, 0, 0, tiled=True)]
    all_to_all x3 -> x1, starting transfers between devices: 15.4 us -> 5.43 us  [exchange(): return lax.all_to_all(a, axis, 0, 0, tiled=True)]
    convert_element_type x10 -> x4, other arithmetic: 9.62 us -> 0.24 us  [the longest x1 0.15 us: per_device(): pick_t = pick_t.astype(BF)]
    gather x2 -> x0, other arithmetic: 4.47 us -> none  [per_device(): owned[row // RANK].astype(F32)[None, None, :]]
  transfers between devices with their start and end apart: 6 -> 4, of which waited for: 4 -> 2; matrix products, arithmetic and copies ran while one was open for 49% -> 5% of each run, Pallas kernels for 0% -> 14%
where the time goes in v2:
time: 174 us; the launch traced here: 173 us
  waiting for transfers between devices  62 us (36%)
  Pallas kernels  44.8 us (26%)
  blocking collectives  32.9 us (19%)
  between operations  15.5 us (9%)
  starting transfers between devices  6.11 us (4%)
  other arithmetic  4.14 us (2%)
  local copies, waits for them, and re-layouts  3.96 us (2%)
  matrix products  3.3 us (2%)
    all_to_all x1, waiting for transfers between devices, exchange(): return lax.all_to_all(a, axis, 0, 0, tiled=True)  58.4 us
    all_to_all x2, blocking collectives, exchange(): return lax.all_to_all(a, axis, 0, 0, tiled=True)  32.9 us
    pallas_call x1, Pallas kernels, project(): call(body, jax.ShapeDtypeStruct((n_tok, kv), BF), (steps,), [pl.BlockSpec...  20.6 us
    pallas_call x1, Pallas kernels, terms(): call(body, (jax.ShapeDtypeStruct((n_tok, cols), BF), jax.ShapeDtypeStruct...  19.6 us
    all_to_all x1, starting transfers between devices, exchange(): return lax.all_to_all(a, axis, 0, 0, tiled=True)  5.43 us
  transfers between devices with their start and end apart: 4, of which 2 were waited for; matrix products, arithmetic and copies ran while one was open for 5% of the time, Pallas kernels for 14%

profile of v2, /device:TPU:0, one launch (start us, length us, event | category | flops | bytes accessed | tf_op | source)
XLA Modules:
  0.0 173.0 jit_solution(4666129811248870498)
XLA Ops:
  7.2 0.0 all-gather.2.cloned.1.call-start
  7.2 0.7 all-gather.2.cloned.1.call-update
  7.9 0.1 collective-permute-start
  8.0 0.7 convert_element_type.61
  8.7 0.8 select_reduce_fusion
  9.4 0.0 copy-start.4
  9.5 1.5 multiply_convert_fusion
  10.9 0.0 copy-start.1
  10.9 1.3 fusion.31.sca
  12.3 0.0 copy-done.4
  12.3 0.2 copy.17.task
  12.4 0.0 collective-permute-done
  12.5 0.1 fusion.45
  12.6 0.1 convert_reduce_fusion
  12.7 0.1 select_reduce_fusion.1
  12.8 0.2 fusion.35.pick
  13.0 2.0 %fusion.34.low = bf16[256,512]{1,0:T(8,128)(2,1)S(1)} fusion(bf16[512,1024]{1,0:T(8,128)(2,1)S(1)} %multiply_convert_fusion, bf16[1024,512]{1,0:T(8,128)(2,1)} %u.1, s32[512]{0:T(512)S(1)} %get-tuple-element.93, s32[512]{0:T(512)S(1)} %get-tuple-element.94, s32[512]{0:T(512)S(1)} %copy-done.4, s32[256]{0:T(256)S(1)} %get-tuple-element.95, ...), kind=kOutput, calls=%fused_computation.66 | convolution fusion | flops 537919488 | bytes 2367488 | tf_op jit(solution)/shard_map/dot_general | solution.py:19
  14.9 0.0 copy-done.1
  14.9 19.6 %shard_map.103 = (bf16[512,512]{1,0:T(8,128)(2,1)}, bf16[4,256,1152]{2,1,0:T(8,128)(2,1)}, f32[4,256,1152]{2,1,0:T(8,128)}) custom-call(s32[1]{0:T(128)} %bitcast.20.me, bf16[512,8192]{1,0:T(8,128)(2,1)} %t.1, bf16[8192,512]{1,0:T(8,128)(2,1)} %dn.1, bf16[256,512]{1,0:T(8,128)(2,1)S(1)} %fusion.34.low, bf16[512,1024]{1,0:T(8,128)(2,1)S(1)} %fusion.31.sca, ...), custom_call_target="tpu_custom_call" | custom-call | flops 6442450944 | bytes 29360128 | tf_op jit(solution)/shard_map/pallas_call | solution.py:83
  34.6 0.6 collective-permute-start.1
  35.1 0.6 convert_reduce_fusion.1
  36.4 0.1 select_convert_fusion.c
  36.5 3.0 %collective-permute-done.1.b = bf16[4,256,1152]{2,1,0:T(8,128)(2,1)S(1)} collective-permute-done((bf16[4,256,1152]{2,1,0:T(8,128)(2,1)}, bf16[4,256,1152]{2,1,0:T(8,128)(2,1)S(1)}, u32[]{:S(2)}, u32[]{:S(2)}) %collective-permute-start.1) | collective-permute-done | bytes 2359328 | tf_op jit(solution)/shard_map/ppermute | solution.py:296
  39.5 0.0 copy-start
  39.5 2.3 %copy-done = f32[4,256,1152]{2,1,0:T(8,128)S(1)} copy-done((f32[4,256,1152]{2,1,0:T(8,128)S(1)}, f32[4,256,1152]{2,1,0:T(8,128)}, u32[]{:S(2)}) %copy-start) | copy-done | bytes 4718616
  41.8 2.1 %shard_map.104 = bf16[4,272,1152]{2,1,0:T(8,128)(2,1)} custom-call(f32[4,256,1152]{2,1,0:T(8,128)S(1)} %copy-done, bf16[4,256,1152]{2,1,0:T(8,128)(2,1)S(1)} %collective-permute-done.1.b, bf16[16,1152]{1,0:T(8,128)(2,1)S(1)} %select_convert_fusion.c), custom_call_target="tpu_custom_call" | custom-call | bytes 10485760 | tf_op jit(solution)/shard_map/pallas_call | solution.py:116
  44.0 0.0 copy-start.5
  44.0 5.4 %all-to-all-start = ((bf16[4,272,1152]{2,1,0:T(8,128)(2,1)}), bf16[4,272,1152]{2,1,0:T(8,128)(2,1)S(1)}, u32[]{:S(2)}, u32[]{:S(2)}) async-start(bf16[4,272,1152]{2,1,0:T(8,128)(2,1)} %shard_map.104), calls=%async_computation.8 | async-start | bytes 5013504 | tf_op jit(solution)/shard_map/all_to_all | solution.py:23
  49.4 0.0 copy-done.5
  49.4 0.1 broadcast_in_dim.119
  49.5 0.2 broadcast_in_dim_reshape.4.ow
  49.7 58.4 %all-to-all-done.g = bf16[4,272,1152]{2,1,0:T(8,128)(2,1)S(1)} async-done(((bf16[4,272,1152]{2,1,0:T(8,128)(2,1)}), bf16[4,272,1152]{2,1,0:T(8,128)(2,1)S(1)}, u32[]{:S(2)}, u32[]{:S(2)}) %all-to-all-start) | async-done | bytes 2506784 | tf_op jit(solution)/shard_map/all_to_all | solution.py:23
  108.1 2.2 %shard_map.105 = bf16[4,144,1152]{2,1,0:T(8,128)(2,1)S(1)} custom-call(bf16[4,272,1152]{2,1,0:T(8,128)(2,1)S(1)} %all-to-all-done.g, f32[512,1]{1,0:T(8,128)S(1)} %broadcast_in_dim_reshape.4.ow), custom_call_target="tpu_custom_call" | custom-call | flops 1207959552 | bytes 5242880 | tf_op jit(solution)/shard_map/pallas_call | solution.py:148
  110.3 0.0 copy-start.7
  110.3 21.9 %all_to_all.15.g = bf16[4,144,1152]{2,1,0:T(8,128)(2,1)S(1)} all-to-all(bf16[4,144,1152]{2,1,0:T(8,128)(2,1)S(1)} %shard_map.105), channel_id=1, replica_groups=mesh['y'=4,'x'=4,'z'=4,'c'=2] {'y'}, dimensions={0} | all-to-all | bytes 2654208 | tf_op jit(solution)/shard_map/all_to_all | solution.py:23
  132.2 0.2 shard_map.106
  132.4 11.0 %all_to_all.16.g = bf16[4,304,128]{2,1,0:T(8,128)(2,1)S(1)} all-to-all(bf16[4,304,128]{2,1,0:T(8,128)(2,1)S(1)} %shard_map.106), channel_id=1, replica_groups=mesh['y'=4,'x'=4,'z'=4,'c'=2] {'x'}, dimensions={0} | all-to-all | bytes 622592 | tf_op jit(solution)/shard_map/all_to_all | solution.py:23
  143.5 0.5 slice.3
  144.0 0.0 copy-start.2
  144.0 0.0 copy-done.7
  144.0 20.6 %shard_map.108 = bf16[512,1024]{1,0:T(8,128)(2,1)} custom-call(bf16[512,8192]{1,0:T(8,128)(2,1)} %t.1, bf16[8192,1024]{1,0:T(8,128)(2,1)} %all-gather.2.cloned.1.call-done.w, bf16[512,512]{1,0:T(8,128)(2,1)} %get-tuple-element.113.h, bf16[1024,512]{1,0:T(8,128)(2,1)S(1)} %copy-done.7), custom_call_target="tpu_custom_call" | custom-call | flops 9126805504 | bytes 27262976 | tf_op jit(solution)/shard_map/pallas_call | solution.py:230
  165.3 0.0 copy-done.2
  165.3 0.0 copy-done.9
  165.3 0.2 conditional.1
  165.5 0.0 copy-start.3
  165.5 0.0 copy-start.6
  165.6 0.6 copy-done.3
  166.2 0.0 copy-done.6
  (13 shorter events, 0.1 us)
Async XLA Ops:
  7.2 136.9 %all-gather.2.cloned.1.call-start = ((), (), s32[]{:S(2)}) async-start(), calls=%async_computation.19 | async-start | bytes 17301504 | tf_op jit(solution)/shard_map/all_gather | solution.py:258
  7.9 4.6 %collective-permute-start = (s32[512]{0:T(512)}, s32[512]{0:T(512)S(1)}, u32[]{:S(2)}, u32[]{:S(2)}) collective-permute-start(s32[512]{0:T(512)} %param.15), channel_id=1, source_target_pairs={{0,1},{1,0},{2,3},{3,2},{4,5},{5,4},{6,7},{7,6},{8,9},{9,8},{10,11... | collective-permute-start | bytes 6152 | tf_op jit(solution)/shard_map/ppermute | solution.py:261
  9.4 2.8 %copy-start.4 = (s32[512]{0:T(512)S(1)}, s32[512]{0:T(512)}, u32[]{:S(2)}) copy-start(s32[512]{0:T(512)} %param.15) | copy-start | bytes 6148
  10.9 4.0 %copy-start.1 = (bf16[512,1024]{1,0:T(8,128)(2,1)}, bf16[512,1024]{1,0:T(8,128)(2,1)S(1)}, u32[]{:S(2)}) copy-start(bf16[512,1024]{1,0:T(8,128)(2,1)S(1)} %multiply_convert_fusion) | copy-start | bytes 3145732
  34.6 4.9 %collective-permute-start.1 = (bf16[4,256,1152]{2,1,0:T(8,128)(2,1)}, bf16[4,256,1152]{2,1,0:T(8,128)(2,1)S(1)}, u32[]{:S(2)}, u32[]{:S(2)}) collective-permute-start(bf16[4,256,1152]{2,1,0:T(8,128)(2,1)} %get-tuple-element.66), channel_id=1, source_target_pairs={{0,1},{1,0},{2,3},{3,2},{4,5},{5,4},{6,7},{7,6},{8,9},{9,8},{10,11... | collective-permute-start | bytes 7077896 | tf_op jit(solution)/shard_map/ppermute | solution.py:296
  39.5 2.3 %copy-start = (f32[4,256,1152]{2,1,0:T(8,128)S(1)}, f32[4,256,1152]{2,1,0:T(8,128)}, u32[]{:S(2)}) copy-start(f32[4,256,1152]{2,1,0:T(8,128)} %get-tuple-element.65.a) | copy-start | bytes 14155780
  44.0 5.4 %copy-start.5 = (s32[8]{0:T(128)S(1)}, s32[8]{0:T(128)}, u32[]{:S(2)}) copy-start(s32[8]{0:T(128)} %param.16) | copy-start | bytes 100
  44.0 64.1 %all-to-all-start = ((bf16[4,272,1152]{2,1,0:T(8,128)(2,1)}), bf16[4,272,1152]{2,1,0:T(8,128)(2,1)S(1)}, u32[]{:S(2)}, u32[]{:S(2)}) async-start(bf16[4,272,1152]{2,1,0:T(8,128)(2,1)} %shard_map.104), calls=%async_computation.8 | async-start | bytes 5013504 | tf_op jit(solution)/shard_map/all_to_all | solution.py:23
  110.3 33.7 %copy-start.7 = (bf16[1024,512]{1,0:T(8,128)(2,1)S(1)}, bf16[1024,512]{1,0:T(8,128)(2,1)}, u32[]{:S(2)}) copy-start(bf16[1024,512]{1,0:T(8,128)(2,1)} %u.1) | copy-start | bytes 3145732
  144.0 21.3 %copy-start.2 = (bf16[512,1024]{1,0:T(8,128)(2,1)S(1)}, bf16[512,1024]{1,0:T(8,128)(2,1)}, u32[]{:S(2)}) copy-start(bf16[512,1024]{1,0:T(8,128)(2,1)} %copy-done.1) | copy-start | bytes 3145732
  144.0 21.3 %copy-start.9 = (bf16[512,512]{1,0:T(8,128)(2,1)S(1)}, bf16[512,512]{1,0:T(8,128)(2,1)}, u32[]{:S(2)}) copy-start(bf16[512,512]{1,0:T(8,128)(2,1)} %get-tuple-element.113.h) | copy-start | bytes 1572868
  165.5 0.7 copy-start.3
  165.5 0.6 copy-start.6
Sparse Core Ops, SparseCore 0:
  10.3 101.9 all-gather.1

commit v3 on v2

--- a/solution.py
+++ b/solution.py
@@ -9,7 +9,7 @@
 SCALE = 0.5
 BF = jnp.bfloat16
 F32 = jnp.float32
-SLOTS = 4
+SLOTS = 2
 INFO = 16
 MIB = 1 << 20
 SWAP = [(0, 1), (1, 0)]
@@ -45,28 +45,35 @@
     cols = down.shape[1]
     sc = low_t.shape[0]
     kv = scaled.shape[1]
-    steps = nx * nz
+    per = 2
+    steps = nx * nz // per
     blk = width // steps
-    d = blk // 2
+    d = width // (nx * nz * 2)
     half = kv // 2
     u = half // nz
     lanes = nx * d + u
 
     def body(me, tok, dn, low, sca, task, pick, hidden, theirs, mine, acc):
         i = pl.program_id(0)
-        x, z = i // nz, i % nz
         first = me[0] == 0
+        t = tok[...]
+        part = dot(t, dn[...])
 
         @pl.when(i == 0)
         def _():
-            acc[...] = jnp.zeros_like(acc)
-
-        t = tok[...]
-        acc[...] += dot(t, dn[...])
+            acc[...] = part
+
+        @pl.when(i > 0)
+        def _():
+            acc[...] += part
+
         r = dot(low[...], t)
-        at = pl.ds(pl.multiple_of(x * d, d), d)
-        mine[z, :, at] = jnp.where(first, r[:, :d], r[:, d:])
-        theirs[z, :, at] = jnp.where(first, r[:, d:], r[:, :d]).astype(BF)
+        for k in range(per):
+            x, z = (i * per + k) // nz, (i * per + k) % nz
+            at = pl.ds(pl.multiple_of(x * d, d), d)
+            a, b = r[:, 2 * k * d : (2 * k + 1) * d], r[:, (2 * k + 1) * d : (2 * k + 2) * d]
+            mine[z, :, at] = jnp.where(first, a, b)
+            theirs[z, :, at] = jnp.where(first, b, a).astype(BF)
 
         @pl.when(i == steps - 1)
         def _():
@@ -208,40 +215,77 @@
     )(got)
 
 
-def project(tokens, weight, hidden, up):
-    n_tok, width = tokens.shape
-    kv, cols = up.shape
-    blk = 512
-    steps = width // blk
-
-    def body(t, w, h, u, out, acc):
+def shifted(a, axis, step):
+    n = lax.axis_size(axis)
+    return lax.ppermute(a, axis, [(i, (i + step) % n) for i in range(n)])
+
+
+def add_blocks(own, other, groups, where_from, before=None, lora=None, final=False):
+    n_tok = own.shape[0]
+    rows = sum(w.shape[0] for w in groups[0])
+    n = groups[0][0].shape[1]
+    steps = len(groups)
+    per = where_from.shape[0] // steps
+    blk = rows // per
+    flat = [w for group in groups for w in group]
+    extra = [] if before is None else [before]
+    if lora is not None:
+        extra += list(lora)
+
+    def body(at, *refs):
+        tok_a, tok_b = refs[:per], refs[per : 2 * per]
+        ws = refs[2 * per : 2 * per + len(flat)]
+        more = refs[2 * per + len(flat) : 2 * per + len(flat) + len(extra)]
+        out = refs[2 * per + len(flat) + len(extra)]
+        acc = refs[-1]
         i = pl.program_id(0)
 
         @pl.when(i == 0)
         def _():
-            acc[...] = SCALE * dot(h[...], u[...], ((1,), (1,)))
-
-        acc[...] += dot(t[...], w[...])
-
-        @pl.when(i == steps - 1)
-        def _():
-            out[...] = acc[...].astype(BF)
-
-    return call(
-        body,
-        jax.ShapeDtypeStruct((n_tok, kv), BF),
-        (steps,),
-        [
-            pl.BlockSpec((n_tok, blk), lambda i: (0, i)),
-            pl.BlockSpec((blk, kv), lambda i: (i, 0)),
-            whole((n_tok, cols)),
-            whole((kv, cols)),
-        ],
-        whole((n_tok, kv)),
-        [pltpu.VMEM((n_tok, kv), F32)],
-        flops=2 * n_tok * kv * (width + cols),
-        data=26 * MIB,
-    )(tokens, weight, hidden, up)
+            if before is not None:
+                acc[...] = more[0][...]
+            else:
+                acc[...] = jnp.zeros_like(acc)
+            if lora is not None:
+                h_a, h_b, u = more[-3:]
+                acc[:n_tok] += SCALE * dot(h_a[...], u[...], ((1,), (1,)))
+                acc[n_tok:] += SCALE * dot(h_b[...], u[...], ((1,), (1,)))
+
+        left = 0
+        for p in range(steps):
+            mine = ws[left : left + len(groups[p])]
+            left += len(groups[p])
+
+            @pl.when(i == p)
+            def _(mine=mine):
+                parts = [w[...] for w in mine]
+                w = parts[0] if len(parts) == 1 else jnp.concatenate(parts, axis=0)
+                acc[:n_tok] += dot(jnp.concatenate([t[...] for t in tok_a], axis=1), w)
+                acc[n_tok:] += dot(jnp.concatenate([t[...] for t in tok_b], axis=1), w)
+
+        if final:
+
+            @pl.when(i == steps - 1)
+            def _():
+                out[...] = acc[...].astype(BF)
+
+    tok_specs = [pl.BlockSpec((n_tok, blk), lambda i, s, k=k: (0, s[i * per + k])) for k in range(per)]
+    shape = (2 * n_tok, n)
+    return pl.pallas_call(
+        body,
+        out_shape=jax.ShapeDtypeStruct(shape, BF if final else F32),
+        grid_spec=pltpu.PrefetchScalarGridSpec(
+            num_scalar_prefetch=1,
+            grid=(steps,),
+            in_specs=tok_specs * 2 + [whole(w.shape) for w in flat] + [whole(e.shape) for e in extra],
+            out_specs=whole(shape),
+            scratch_shapes=[pltpu.VMEM(shape, F32)] if final else [],
+        ),
+        compiler_params=pltpu.CompilerParams(vmem_limit_bytes=40 * MIB),
+        cost_estimate=pl.CostEstimate(
+            flops=4 * n_tok * rows * n * steps, bytes_accessed=8 * n_tok * rows * steps, transcendentals=0
+        ),
+    )(where_from, *([own] * per), *([other] * per), *flat, *extra)
 
 
 def per_device(tokens, weight, down, up, cotangent, tasks, owned, counts):
@@ -252,10 +296,34 @@
     ny, nx, nz = lax.axis_size("y"), lax.axis_size("x"), lax.axis_size("z")
     me_c = lax.axis_index("c")
     d_rows, v_rows = width // (nx * nz * 2), kv // (nx * nz * 2)
+    me_x, me_z = lax.axis_index("x"), lax.axis_index("z")
     sc = SLOTS * RANK
     lanes = nx * (d_rows + v_rows)
-
-    full_weight = lax.all_gather(weight, ("x", "z", "c"), axis=0, tiled=True)
+    half = kv // 2
+
+    def columns(a, core):
+        return lax.dynamic_slice_in_dim(a, core * half, half, 1)
+
+    block_a = columns(weight, me_c)
+    block_b = lax.ppermute(columns(weight, 1 - me_c), "c", SWAP)
+    near_a = jnp.concatenate([block_a] + [shifted(block_a, "x", k) for k in range(1, nx)])
+    near_b = jnp.concatenate([block_b] + [shifted(block_b, "z", k) for k in range(1, nz)])
+    cut_a, cut_b = near_a.shape[0] // 2, near_b.shape[0] // 2
+    a_down, a_up = shifted(near_a, "z", 1), shifted(near_a, "z", nz - 1)
+    b_down, b_up = shifted(near_b, "x", 1), shifted(near_b, "x", nx - 1)
+    a_far = [shifted(a_down[:cut_a], "z", 1), shifted(a_up[cut_a:], "z", nz - 1)]
+    b_far = [shifted(b_down[:cut_b], "x", 1), shifted(b_up[cut_b:], "x", nx - 1)]
+
+    def blocks_a(step):
+        z = (me_z + step) % nz
+        return [(((me_x - k) % nx) * nz + z) * 2 + me_c for k in range(nx)]
+
+    def blocks_b(step):
+        x = (me_x + step) % nx
+        return [(x * nz + (me_z - k) % nz) * 2 + 1 - me_c for k in range(nz)]
+
+    def at(*lists):
+        return jnp.stack([i for one in lists for i in one]).astype(jnp.int32)
 
     ids = jnp.arange(adapters, dtype=jnp.int32)
     partner_tasks = lax.ppermute(tasks, "c", SWAP)
@@ -264,14 +332,7 @@
     rank_of = jnp.sum((ids[None, :] < ids[:, None]) & present[None, :], axis=1)
     col_slot = jnp.arange(sc, dtype=jnp.int32) // RANK
     col_rank = jnp.arange(sc, dtype=jnp.int32) % RANK
-    chosen = present[None, :] & (rank_of[None, :] == col_slot[:, None])
-    col_task = jnp.sum(jnp.where(chosen, ids[None, :] + 1, 0), axis=1) - 1
-    overflow = (jnp.sum(present.astype(jnp.int32)) > SLOTS).astype(F32)
-
     row = jnp.arange(cols, dtype=jnp.int32)
-    pick_t = ((row // RANK)[None, :] == col_task[:, None]) & ((row % RANK)[None, :] == col_rank[:, None])
-    pick_t = pick_t.astype(BF)
-    mask_slot_t = (tasks[None, :] == col_task[:, None]).astype(F32)
 
     token_count = jnp.sum(jnp.where(hit, counts.astype(F32)[None, :], 0.0), axis=1)
     scaled = (cotangent.astype(F32) * (SCALE / token_count)[:, None]).astype(BF)
@@ -284,50 +345,60 @@
     )
     scaled_by_core = dot(scaled, (v_in[:, None] == v_from[None, :]).astype(BF)).astype(BF)
 
-    up_slot_t = dot(pick_t, up, ((1,), (1,))).astype(BF)
-    low_t = (dot(up_slot_t, scaled, ((1,), (1,))) * mask_slot_t).astype(BF)
-
-    hidden, theirs, mine = terms(
-        tokens, down, low_t, scaled_by_core, tasks[:, None], pick_t, me_c.astype(jnp.int32)[None], nx, nz
+    owned_col = jnp.repeat(owned.astype(F32), RANK)[:, None]
+
+    def round_of(first, after):
+        chosen = present[None, :] & (rank_of[None, :] == first + col_slot[:, None])
+        col_task = jnp.sum(jnp.where(chosen, ids[None, :] + 1, 0), axis=1) - 1
+        more = (jnp.sum(present.astype(jnp.int32)) > first + SLOTS).astype(F32)
+        pick_t = ((row // RANK)[None, :] == col_task[:, None]) & ((row % RANK)[None, :] == col_rank[:, None])
+        pick_t = pick_t.astype(BF)
+        mask_slot_t = (tasks[None, :] == col_task[:, None]).astype(F32)
+        up_slot_t = dot(pick_t, up, ((1,), (1,))).astype(BF)
+        low_t = (dot(up_slot_t, scaled, ((1,), (1,))) * mask_slot_t).astype(BF)
+        low_t, _ = lax.optimization_barrier((low_t, after))
+        hidden, theirs, mine = terms(
+            tokens, down, low_t, scaled_by_core, tasks[:, None], pick_t, me_c.astype(jnp.int32)[None], nx, nz
+        )
+        note_row = lax.broadcasted_iota(jnp.int32, (INFO, lanes), 0)
+        note = jnp.where(note_row == 0, jnp.pad(col_task.astype(F32), (0, lanes - sc))[None, :], more)
+        got = lax.ppermute(theirs, "c", SWAP)
+        chip = pack(mine, got, note.astype(BF))
+        by_owner = spread(exchange(chip, "z"), owned_col, ny)
+        by_x = turn(exchange(by_owner, "y"), nx, d_rows)
+        grad_down, grad_up, flags = finish(exchange(by_x, "x"), d_rows)
+        return hidden, got, grad_down, grad_up, flags[0, 0]
+
+    hidden, got, grad_down, grad_up, flag = round_of(jnp.int32(0), (near_a, near_b))
+
+    sent_tokens, sent_hidden, _ = lax.optimization_barrier((tokens, hidden, got))
+    other = lax.ppermute(sent_tokens, "c", SWAP)
+    other_hidden = lax.ppermute(sent_hidden, "c", SWAP)
+    acc = add_blocks(tokens, other, [[near_a], [near_b]], at(blocks_a(0), blocks_b(0)))
+    acc = add_blocks(
+        tokens,
+        other,
+        [[a_down], [a_up], [b_down], [b_up]],
+        at(blocks_a(-1), blocks_a(1), blocks_b(-1), blocks_b(1)),
+        before=acc,
+        lora=(hidden, other_hidden, lax.dynamic_slice_in_dim(up, me_c * half, half, 0)),
     )
-
-    note_row = lax.broadcasted_iota(jnp.int32, (INFO, lanes), 0)
-    note = jnp.where(note_row == 0, jnp.pad(col_task.astype(F32), (0, lanes - sc))[None, :], overflow)
-    chip = pack(mine, lax.ppermute(theirs, "c", SWAP), note.astype(BF))
-
-    owned_col = jnp.repeat(owned.astype(F32), RANK)[:, None]
-    by_owner = spread(exchange(chip, "z"), owned_col, ny)
-    by_x = turn(exchange(by_owner, "y"), nx, d_rows)
-    grad_down, grad_up, flags = finish(exchange(by_x, "x"), d_rows)
-
-    keys = project(tokens, full_weight, hidden, up)
-
-    flag, keys = lax.optimization_barrier((flags[0, 0], keys))
-
-    def rest(grads):
-        own = cols // ny
-        left = jnp.all(tasks[:, None] != col_task[None, :], axis=1)[:, None]
-        mask = (tasks[:, None] == (row // RANK)[None, :]) & left
-        order = ((row // RANK)[:, None] == owned[row // RANK][None, :]) & (
-            (row % RANK)[:, None] == (row % RANK)[None, :]
-        )
-        order = order.astype(BF)
-        low_left = jnp.where(mask, dot(scaled, up), 0.0).astype(BF)
-        low_left = dot(low_left, order).astype(BF)
-        hid_left = dot(jnp.where(left, hidden, 0.0).astype(BF), order).astype(BF)
-
-        def summed(a, b):
-            t = lax.dot_general(
-                a, b.reshape(n_tok, ny, own), (((0,), (0,)), ((), ())), preferred_element_type=F32
-            )
-            t = jnp.transpose(t, (1, 0, 2)).reshape(-1, own)
-            for axis in ("y", "x", "z", "c"):
-                t = lax.psum_scatter(t, axis, scatter_dimension=0, tiled=True)
-            return t
-
-        return grads[0] + summed(tokens, low_left), grads[1] + summed(scaled, hid_left)
-
-    grad_down, grad_up = lax.cond(flag > 0.5, rest, lambda g: g, (grad_down, grad_up))
+    tile = add_blocks(tokens, other, [a_far, b_far], at(blocks_a(2), blocks_b(2)), before=acc, final=True)
+    back = lax.ppermute(tile[n_tok:], "c", SWAP)
+    low_half = jnp.where(me_c == 0, tile[:n_tok], back)
+    high_half = jnp.where(me_c == 0, back, tile[:n_tok])
+    keys = jnp.concatenate([low_half, high_half], axis=1)
+
+    flag, keys = lax.optimization_barrier((flag, keys))
+
+    def again(state):
+        first, down_sum, up_sum, _ = state
+        _, _, down_more, up_more, flag = round_of(first, ())
+        return first + SLOTS, down_sum + down_more, up_sum + up_more, flag
+
+    _, grad_down, grad_up, _ = lax.while_loop(
+        lambda state: state[3] > 0.5, again, (jnp.int32(SLOTS), grad_down, grad_up, flag)
+    )
     return keys, grad_down[None], grad_up[None]
 
 

time: 174 us -> 144 us (0.83)
  blocking collectives: 32.9 us -> 0 us
  starting transfers between devices: 6.11 us -> 36.7 us
  waiting for transfers between devices: 62 us -> 33.9 us
  local copies, waits for them, and re-layouts: 3.96 us -> 19.2 us
  between operations: 15.5 us -> 1.61 us
  Pallas kernels: 44.8 us -> 40.1 us
  other arithmetic: 4.14 us -> 6.27 us
    all_to_all x1 -> x3, waiting for transfers between devices: 58.4 us -> 9.26 us  [exchange(): return lax.all_to_all(a, axis, 0, 0, tiled=True)]
    all_to_all x2 -> x0, blocking collectives: 32.9 us -> none  [exchange(): return lax.all_to_all(a, axis, 0, 0, tiled=True)]
    ppermute x1 -> x19, starting transfers between devices: 0.55 us -> 25.1 us  [the longest x14 24.3 us: shifted(): return lax.ppermute(a, axis, [(i, (i + step) % n) for i in range(n)])]
    ppermute x1 -> x19, waiting for transfers between devices: 2.98 us -> 24.6 us  [the longest x14 21.7 us: shifted(): return lax.ppermute(a, axis, [(i, (i + step) % n) for i in range(n)])]
    pallas_call x1, Pallas kernels: 19.6 us -> 12.7 us  [terms(): call(body, (jax.ShapeDtypeStruct((n_tok, cols), BF), jax.ShapeDtypeStruct...]
    slice x1 -> x6, local copies, waits for them, and re-layouts: 0.51 us -> 7.07 us  [the longest x1 1.88 us: per_device(): a_up[cut_a:]]
    all_to_all x1 -> x3, starting transfers between devices: 5.43 us -> 11.6 us  [exchange(): return lax.all_to_all(a, axis, 0, 0, tiled=True)]
    unnamed x18 -> x29, local copies, waits for them, and re-layouts: 3.01 us -> 7.05 us
  transfers between devices with their start and end apart: 4 -> 23, of which waited for: 2 -> 6; matrix products, arithmetic and copies ran while one was open for 5% -> 15% of each run, Pallas kernels for 14% -> 19%
where the time goes in v3:
time: 144 us; the launch traced here: 143 us
  Pallas kernels  40.1 us (28%)
  starting transfers between devices  36.7 us (25%)
  waiting for transfers between devices  33.9 us (24%)
  local copies, waits for them, and re-layouts  19.2 us (13%)
  other arithmetic  6.27 us (4%)
  matrix products  4.35 us (3%)
  between operations  1.61 us (1%)
    ppermute x14, starting transfers between devices, shifted(): return lax.ppermute(a, axis, [(i, (i + step) % n) for i in range(n)])  24.3 us
    ppermute x14, waiting for transfers between devices, shifted(): return lax.ppermute(a, axis, [(i, (i + step) % n) for i in range(n)])  21.7 us
    pallas_call x3, Pallas kernels, add_blocks(): pl.pallas_call(body, out_shape=jax.ShapeDtypeStruct(shape, BF if final el...  21.1 us
    pallas_call x1, Pallas kernels, terms(): call(body, (jax.ShapeDtypeStruct((n_tok, cols), BF), jax.ShapeDtypeStruct...  12.7 us
    all_to_all x3, starting transfers between devices, exchange(): return lax.all_to_all(a, axis, 0, 0, tiled=True)  11.6 us
    all_to_all x3, waiting for transfers between devices, exchange(): return lax.all_to_all(a, axis, 0, 0, tiled=True)  9.26 us
    unnamed x29, local copies, waits for them, and re-layouts  7.05 us
    dot_general x2, matrix products, dot(): return lax.dot_general(a, b, (dims, ((), ())), preferred_element_type=F32)  4.35 us
  transfers between devices with their start and end apart: 23, of which 6 were waited for; matrix products, arithmetic and copies ran while one was open for 15% of the time, Pallas kernels for 19%

profile of v3, /device:TPU:0, one launch (start us, length us, event | category | flops | bytes accessed | tf_op | source)
XLA Modules:
  0.0 142.8 jit_solution(78165003305637221)
XLA Ops:
  0.6 1.1 constant_dynamic-slice_fusion
  1.7 2.9 %collective-permute-start.4 = (bf16[256,512]{1,0:T(8,128)(2,1)S(1)}, bf16[256,512]{1,0:T(8,128)(2,1)S(1)}, u32[]{:S(2)}, u32[]{:S(2)}) collective-permute-start(bf16[256,512]{1,0:T(8,128)(2,1)S(1)} %get-tuple-element.532), channel_id=1, source_target_pairs={{0,24},{8,0},{16,8},{24,16},{1,25},{9,1},{17,9},{25,17},{2,26},{10... | collective-permute-start | bytes 786440 | tf_op jit(solution)/shard_map/ppermute | solution.py:220
  4.6 0.8 collective-permute-start.3
  5.4 0.9 collective-permute-start.2
  7.0 0.8 select_reduce_fusion.1
  7.8 1.5 %multiply_convert_fusion = bf16[512,1024]{1,0:T(8,128)(2,1)S(1)} fusion(bf16[512,1024]{1,0:T(8,128)(2,1)} %param.14, f32[512]{0:T(512)S(1)} %broadcast_divide_fusion), kind=kLoop, calls=%fused_computation.42 | loop fusion | flops 1572864 | bytes 2099200 | tf_op jit(solution)/shard_map/convert_element_type | solution.py:338
  9.3 2.3 %fusion.35.sca = bf16[512,1024]{1,0:T(8,128)(2,1)} fusion(bf16[512,1024]{1,0:T(8,128)(2,1)S(1)} %multiply_convert_fusion, s32[1024]{0:T(1024)S(1)} %fusion.58), kind=kOutput, calls=%fused_computation.43 | convolution fusion | flops 1075314688 | bytes 2101248 | tf_op jit(solution)/shard_map/dot_general | solution.py:19
  12.6 2.1 %fusion.36.low = bf16[128,512]{1,0:T(8,128)(2,1)S(1)} fusion(bf16[512,1024]{1,0:T(8,128)(2,1)S(1)} %multiply_convert_fusion, bf16[1024,512]{1,0:T(8,128)(2,1)} %param.13, s32[512]{0:T(512)S(1)} %get-tuple-element.535, s32[512]{0:T(512)S(1)} %get-tuple-element.536, s32[512]{0:T(512)S(1)} %copy-done.10, s32[128]{0:T(128)S(1)} %and_select_fusion.2, ...), kind=kOutput, calls=%fused_computation.46 | convolution fusion | flops 268959744 | bytes 2235392 | tf_op jit(solution)/shard_map/dot_general | solution.py:19
  14.7 2.0 %collective-permute-start.6 = (bf16[256,512]{1,0:T(8,128)(2,1)S(1)}, bf16[256,512]{1,0:T(8,128)(2,1)S(1)}, u32[]{:S(2)}, u32[]{:S(2)}) collective-permute-start(bf16[256,512]{1,0:T(8,128)(2,1)S(1)} %collective-permute-done.5), channel_id=1, source_target_pairs={{0,2},{2,4},{4,6},{6,0},{1,3},{3,5},{5,7},{7,1},{8,10},{10,12},{12... | collective-permute-start | bytes 786440 | tf_op jit(solution)/shard_map/ppermute | solution.py:220
  16.8 3.7 %collective-permute-start.7 = (bf16[256,512]{1,0:T(8,128)(2,1)S(1)}, bf16[256,512]{1,0:T(8,128)(2,1)S(1)}, u32[]{:S(2)}, u32[]{:S(2)}) collective-permute-start(bf16[256,512]{1,0:T(8,128)(2,1)S(1)} %collective-permute-done.5), channel_id=1, source_target_pairs={{0,4},{2,6},{4,0},{6,2},{1,5},{3,7},{5,1},{7,3},{8,12},{10,14},{12... | collective-permute-start | bytes 786440 | tf_op jit(solution)/shard_map/ppermute | solution.py:220
  20.5 1.0 collective-permute-start.8
  21.5 1.0 pad_maximum_fusion.refs_8_
  22.5 0.7 constant_dynamic-update-slice_fusion.3
  23.3 2.1 %collective-permute-done.6 = bf16[256,512]{1,0:T(8,128)(2,1)S(1)} collective-permute-done((bf16[256,512]{1,0:T(8,128)(2,1)S(1)}, bf16[256,512]{1,0:T(8,128)(2,1)S(1)}, u32[]{:S(2)}, u32[]{:S(2)}) %collective-permute-start.6) | collective-permute-done | bytes 262176 | tf_op jit(solution)/shard_map/ppermute | solution.py:220
  25.3 0.7 constant_dynamic-update-slice_fusion.2
  26.0 6.1 %collective-permute-done.7 = bf16[256,512]{1,0:T(8,128)(2,1)S(1)} collective-permute-done((bf16[256,512]{1,0:T(8,128)(2,1)S(1)}, bf16[256,512]{1,0:T(8,128)(2,1)S(1)}, u32[]{:S(2)}, u32[]{:S(2)}) %collective-permute-start.7) | collective-permute-done | bytes 262176 | tf_op jit(solution)/shard_map/ppermute | solution.py:220
  32.1 0.7 constant_dynamic-update-slice_fusion.1
  32.8 0.7 constant_dynamic-update-slice_fusion.refs_9_
  33.6 12.7 %shard_map.103 = (bf16[512,512]{1,0:T(8,128)(2,1)S(1)}, bf16[4,128,1152]{2,1,0:T(8,128)(2,1)S(1)}, f32[4,128,1152]{2,1,0:T(8,128)S(1)}) custom-call(s32[1]{0:T(128)} %bitcast.me, bf16[512,8192]{1,0:T(8,128)(2,1)} %refs_3_.5, bf16[8192,512]{1,0:T(8,128)(2,1)} %dn.1, bf16[128,512]{1,0:T(8,128)(2,1)S(1)} %fusion.36.low, bf16[512,1024]{1,0:T(8,128)(2,1)S(1)} %copy-done.19, ...), custom_call_target="tpu_custom_call" | custom-call | flops 5368709120 | bytes 29360128 | tf_op jit(solution)/shard_map/pallas_call | solution.py:90
  46.3 1.4 copy-done
  47.7 2.8 %collective-permute-done.9.b = bf16[4,128,1152]{2,1,0:T(8,128)(2,1)S(1)} collective-permute-done((bf16[4,128,1152]{2,1,0:T(8,128)(2,1)S(1)}, bf16[4,128,1152]{2,1,0:T(8,128)(2,1)S(1)}, u32[]{:S(2)}, u32[]{:S(2)}) %collective-permute-start.9) | collective-permute-done | bytes 1179680 | tf_op jit(solution)/shard_map/ppermute | solution.py:365
  52.7 2.6 %collective-permute-start.13 = (bf16[1024,512]{1,0:T(8,128)(2,1)S(1)}, bf16[1024,512]{1,0:T(8,128)(2,1)}, u32[]{:S(2)}, u32[]{:S(2)}) collective-permute-start(bf16[1024,512]{1,0:T(8,128)(2,1)S(1)} %pad_maximum_fusion.refs_8_), channel_id=1, source_target_pairs={{0,6},{2,0},{4,2},{6,4},{1,7},{3,1},{5,3},{7,5},{8,14},{10,8},{12,... | collective-permute-start | bytes 3145736 | tf_op jit(solution)/shard_map/ppermute | solution.py:220
  55.3 1.8 %collective-permute-start.15 = (bf16[1024,512]{1,0:T(8,128)(2,1)}, bf16[1024,512]{1,0:T(8,128)(2,1)}, u32[]{:S(2)}, u32[]{:S(2)}) collective-permute-start(bf16[1024,512]{1,0:T(8,128)(2,1)} %constant_dynamic-update-slice_fusion.refs_9_), channel_id=1, source_target_pairs={{0,8},{8,16},{16,24},{24,0},{1,9},{9,17},{17,25},{25,1},{2,10},{10... | collective-permute-start | bytes 3145736 | tf_op jit(solution)/shard_map/ppermute | solution.py:220
  57.1 1.4 %collective-permute-start.17 = (bf16[1024,512]{1,0:T(8,128)(2,1)}, bf16[1024,512]{1,0:T(8,128)(2,1)}, u32[]{:S(2)}, u32[]{:S(2)}) collective-permute-start(bf16[1024,512]{1,0:T(8,128)(2,1)} %constant_dynamic-update-slice_fusion.refs_9_), channel_id=1, source_target_pairs={{0,24},{8,0},{16,8},{24,16},{1,25},{9,1},{17,9},{25,17},{2,26},{10... | collective-permute-start | bytes 3145736 | tf_op jit(solution)/shard_map/ppermute | solution.py:220
  58.6 1.7 %copy-done.1 = f32[4,128,1152]{2,1,0:T(8,128)S(1)} copy-done((f32[4,128,1152]{2,1,0:T(8,128)S(1)}, f32[4,128,1152]{2,1,0:T(8,128)}, u32[]{:S(2)}) %copy-start.1) | copy-done | bytes 2359320
  60.3 1.7 %shard_map.104 = bf16[4,144,1152]{2,1,0:T(8,128)(2,1)} custom-call(f32[4,128,1152]{2,1,0:T(8,128)S(1)} %copy-done.1, bf16[4,128,1152]{2,1,0:T(8,128)(2,1)S(1)} %collective-permute-done.9.b, bf16[16,1152]{1,0:T(8,128)(2,1)S(1)} %select_convert_fusion.1.c), custom_call_target="tpu_custom_call" | custom-call | bytes 10485760 | tf_op jit(solution)/shard_map/pallas_call | solution.py:123
  62.0 3.7 %all-to-all-start.3 = ((bf16[4,144,1152]{2,1,0:T(8,128)(2,1)}), bf16[4,144,1152]{2,1,0:T(8,128)(2,1)S(1)}, u32[]{:S(2)}, u32[]{:S(2)}) async-start(bf16[4,144,1152]{2,1,0:T(8,128)(2,1)} %shard_map.104), calls=%async_computation.3 | async-start | bytes 2654208 | tf_op jit(solution)/shard_map/all_to_all | solution.py:23
  65.6 13.6 %collective-permute-done.11.refs_8_ = bf16[1024,512]{1,0:T(8,128)(2,1)S(1)} collective-permute-done((bf16[1024,512]{1,0:T(8,128)(2,1)S(1)}, bf16[1024,512]{1,0:T(8,128)(2,1)S(1)}, u32[]{:S(2)}, u32[]{:S(2)}) %collective-permute-start.11) | collective-permute-done | bytes 1048608 | tf_op jit(solution)/shard_map/ppermute | solution.py:220
  79.3 0.9 broadcast_in_dim_reshape.8.ow
  80.5 1.9 %constant_dynamic-slice_fusion.2.refs_15_ = bf16[512,512]{1,0:T(8,128)(2,1)} fusion(bf16[1024,512]{1,0:T(8,128)(2,1)} %param.13, s32[]{:T(128)S(6)} %select_n.285), kind=kLoop, calls=%fused_computation.125 | loop fusion | bytes 1048580 | tf_op jit(solution)/shard_map/dynamic_slice | solution.py:384
  82.4 0.8 slice.39
  83.2 1.9 %slice.40 = bf16[512,512]{1,0:T(8,128)(2,1)} slice(bf16[1024,512]{1,0:T(8,128)(2,1)} %collective-permute-done.13.refs_9_), slice={[512:1024], [0:512]} | slice | bytes 1048576 | tf_op jit(solution)/shard_map/slice | solution.py:314
  85.1 1.9 %slice.41 = bf16[512,512]{1,0:T(8,128)(2,1)} slice(bf16[1024,512]{1,0:T(8,128)(2,1)} %collective-permute-done.15.refs_10_), slice={[0:512], [0:512]} | slice | bytes 1048576 | tf_op jit(solution)/shard_map/slice | solution.py:315
  87.0 3.2 %collective-permute-start.14 = (bf16[512,512]{1,0:T(8,128)(2,1)}, bf16[512,512]{1,0:T(8,128)(2,1)}, u32[]{:S(2)}, u32[]{:S(2)}) collective-permute-start(bf16[512,512]{1,0:T(8,128)(2,1)} %slice.40), channel_id=1, source_target_pairs={{0,6},{2,0},{4,2},{6,4},{1,7},{3,1},{5,3},{7,5},{8,14},{10,8},{12,... | collective-permute-start | bytes 1572872 | tf_op jit(solution)/shard_map/ppermute | solution.py:220
  90.2 1.9 %slice.42 = bf16[512,512]{1,0:T(8,128)(2,1)} slice(bf16[1024,512]{1,0:T(8,128)(2,1)} %collective-permute-done.17.refs_11_), slice={[512:1024], [0:512]} | slice | bytes 1048576 | tf_op jit(solution)/shard_map/slice | solution.py:315
  92.1 1.2 all-to-all-done.3.g
  93.3 0.9 copy-done.3
  94.2 3.0 %shard_map.105 = bf16[4,144,1152]{2,1,0:T(8,128)(2,1)} custom-call(bf16[4,144,1152]{2,1,0:T(8,128)(2,1)S(1)} %all-to-all-done.3.g, f32[512,1]{1,0:T(8,128)S(1)} %copy-done.3), custom_call_target="tpu_custom_call" | custom-call | flops 603979776 | bytes 5242880 | tf_op jit(solution)/shard_map/pallas_call | solution.py:155
  97.2 1.8 %collective-permute-start.16 = (bf16[512,512]{1,0:T(8,128)(2,1)}, bf16[512,512]{1,0:T(8,128)(2,1)}, u32[]{:S(2)}, u32[]{:S(2)}) collective-permute-start(bf16[512,512]{1,0:T(8,128)(2,1)} %slice.41), channel_id=1, source_target_pairs={{0,8},{8,16},{16,24},{24,0},{1,9},{9,17},{17,25},{25,1},{2,10},{10... | collective-permute-start | bytes 1572872 | tf_op jit(solution)/shard_map/ppermute | solution.py:220
  99.0 1.4 %collective-permute-start.18 = (bf16[512,512]{1,0:T(8,128)(2,1)}, bf16[512,512]{1,0:T(8,128)(2,1)}, u32[]{:S(2)}, u32[]{:S(2)}) collective-permute-start(bf16[512,512]{1,0:T(8,128)(2,1)} %slice.42), channel_id=1, source_target_pairs={{0,24},{8,0},{16,8},{24,16},{1,25},{9,1},{17,9},{25,17},{2,26},{10... | collective-permute-start | bytes 1572872 | tf_op jit(solution)/shard_map/ppermute | solution.py:220
  100.5 4.5 %all-to-all-start.4 = ((bf16[4,144,1152]{2,1,0:T(8,128)(2,1)}), bf16[4,144,1152]{2,1,0:T(8,128)(2,1)S(1)}, u32[]{:S(2)}, u32[]{:S(2)}) async-start(bf16[4,144,1152]{2,1,0:T(8,128)(2,1)} %shard_map.105), calls=%async_computation.4 | async-start | bytes 2654208 | tf_op jit(solution)/shard_map/all_to_all | solution.py:23
  104.9 5.5 %shard_map.108.refs_12_ = f32[1024,512]{1,0:T(8,128)S(1)} custom-call(s32[8]{0:T(128)S(1)} %stack.139.at, bf16[512,8192]{1,0:T(8,128)(2,1)} %refs_3_.5, bf16[512,8192]{1,0:T(8,128)(2,1)} %refs_3_.5, bf16[512,8192]{1,0:T(8,128)(2,1)} %refs_3_.5, bf16[512,8192]{1,0:T(8,128)(2,1)} %refs_3_.5, ...), custom_call_target="tpu_custom_call" | custom-call | flops 2147483648 | bytes 8388608 | tf_op jit(solution)/shard_map/pallas_call | solution.py:274
  110.5 9.8 %shard_map.109.refs_12_ = f32[1024,512]{1,0:T(8,128)S(1)} custom-call(s32[16]{0:T(128)S(1)} %stack.130.at, bf16[512,8192]{1,0:T(8,128)(2,1)} %refs_3_.5, bf16[512,8192]{1,0:T(8,128)(2,1)} %refs_3_.5, bf16[512,8192]{1,0:T(8,128)(2,1)} %refs_3_.5, bf16[512,8192]{1,0:T(8,128)(2,1)} %refs_3_.5, ...), custom_call_target="tpu_custom_call" | custom-call | flops 4294967296 | bytes 16777216 | tf_op jit(solution)/shard_map/pallas_call | solution.py:274
  120.3 5.8 %shard_map.110 = bf16[1024,512]{1,0:T(8,128)(2,1)S(1)} custom-call(s32[8]{0:T(128)S(1)} %stack.113.at, bf16[512,8192]{1,0:T(8,128)(2,1)} %refs_3_.5, bf16[512,8192]{1,0:T(8,128)(2,1)} %refs_3_.5, bf16[512,8192]{1,0:T(8,128)(2,1)} %refs_3_.5, bf16[512,8192]{1,0:T(8,128)(2,1)} %refs_3_.5, ...), custom_call_target="tpu_custom_call" | custom-call | flops 2147483648 | bytes 8388608 | tf_op jit(solution)/shard_map/pallas_call | solution.py:274
  126.3 0.9 shard_map.106
  127.2 3.5 %all-to-all-start.5 = ((bf16[4,304,128]{2,1,0:T(8,128)(2,1)}), bf16[4,304,128]{2,1,0:T(8,128)(2,1)S(1)}, u32[]{:S(2)}, u32[]{:S(2)}) async-start(bf16[4,304,128]{2,1,0:T(8,128)(2,1)} %shard_map.106), calls=%async_computation.5 | async-start | bytes 622592 | tf_op jit(solution)/shard_map/all_to_all | solution.py:23
  130.7 8.1 %all-to-all-done.5.g = bf16[4,304,128]{2,1,0:T(8,128)(2,1)S(1)} async-done(((bf16[4,304,128]{2,1,0:T(8,128)(2,1)}), bf16[4,304,128]{2,1,0:T(8,128)(2,1)S(1)}, u32[]{:S(2)}, u32[]{:S(2)}) %all-to-all-start.5) | async-done | bytes 311328 | tf_op jit(solution)/shard_map/all_to_all | solution.py:23
  140.1 1.1 pad_maximum_fusion.1
  (75 shorter events, 6.9 us)
Async XLA Ops:
  1.7 18.8 %collective-permute-start.4 = (bf16[256,512]{1,0:T(8,128)(2,1)S(1)}, bf16[256,512]{1,0:T(8,128)(2,1)S(1)}, u32[]{:S(2)}, u32[]{:S(2)}) collective-permute-start(bf16[256,512]{1,0:T(8,128)(2,1)S(1)} %get-tuple-element.532), channel_id=1, source_target_pairs={{0,24},{8,0},{16,8},{24,16},{1,25},{9,1},{17,9},{25,17},{2,26},{10... | collective-permute-start | bytes 786440 | tf_op jit(solution)/shard_map/ppermute | solution.py:220
  4.6 16.9 %collective-permute-start.3 = (bf16[256,512]{1,0:T(8,128)(2,1)S(1)}, bf16[256,512]{1,0:T(8,128)(2,1)S(1)}, u32[]{:S(2)}, u32[]{:S(2)}) collective-permute-start(bf16[256,512]{1,0:T(8,128)(2,1)S(1)} %get-tuple-element.532), channel_id=1, source_target_pairs={{0,16},{8,24},{16,0},{24,8},{1,17},{9,25},{17,1},{25,9},{2,18},{10... | collective-permute-start | bytes 786440 | tf_op jit(solution)/shard_map/ppermute | solution.py:220
  5.4 16.1 %collective-permute-start.2 = (bf16[256,512]{1,0:T(8,128)(2,1)S(1)}, bf16[256,512]{1,0:T(8,128)(2,1)}, u32[]{:S(2)}, u32[]{:S(2)}) collective-permute-start(bf16[256,512]{1,0:T(8,128)(2,1)S(1)} %get-tuple-element.532), channel_id=1, source_target_pairs={{0,8},{8,16},{16,24},{24,0},{1,9},{9,17},{17,25},{25,1},{2,10},{10... | collective-permute-start | bytes 786440 | tf_op jit(solution)/shard_map/ppermute | solution.py:220
  6.3 6.0 %collective-permute-start.1 = (s32[512]{0:T(512)}, s32[512]{0:T(512)S(1)}, u32[]{:S(2)}, u32[]{:S(2)}) collective-permute-start(s32[512]{0:T(512)} %param.15), channel_id=1, source_target_pairs={{0,1},{1,0},{2,3},{3,2},{4,5},{5,4},{6,7},{7,6},{8,9},{9,8},{10,11... | collective-permute-start | bytes 6152 | tf_op jit(solution)/shard_map/ppermute | solution.py:329
  9.2 3.4 %copy-start.6 = (bf16[512,1024]{1,0:T(8,128)(2,1)}, bf16[512,1024]{1,0:T(8,128)(2,1)S(1)}, u32[]{:S(2)}) copy-start(bf16[512,1024]{1,0:T(8,128)(2,1)S(1)} %multiply_convert_fusion) | copy-start | bytes 3145732
  9.3 2.3 %copy-start.10 = (s32[512]{0:T(512)S(1)}, s32[512]{0:T(512)}, u32[]{:S(2)}) copy-start(s32[512]{0:T(512)} %param.15) | copy-start | bytes 6148
  11.7 3.0 %collective-permute-start.5 = (bf16[256,512]{1,0:T(8,128)(2,1)S(1)}, bf16[256,512]{1,0:T(8,128)(2,1)S(1)}, u32[]{:S(2)}, u32[]{:S(2)}) collective-permute-start(bf16[256,512]{1,0:T(8,128)(2,1)S(1)} %get-tuple-element.531), channel_id=1, source_target_pairs={{0,1},{1,0},{2,3},{3,2},{4,5},{5,4},{6,7},{7,6},{8,9},{9,8},{10,11... | collective-permute-start | bytes 786440 | tf_op jit(solution)/shard_map/ppermute | solution.py:308
  14.7 10.6 %collective-permute-start.6 = (bf16[256,512]{1,0:T(8,128)(2,1)S(1)}, bf16[256,512]{1,0:T(8,128)(2,1)S(1)}, u32[]{:S(2)}, u32[]{:S(2)}) collective-permute-start(bf16[256,512]{1,0:T(8,128)(2,1)S(1)} %collective-permute-done.5), channel_id=1, source_target_pairs={{0,2},{2,4},{4,6},{6,0},{1,3},{3,5},{5,7},{7,1},{8,10},{10,12},{12... | collective-permute-start | bytes 786440 | tf_op jit(solution)/shard_map/ppermute | solution.py:220
  16.8 16.7 %copy-start.19 = (bf16[512,1024]{1,0:T(8,128)(2,1)S(1)}, bf16[512,1024]{1,0:T(8,128)(2,1)}, u32[]{:S(2)}) copy-start(bf16[512,1024]{1,0:T(8,128)(2,1)} %fusion.35.sca) | copy-start | bytes 3145732
  16.8 15.3 %collective-permute-start.7 = (bf16[256,512]{1,0:T(8,128)(2,1)S(1)}, bf16[256,512]{1,0:T(8,128)(2,1)S(1)}, u32[]{:S(2)}, u32[]{:S(2)}) collective-permute-start(bf16[256,512]{1,0:T(8,128)(2,1)S(1)} %collective-permute-done.5), channel_id=1, source_target_pairs={{0,4},{2,6},{4,0},{6,2},{1,5},{3,7},{5,1},{7,3},{8,12},{10,14},{12... | collective-permute-start | bytes 786440 | tf_op jit(solution)/shard_map/ppermute | solution.py:220
  20.5 12.3 %collective-permute-start.8 = (bf16[256,512]{1,0:T(8,128)(2,1)S(1)}, bf16[256,512]{1,0:T(8,128)(2,1)S(1)}, u32[]{:S(2)}, u32[]{:S(2)}) collective-permute-start(bf16[256,512]{1,0:T(8,128)(2,1)S(1)} %collective-permute-done.5), channel_id=1, source_target_pairs={{0,6},{2,0},{4,2},{6,4},{1,7},{3,1},{5,3},{7,5},{8,14},{10,8},{12,... | collective-permute-start | bytes 786440 | tf_op jit(solution)/shard_map/ppermute | solution.py:220
  46.3 1.4 copy-start
  47.7 2.9 %copy-start.4 = (bf16[512,512]{1,0:T(8,128)(2,1)}, bf16[512,512]{1,0:T(8,128)(2,1)S(1)}, u32[]{:S(2)}) copy-start(bf16[512,512]{1,0:T(8,128)(2,1)S(1)} %get-tuple-element.397.refs_13_) | copy-start | bytes 1572868
  47.7 2.8 %collective-permute-start.9 = (bf16[4,128,1152]{2,1,0:T(8,128)(2,1)S(1)}, bf16[4,128,1152]{2,1,0:T(8,128)(2,1)S(1)}, u32[]{:S(2)}, u32[]{:S(2)}) collective-permute-start(bf16[4,128,1152]{2,1,0:T(8,128)(2,1)S(1)} %get-tuple-element.393), channel_id=1, source_target_pairs={{0,1},{1,0},{2,3},{3,2},{4,5},{5,4},{6,7},{7,6},{8,9},{9,8},{10,11... | collective-permute-start | bytes 3538952 | tf_op jit(solution)/shard_map/ppermute | solution.py:365
  50.5 48.5 %collective-permute-start.10 = (bf16[512,8192]{1,0:T(8,128)(2,1)}, bf16[512,8192]{1,0:T(8,128)(2,1)}, u32[]{:S(2)}, u32[]{:S(2)}) collective-permute-start(bf16[512,8192]{1,0:T(8,128)(2,1)} %refs_3_.5), channel_id=1, source_target_pairs={{0,1},{1,0},{2,3},{3,2},{4,5},{5,4},{6,7},{7,6},{8,9},{9,8},{10,11... | collective-permute-start | bytes 25165832 | tf_op jit(solution)/shard_map/ppermute | solution.py:375
  52.0 27.3 %collective-permute-start.11 = (bf16[1024,512]{1,0:T(8,128)(2,1)S(1)}, bf16[1024,512]{1,0:T(8,128)(2,1)S(1)}, u32[]{:S(2)}, u32[]{:S(2)}) collective-permute-start(bf16[1024,512]{1,0:T(8,128)(2,1)S(1)} %pad_maximum_fusion.refs_8_), channel_id=1, source_target_pairs={{0,2},{2,4},{4,6},{6,0},{1,3},{3,5},{5,7},{7,1},{8,10},{10,12},{12... | collective-permute-start | bytes 3145736 | tf_op jit(solution)/shard_map/ppermute | solution.py:220
  52.7 30.6 %collective-permute-start.13 = (bf16[1024,512]{1,0:T(8,128)(2,1)S(1)}, bf16[1024,512]{1,0:T(8,128)(2,1)}, u32[]{:S(2)}, u32[]{:S(2)}) collective-permute-start(bf16[1024,512]{1,0:T(8,128)(2,1)S(1)} %pad_maximum_fusion.refs_8_), channel_id=1, source_target_pairs={{0,6},{2,0},{4,2},{6,4},{1,7},{3,1},{5,3},{7,5},{8,14},{10,8},{12,... | collective-permute-start | bytes 3145736 | tf_op jit(solution)/shard_map/ppermute | solution.py:220
  55.3 29.9 %collective-permute-start.15 = (bf16[1024,512]{1,0:T(8,128)(2,1)}, bf16[1024,512]{1,0:T(8,128)(2,1)}, u32[]{:S(2)}, u32[]{:S(2)}) collective-permute-start(bf16[1024,512]{1,0:T(8,128)(2,1)} %constant_dynamic-update-slice_fusion.refs_9_), channel_id=1, source_target_pairs={{0,8},{8,16},{16,24},{24,0},{1,9},{9,17},{17,25},{25,1},{2,10},{10... | collective-permute-start | bytes 3145736 | tf_op jit(solution)/shard_map/ppermute | solution.py:220
  57.1 33.2 %collective-permute-start.17 = (bf16[1024,512]{1,0:T(8,128)(2,1)}, bf16[1024,512]{1,0:T(8,128)(2,1)}, u32[]{:S(2)}, u32[]{:S(2)}) collective-permute-start(bf16[1024,512]{1,0:T(8,128)(2,1)} %constant_dynamic-update-slice_fusion.refs_9_), channel_id=1, source_target_pairs={{0,24},{8,0},{16,8},{24,16},{1,25},{9,1},{17,9},{25,17},{2,26},{10... | collective-permute-start | bytes 3145736 | tf_op jit(solution)/shard_map/ppermute | solution.py:220
  58.6 1.7 %copy-start.1 = (f32[4,128,1152]{2,1,0:T(8,128)S(1)}, f32[4,128,1152]{2,1,0:T(8,128)}, u32[]{:S(2)}) copy-start(f32[4,128,1152]{2,1,0:T(8,128)} %copy-done) | copy-start | bytes 7077892
  62.0 17.3 %copy-start.18 = (s32[8]{0:T(128)S(1)}, s32[8]{0:T(128)}, u32[]{:S(2)}) copy-start(s32[8]{0:T(128)} %param.16) | copy-start | bytes 100
  62.0 31.3 %all-to-all-start.3 = ((bf16[4,144,1152]{2,1,0:T(8,128)(2,1)}), bf16[4,144,1152]{2,1,0:T(8,128)(2,1)S(1)}, u32[]{:S(2)}, u32[]{:S(2)}) async-start(bf16[4,144,1152]{2,1,0:T(8,128)(2,1)} %shard_map.104), calls=%async_computation.3 | async-start | bytes 2654208 | tf_op jit(solution)/shard_map/all_to_all | solution.py:23
  79.2 31.2 %collective-permute-start.19 = (bf16[512,512]{1,0:T(8,128)(2,1)}, bf16[512,512]{1,0:T(8,128)(2,1)}, u32[]{:S(2)}, u32[]{:S(2)}) collective-permute-start(bf16[512,512]{1,0:T(8,128)(2,1)} %copy-done.4), channel_id=1, source_target_pairs={{0,1},{1,0},{2,3},{3,2},{4,5},{5,4},{6,7},{7,6},{8,9},{9,8},{10,11... | collective-permute-start | bytes 1572872 | tf_op jit(solution)/shard_map/ppermute | solution.py:376
  79.2 1.0 copy-start.16
  85.1 35.1 %collective-permute-start.12 = (bf16[512,512]{1,0:T(8,128)(2,1)}, bf16[512,512]{1,0:T(8,128)(2,1)}, u32[]{:S(2)}, u32[]{:S(2)}) collective-permute-start(bf16[512,512]{1,0:T(8,128)(2,1)} %slice.39), channel_id=1, source_target_pairs={{0,2},{2,4},{4,6},{6,0},{1,3},{3,5},{5,7},{7,1},{8,10},{10,12},{12... | collective-permute-start | bytes 1572872 | tf_op jit(solution)/shard_map/ppermute | solution.py:220
  87.0 33.3 %collective-permute-start.14 = (bf16[512,512]{1,0:T(8,128)(2,1)}, bf16[512,512]{1,0:T(8,128)(2,1)}, u32[]{:S(2)}, u32[]{:S(2)}) collective-permute-start(bf16[512,512]{1,0:T(8,128)(2,1)} %slice.40), channel_id=1, source_target_pairs={{0,6},{2,0},{4,2},{6,4},{1,7},{3,1},{5,3},{7,5},{8,14},{10,8},{12,... | collective-permute-start | bytes 1572872 | tf_op jit(solution)/shard_map/ppermute | solution.py:220
  93.3 1.0 copy-start.3
  97.2 23.1 %collective-permute-start.16 = (bf16[512,512]{1,0:T(8,128)(2,1)}, bf16[512,512]{1,0:T(8,128)(2,1)}, u32[]{:S(2)}, u32[]{:S(2)}) collective-permute-start(bf16[512,512]{1,0:T(8,128)(2,1)} %slice.41), channel_id=1, source_target_pairs={{0,8},{8,16},{16,24},{24,0},{1,9},{9,17},{17,25},{25,1},{2,10},{10... | collective-permute-start | bytes 1572872 | tf_op jit(solution)/shard_map/ppermute | solution.py:220
  99.0 21.3 %collective-permute-start.18 = (bf16[512,512]{1,0:T(8,128)(2,1)}, bf16[512,512]{1,0:T(8,128)(2,1)}, u32[]{:S(2)}, u32[]{:S(2)}) collective-permute-start(bf16[512,512]{1,0:T(8,128)(2,1)} %slice.42), channel_id=1, source_target_pairs={{0,24},{8,0},{16,8},{24,16},{1,25},{9,1},{17,9},{25,17},{2,26},{10... | collective-permute-start | bytes 1572872 | tf_op jit(solution)/shard_map/ppermute | solution.py:220
  100.5 25.8 %all-to-all-start.4 = ((bf16[4,144,1152]{2,1,0:T(8,128)(2,1)}), bf16[4,144,1152]{2,1,0:T(8,128)(2,1)S(1)}, u32[]{:S(2)}, u32[]{:S(2)}) async-start(bf16[4,144,1152]{2,1,0:T(8,128)(2,1)} %shard_map.105), calls=%async_computation.4 | async-start | bytes 2654208 | tf_op jit(solution)/shard_map/all_to_all | solution.py:23
  104.9 5.5 %copy-start.2 = (bf16[512,512]{1,0:T(8,128)(2,1)S(1)}, bf16[512,512]{1,0:T(8,128)(2,1)}, u32[]{:S(2)}) copy-start(bf16[512,512]{1,0:T(8,128)(2,1)} %constant_dynamic-slice_fusion.2.refs_15_) | copy-start | bytes 1572868
  104.9 5.5 %copy-start.5 = (bf16[512,512]{1,0:T(8,128)(2,1)S(1)}, bf16[512,512]{1,0:T(8,128)(2,1)}, u32[]{:S(2)}) copy-start(bf16[512,512]{1,0:T(8,128)(2,1)} %copy-done.4) | copy-start | bytes 1572868
  126.2 13.9 %collective-permute-start.20 = (bf16[512,512]{1,0:T(8,128)(2,1)S(1)}, bf16[512,512]{1,0:T(8,128)(2,1)S(1)}, u32[]{:S(2)}, u32[]{:S(2)}) collective-permute-start(bf16[512,512]{1,0:T(8,128)(2,1)S(1)} %slice.44), channel_id=1, source_target_pairs={{0,1},{1,0},{2,3},{3,2},{4,5},{5,4},{6,7},{7,6},{8,9},{9,8},{10,11... | collective-permute-start | bytes 1572872 | tf_op jit(solution)/shard_map/ppermute | solution.py:387
  127.2 11.6 %all-to-all-start.5 = ((bf16[4,304,128]{2,1,0:T(8,128)(2,1)}), bf16[4,304,128]{2,1,0:T(8,128)(2,1)S(1)}, u32[]{:S(2)}, u32[]{:S(2)}) async-start(bf16[4,304,128]{2,1,0:T(8,128)(2,1)} %shard_map.106), calls=%async_computation.5 | async-start | bytes 622592 | tf_op jit(solution)/shard_map/all_to_all | solution.py:23
  140.0 1.4 %copy-start.7 = (bf16[512,1024]{1,0:T(8,128)(2,1)S(1)}, bf16[512,1024]{1,0:T(8,128)(2,1)}, u32[]{:S(2)}) copy-start(bf16[512,1024]{1,0:T(8,128)(2,1)} %copy-done.6) | copy-start | bytes 3145732
  142.2 0.6 copy-start.9

commit v4 on v3

--- a/solution.py
+++ b/solution.py
@@ -45,7 +45,7 @@
     cols = down.shape[1]
     sc = low_t.shape[0]
     kv = scaled.shape[1]
-    per = 2
+    per = 4
     steps = nx * nz // per
     blk = width // steps
     d = width // (nx * nz * 2)
@@ -72,7 +72,7 @@
             x, z = (i * per + k) // nz, (i * per + k) % nz
             at = pl.ds(pl.multiple_of(x * d, d), d)
             a, b = r[:, 2 * k * d : (2 * k + 1) * d], r[:, (2 * k + 1) * d : (2 * k + 2) * d]
-            mine[z, :, at] = jnp.where(first, a, b)
+            mine[z, :, at] = jnp.where(first, a, b).astype(BF)
             theirs[z, :, at] = jnp.where(first, b, a).astype(BF)
 
         @pl.when(i == steps - 1)
@@ -84,7 +84,7 @@
             g = dot(h_t, sca[...])
             for k in range(nz):
                 a, b = g[:, k * u : (k + 1) * u], g[:, half + k * u : half + (k + 1) * u]
-                mine[k, :, nx * d :] = jnp.where(first, a, b)
+                mine[k, :, nx * d :] = jnp.where(first, a, b).astype(BF)
                 theirs[k, :, nx * d :] = jnp.where(first, b, a).astype(BF)
 
     return call(
@@ -92,7 +92,7 @@
         (
             jax.ShapeDtypeStruct((n_tok, cols), BF),
             jax.ShapeDtypeStruct((nz, sc, lanes), BF),
-            jax.ShapeDtypeStruct((nz, sc, lanes), F32),
+            jax.ShapeDtypeStruct((nz, sc, lanes), BF),
         ),
         (steps,),
         [
@@ -116,7 +116,7 @@
     n, sc, lanes = mine.shape
 
     def body(a, b, c, out):
-        out[0, :sc] = (a[0] + b[0].astype(F32)).astype(BF)
+        out[0, :sc] = (a[0].astype(F32) + b[0].astype(F32)).astype(BF)
         out[0, sc:] = c[...]
 
     block = pl.BlockSpec((1, sc, lanes), lambda i: (i, 0, 0))
@@ -306,14 +306,9 @@
 
     block_a = columns(weight, me_c)
     block_b = lax.ppermute(columns(weight, 1 - me_c), "c", SWAP)
-    near_a = jnp.concatenate([block_a] + [shifted(block_a, "x", k) for k in range(1, nx)])
-    near_b = jnp.concatenate([block_b] + [shifted(block_b, "z", k) for k in range(1, nz)])
-    cut_a, cut_b = near_a.shape[0] // 2, near_b.shape[0] // 2
-    a_down, a_up = shifted(near_a, "z", 1), shifted(near_a, "z", nz - 1)
-    b_down, b_up = shifted(near_b, "x", 1), shifted(near_b, "x", nx - 1)
-    a_far = [shifted(a_down[:cut_a], "z", 1), shifted(a_up[cut_a:], "z", nz - 1)]
-    b_far = [shifted(b_down[:cut_b], "x", 1), shifted(b_up[cut_b:], "x", nx - 1)]
-
+    partner_tasks = lax.ppermute(tasks, "c", SWAP)
+    block_b, partner_tasks, cotangent, counts = lax.optimization_barrier((block_b, partner_tasks, cotangent, counts))
+    first_hop = [shifted(block_a, "x", k) for k in range(1, nx)] + [shifted(block_b, "z", k) for k in range(1, nz)]
     def blocks_a(step):
         z = (me_z + step) % nz
         return [(((me_x - k) % nx) * nz + z) * 2 + me_c for k in range(nx)]
@@ -326,7 +321,6 @@
         return jnp.stack([i for one in lists for i in one]).astype(jnp.int32)
 
     ids = jnp.arange(adapters, dtype=jnp.int32)
-    partner_tasks = lax.ppermute(tasks, "c", SWAP)
     hit = tasks[:, None] == ids[None, :]
     present = jnp.any(hit | (partner_tasks[:, None] == ids[None, :]), axis=0)
     rank_of = jnp.sum((ids[None, :] < ids[:, None]) & present[None, :], axis=1)
@@ -347,7 +341,7 @@
 
     owned_col = jnp.repeat(owned.astype(F32), RANK)[:, None]
 
-    def round_of(first, after):
+    def local_terms(first):
         chosen = present[None, :] & (rank_of[None, :] == first + col_slot[:, None])
         col_task = jnp.sum(jnp.where(chosen, ids[None, :] + 1, 0), axis=1) - 1
         more = (jnp.sum(present.astype(jnp.int32)) > first + SLOTS).astype(F32)
@@ -356,25 +350,32 @@
         mask_slot_t = (tasks[None, :] == col_task[:, None]).astype(F32)
         up_slot_t = dot(pick_t, up, ((1,), (1,))).astype(BF)
         low_t = (dot(up_slot_t, scaled, ((1,), (1,))) * mask_slot_t).astype(BF)
-        low_t, _ = lax.optimization_barrier((low_t, after))
         hidden, theirs, mine = terms(
             tokens, down, low_t, scaled_by_core, tasks[:, None], pick_t, me_c.astype(jnp.int32)[None], nx, nz
         )
         note_row = lax.broadcasted_iota(jnp.int32, (INFO, lanes), 0)
         note = jnp.where(note_row == 0, jnp.pad(col_task.astype(F32), (0, lanes - sc))[None, :], more)
-        got = lax.ppermute(theirs, "c", SWAP)
-        chip = pack(mine, got, note.astype(BF))
-        by_owner = spread(exchange(chip, "z"), owned_col, ny)
-        by_x = turn(exchange(by_owner, "y"), nx, d_rows)
-        grad_down, grad_up, flags = finish(exchange(by_x, "x"), d_rows)
-        return hidden, got, grad_down, grad_up, flags[0, 0]
-
-    hidden, got, grad_down, grad_up, flag = round_of(jnp.int32(0), (near_a, near_b))
+        return hidden, theirs, mine, note.astype(BF)
+
+    hidden, theirs, mine, note = local_terms(jnp.int32(0))
+    first_hop, theirs = lax.optimization_barrier((first_hop, theirs))
+    got = lax.ppermute(theirs, "c", SWAP)
+    near_a = jnp.concatenate([block_a] + first_hop[: nx - 1])
+    near_b = jnp.concatenate([block_b] + first_hop[nx - 1 :])
+    cut_a, cut_b = near_a.shape[0] // 2, near_b.shape[0] // 2
+    a_down, a_up = shifted(near_a, "z", 1), shifted(near_a, "z", nz - 1)
+    b_down, b_up = shifted(near_b, "x", 1), shifted(near_b, "x", nx - 1)
+    a_far = [shifted(a_down[:cut_a], "z", 1), shifted(a_up[cut_a:], "z", nz - 1)]
+    b_far = [shifted(b_down[:cut_b], "x", 1), shifted(b_up[cut_b:], "x", nx - 1)]
+
+    from_z = exchange(pack(mine, got, note), "z")
 
     sent_tokens, sent_hidden, _ = lax.optimization_barrier((tokens, hidden, got))
     other = lax.ppermute(sent_tokens, "c", SWAP)
     other_hidden = lax.ppermute(sent_hidden, "c", SWAP)
     acc = add_blocks(tokens, other, [[near_a], [near_b]], at(blocks_a(0), blocks_b(0)))
+    from_z, acc = lax.optimization_barrier((from_z, acc))
+    from_y = exchange(spread(from_z, owned_col, ny), "y")
     acc = add_blocks(
         tokens,
         other,
@@ -383,18 +384,23 @@
         before=acc,
         lora=(hidden, other_hidden, lax.dynamic_slice_in_dim(up, me_c * half, half, 0)),
     )
+    from_y, acc = lax.optimization_barrier((from_y, acc))
+    grad_down, grad_up, flags = finish(exchange(turn(from_y, nx, d_rows), "x"), d_rows)
     tile = add_blocks(tokens, other, [a_far, b_far], at(blocks_a(2), blocks_b(2)), before=acc, final=True)
     back = lax.ppermute(tile[n_tok:], "c", SWAP)
     low_half = jnp.where(me_c == 0, tile[:n_tok], back)
     high_half = jnp.where(me_c == 0, back, tile[:n_tok])
     keys = jnp.concatenate([low_half, high_half], axis=1)
 
-    flag, keys = lax.optimization_barrier((flag, keys))
+    flag, keys = lax.optimization_barrier((flags[0, 0], keys))
 
     def again(state):
         first, down_sum, up_sum, _ = state
-        _, _, down_more, up_more, flag = round_of(first, ())
-        return first + SLOTS, down_sum + down_more, up_sum + up_more, flag
+        _, theirs, mine, note = local_terms(first)
+        by_owner = spread(exchange(pack(mine, lax.ppermute(theirs, "c", SWAP), note), "z"), owned_col, ny)
+        by_x = turn(exchange(by_owner, "y"), nx, d_rows)
+        down_more, up_more, flags = finish(exchange(by_x, "x"), d_rows)
+        return first + SLOTS, down_sum + down_more, up_sum + up_more, flags[0, 0]
 
     _, grad_down, grad_up, _ = lax.while_loop(
         lambda state: state[3] > 0.5, again, (jnp.int32(SLOTS), grad_down, grad_up, flag)

time: 144 us -> 130 us (0.903)
  waiting for transfers between devices: 33.9 us -> 18.3 us
  local copies, waits for them, and re-layouts: 19.2 us -> 22.1 us
  Pallas kernels: 40.1 us -> 38.1 us
    ppermute x14, waiting for transfers between devices: 21.7 us -> 7.21 us  [shifted(): return lax.ppermute(a, axis, [(i, (i + step) % n) for i in range(n)])]
    unnamed x29 -> x45, local copies, waits for them, and re-layouts: 7.05 us -> 9.72 us
    dynamic_slice x1, local copies, waits for them, and re-layouts: 1.88 us -> 0.03 us  [per_device(): lax.dynamic_slice_in_dim(up, me_c * half, half, 0)]
    pallas_call x1, Pallas kernels: 12.7 us -> 10.9 us  [terms(): call(body, (jax.ShapeDtypeStruct((n_tok, cols), BF), jax.ShapeDtypeStruct...]
  transfers between devices with their start and end apart: 23 -> 23, of which waited for: 6 -> 5; matrix products, arithmetic and copies ran while one was open for 15% -> 17% of each run, Pallas kernels for 19% -> 25%
where the time goes in v4:
time: 130 us; the launch traced here: 129 us
  Pallas kernels  38.1 us (29%)
  starting transfers between devices  37.6 us (29%)
  local copies, waits for them, and re-layouts  22.1 us (17%)
  waiting for transfers between devices  18.3 us (14%)
  other arithmetic  6.84 us (5%)
  matrix products  3.18 us (2%)
  between operations  1.81 us (1%)
    ppermute x14, starting transfers between devices, shifted(): return lax.ppermute(a, axis, [(i, (i + step) % n) for i in range(n)])  25.3 us
    pallas_call x3, Pallas kernels, add_blocks(): pl.pallas_call(body, out_shape=jax.ShapeDtypeStruct(shape, BF if final el...  21.5 us
    all_to_all x3, starting transfers between devices, exchange(): return lax.all_to_all(a, axis, 0, 0, tiled=True)  11.6 us
    pallas_call x1, Pallas kernels, terms(): call(body, (jax.ShapeDtypeStruct((n_tok, cols), BF), jax.ShapeDtypeStruct...  10.9 us
    unnamed x45, local copies, waits for them, and re-layouts  9.72 us
    all_to_all x3, waiting for transfers between devices, exchange(): return lax.all_to_all(a, axis, 0, 0, tiled=True)  8.21 us
    ppermute x14, waiting for transfers between devices, shifted(): return lax.ppermute(a, axis, [(i, (i + step) % n) for i in range(n)])  7.21 us
    dot_general x2, matrix products, dot(): return lax.dot_general(a, b, (dims, ((), ())), preferred_element_type=F32)  3.18 us
  transfers between devices with their start and end apart: 23, of which 5 were waited for; matrix products, arithmetic and copies ran while one was open for 17% of the time, Pallas kernels for 25%

profile of v4, /device:TPU:0, one launch (start us, length us, event | category | flops | bytes accessed | tf_op | source)
XLA Modules:
  0.0 128.5 jit_solution(8872181242185668293)
XLA Ops:
  0.6 1.2 constant_dynamic-slice_fusion.1
  1.8 1.6 %collective-permute-start.3 = (bf16[256,512]{1,0:T(8,128)(2,1)S(1)}, bf16[256,512]{1,0:T(8,128)(2,1)}, u32[]{:S(2)}, u32[]{:S(2)}) collective-permute-start(bf16[256,512]{1,0:T(8,128)(2,1)S(1)} %get-tuple-element.559), channel_id=1, source_target_pairs={{0,8},{8,16},{16,24},{24,0},{1,9},{9,17},{17,25},{25,1},{2,10},{10... | collective-permute-start | bytes 786440 | tf_op jit(solution)/shard_map/ppermute | solution.py:220
  3.4 2.7 %collective-permute-start.4 = (bf16[256,512]{1,0:T(8,128)(2,1)S(1)}, bf16[256,512]{1,0:T(8,128)(2,1)}, u32[]{:S(2)}, u32[]{:S(2)}) collective-permute-start(bf16[256,512]{1,0:T(8,128)(2,1)S(1)} %get-tuple-element.559), channel_id=1, source_target_pairs={{0,16},{8,24},{16,0},{24,8},{1,17},{9,25},{17,1},{25,9},{2,18},{10... | collective-permute-start | bytes 786440 | tf_op jit(solution)/shard_map/ppermute | solution.py:220
  6.7 0.8 copy.17.task
  7.5 1.5 %collective-permute-start.5 = (bf16[256,512]{1,0:T(8,128)(2,1)S(1)}, bf16[256,512]{1,0:T(8,128)(2,1)}, u32[]{:S(2)}, u32[]{:S(2)}) collective-permute-start(bf16[256,512]{1,0:T(8,128)(2,1)S(1)} %get-tuple-element.559), channel_id=1, source_target_pairs={{0,24},{8,0},{16,8},{24,16},{1,25},{9,1},{17,9},{25,17},{2,26},{10... | collective-permute-start | bytes 786440 | tf_op jit(solution)/shard_map/ppermute | solution.py:220
  9.7 0.8 select_reduce_fusion.1
  10.5 0.8 fusion.47
  11.5 2.0 %collective-permute-start.6 = (bf16[256,512]{1,0:T(8,128)(2,1)S(1)}, bf16[256,512]{1,0:T(8,128)(2,1)}, u32[]{:S(2)}, u32[]{:S(2)}) collective-permute-start(bf16[256,512]{1,0:T(8,128)(2,1)S(1)} %collective-permute-done.1), channel_id=1, source_target_pairs={{0,2},{2,4},{4,6},{6,0},{1,3},{3,5},{5,7},{7,1},{8,10},{10,12},{12... | collective-permute-start | bytes 786440 | tf_op jit(solution)/shard_map/ppermute | solution.py:220
  13.8 2.4 %fusion.35.sca = bf16[512,1024]{1,0:T(8,128)(2,1)} fusion(bf16[512,1024]{1,0:T(8,128)(2,1)S(1)} %multiply_convert_fusion, s32[1024]{0:T(1024)S(1)} %fusion.58), kind=kOutput, calls=%fused_computation.43 | convolution fusion | flops 1075314688 | bytes 2101248 | tf_op jit(solution)/shard_map/dot_general | solution.py:19
  16.3 0.8 fusion.36.low
  17.1 3.7 %collective-permute-start.7 = (bf16[256,512]{1,0:T(8,128)(2,1)S(1)}, bf16[256,512]{1,0:T(8,128)(2,1)S(1)}, u32[]{:S(2)}, u32[]{:S(2)}) collective-permute-start(bf16[256,512]{1,0:T(8,128)(2,1)S(1)} %collective-permute-done.1), channel_id=1, source_target_pairs={{0,4},{2,6},{4,0},{6,2},{1,5},{3,7},{5,1},{7,3},{8,12},{10,14},{12... | collective-permute-start | bytes 786440 | tf_op jit(solution)/shard_map/ppermute | solution.py:220
  20.8 1.0 collective-permute-start.8
  21.8 10.9 %shard_map.103 = (bf16[512,512]{1,0:T(8,128)(2,1)S(1)}, bf16[4,128,1152]{2,1,0:T(8,128)(2,1)S(1)}, bf16[4,128,1152]{2,1,0:T(8,128)(2,1)S(1)}) custom-call(s32[1]{0:T(128)} %bitcast.me, bf16[512,8192]{1,0:T(8,128)(2,1)} %refs_3_.5, bf16[8192,512]{1,0:T(8,128)(2,1)} %dn.1, bf16[128,512]{1,0:T(8,128)(2,1)S(1)} %fusion.36.low, bf16[512,1024]{1,0:T(8,128)(2,1)} %fusion.35.sca, ...), custom_call_target="tpu_custom_call" | custom-call | flops 5368709120 | bytes 29360128 | tf_op jit(solution)/shard_map/pallas_call | solution.py:90
  32.7 0.8 copy-done.14
  33.5 0.7 copy-done.16
  34.2 2.8 %collective-permute-done.9.b = bf16[4,128,1152]{2,1,0:T(8,128)(2,1)S(1)} collective-permute-done((bf16[4,128,1152]{2,1,0:T(8,128)(2,1)S(1)}, bf16[4,128,1152]{2,1,0:T(8,128)(2,1)S(1)}, u32[]{:S(2)}, u32[]{:S(2)}) %collective-permute-start.9) | collective-permute-done | bytes 1179680 | tf_op jit(solution)/shard_map/ppermute | solution.py:362
  38.5 0.7 constant_dynamic-update-slice_fusion.3
  39.3 1.8 %shard_map.104 = bf16[4,144,1152]{2,1,0:T(8,128)(2,1)} custom-call(bf16[4,128,1152]{2,1,0:T(8,128)(2,1)S(1)} %get-tuple-element.408.a, bf16[4,128,1152]{2,1,0:T(8,128)(2,1)S(1)} %collective-permute-done.9.b, bf16[16,1152]{1,0:T(8,128)(2,1)S(1)} %select_convert_fusion.1.c), custom_call_target="tpu_custom_call" | custom-call | bytes 10485760 | tf_op jit(solution)/shard_map/pallas_call | solution.py:123
  41.1 3.7 %all-to-all-start.3 = ((bf16[4,144,1152]{2,1,0:T(8,128)(2,1)}), bf16[4,144,1152]{2,1,0:T(8,128)(2,1)S(1)}, u32[]{:S(2)}, u32[]{:S(2)}) async-start(bf16[4,144,1152]{2,1,0:T(8,128)(2,1)} %shard_map.104), calls=%async_computation.3 | async-start | bytes 2654208 | tf_op jit(solution)/shard_map/all_to_all | solution.py:23
  44.8 1.7 %constant_dynamic-update-slice_fusion.2 = bf16[1024,512]{1,0:T(8,128)(2,1)} fusion(bf16[1024,512]{1,0:T(8,128)(2,1)} %constant_dynamic-update-slice_fusion.3, bf16[256,512]{1,0:T(8,128)(2,1)} %collective-permute-done.6), kind=kLoop, calls=%fused_computation.72 | loop fusion | bytes 524288
  46.4 0.7 constant_dynamic-update-slice_fusion.1
  47.2 0.7 constant_dynamic-update-slice_fusion.refs_9_
  48.5 2.6 %collective-permute-start.14 = (bf16[1024,512]{1,0:T(8,128)(2,1)}, bf16[1024,512]{1,0:T(8,128)(2,1)}, u32[]{:S(2)}, u32[]{:S(2)}) collective-permute-start(bf16[1024,512]{1,0:T(8,128)(2,1)} %constant_dynamic-update-slice_fusion.refs_9_), channel_id=1, source_target_pairs={{0,24},{8,0},{16,8},{24,16},{1,25},{9,1},{17,9},{25,17},{2,26},{10... | collective-permute-start | bytes 3145736 | tf_op jit(solution)/shard_map/ppermute | solution.py:220
  51.1 2.1 %pad_maximum_fusion.refs_8_ = bf16[1024,512]{1,0:T(8,128)(2,1)} fusion(bf16[256,512]{1,0:T(8,128)(2,1)} %collective-permute-done.5, bf16[256,512]{1,0:T(8,128)(2,1)} %collective-permute-done.4, bf16[256,512]{1,0:T(8,128)(2,1)} %collective-permute-done.3, bf16[256,512]{1,0:T(8,128)(2,1)S(1)} %get-tuple-element.559), kind=kLoop, calls=%fused_computation.47 | loop fusion | flops 4194304 | bytes 2097152 | tf_op jit(solution)/shard_map/concatenate | solution.py:363
  53.3 2.0 %collective-permute-start.11 = (bf16[1024,512]{1,0:T(8,128)(2,1)}, bf16[1024,512]{1,0:T(8,128)(2,1)}, u32[]{:S(2)}, u32[]{:S(2)}) collective-permute-start(bf16[1024,512]{1,0:T(8,128)(2,1)} %pad_maximum_fusion.refs_8_), channel_id=1, source_target_pairs={{0,2},{2,4},{4,6},{6,0},{1,3},{3,5},{5,7},{7,1},{8,10},{10,12},{12... | collective-permute-start | bytes 3145736 | tf_op jit(solution)/shard_map/ppermute | solution.py:220
  55.3 1.3 collective-permute-start.12
  56.9 5.8 %shard_map.105.refs_12_ = f32[1024,512]{1,0:T(8,128)S(1)} custom-call(s32[8]{0:T(128)S(1)} %stack.113.at, bf16[512,8192]{1,0:T(8,128)(2,1)} %refs_3_.5, bf16[512,8192]{1,0:T(8,128)(2,1)} %refs_3_.5, bf16[512,8192]{1,0:T(8,128)(2,1)} %refs_3_.5, bf16[512,8192]{1,0:T(8,128)(2,1)} %refs_3_.5, ...), custom_call_target="tpu_custom_call" | custom-call | flops 2147483648 | bytes 8388608 | tf_op jit(solution)/shard_map/pallas_call | solution.py:274
  62.7 1.4 %copy-done = f32[1024,512]{1,0:T(8,128)} copy-done((f32[1024,512]{1,0:T(8,128)}, f32[1024,512]{1,0:T(8,128)S(1)}, u32[]{:S(2)}) %copy-start) | copy-done | bytes 2097176
  64.2 3.0 %shard_map.106 = bf16[4,144,1152]{2,1,0:T(8,128)(2,1)} custom-call(bf16[4,144,1152]{2,1,0:T(8,128)(2,1)S(1)} %all-to-all-done.3.g, f32[512,1]{1,0:T(8,128)S(1)} %broadcast_in_dim_reshape.8.ow), custom_call_target="tpu_custom_call" | custom-call | flops 603979776 | bytes 5242880 | tf_op jit(solution)/shard_map/pallas_call | solution.py:155
  67.2 4.5 %all-to-all-start.4 = ((bf16[4,144,1152]{2,1,0:T(8,128)(2,1)}), bf16[4,144,1152]{2,1,0:T(8,128)(2,1)S(1)}, u32[]{:S(2)}, u32[]{:S(2)}) async-start(bf16[4,144,1152]{2,1,0:T(8,128)(2,1)} %shard_map.106), calls=%async_computation.4 | async-start | bytes 2654208 | tf_op jit(solution)/shard_map/all_to_all | solution.py:23
  72.0 2.9 %collective-permute-done.13.refs_10_ = bf16[1024,512]{1,0:T(8,128)(2,1)} collective-permute-done((bf16[1024,512]{1,0:T(8,128)(2,1)}, bf16[1024,512]{1,0:T(8,128)(2,1)}, u32[]{:S(2)}, u32[]{:S(2)}) %collective-permute-start.13) | collective-permute-done | bytes 1048608 | tf_op jit(solution)/shard_map/ppermute | solution.py:220
  74.8 1.9 %slice.41 = bf16[512,512]{1,0:T(8,128)(2,1)} slice(bf16[1024,512]{1,0:T(8,128)(2,1)} %collective-permute-done.13.refs_10_), slice={[0:512], [0:512]} | slice | bytes 1048576 | tf_op jit(solution)/shard_map/slice | solution.py:369
  76.7 2.0 %slice.42 = bf16[512,512]{1,0:T(8,128)(2,1)} slice(bf16[1024,512]{1,0:T(8,128)(2,1)} %collective-permute-done.14.refs_11_), slice={[512:1024], [0:512]} | slice | bytes 1048576 | tf_op jit(solution)/shard_map/slice | solution.py:369
  78.8 3.1 %collective-permute-start.19 = (bf16[512,512]{1,0:T(8,128)(2,1)}, bf16[512,512]{1,0:T(8,128)(2,1)}, u32[]{:S(2)}, u32[]{:S(2)}) collective-permute-start(bf16[512,512]{1,0:T(8,128)(2,1)} %slice.42), channel_id=1, source_target_pairs={{0,24},{8,0},{16,8},{24,16},{1,25},{9,1},{17,9},{25,17},{2,26},{10... | collective-permute-start | bytes 1572872 | tf_op jit(solution)/shard_map/ppermute | solution.py:220
  81.9 4.3 %collective-permute-done.11.refs_8_ = bf16[1024,512]{1,0:T(8,128)(2,1)} collective-permute-done((bf16[1024,512]{1,0:T(8,128)(2,1)}, bf16[1024,512]{1,0:T(8,128)(2,1)}, u32[]{:S(2)}, u32[]{:S(2)}) %collective-permute-start.11) | collective-permute-done | bytes 1048608 | tf_op jit(solution)/shard_map/ppermute | solution.py:220
  86.2 1.9 %slice.39 = bf16[512,512]{1,0:T(8,128)(2,1)} slice(bf16[1024,512]{1,0:T(8,128)(2,1)} %collective-permute-done.11.refs_8_), slice={[0:512], [0:512]} | slice | bytes 1048576 | tf_op jit(solution)/shard_map/slice | solution.py:368
  88.1 1.9 %slice.40 = bf16[512,512]{1,0:T(8,128)(2,1)} slice(bf16[1024,512]{1,0:T(8,128)(2,1)} %collective-permute-done.12.refs_9_), slice={[512:1024], [0:512]} | slice | bytes 1048576 | tf_op jit(solution)/shard_map/slice | solution.py:368
  89.9 3.2 %collective-permute-start.17 = (bf16[512,512]{1,0:T(8,128)(2,1)}, bf16[512,512]{1,0:T(8,128)(2,1)}, u32[]{:S(2)}, u32[]{:S(2)}) collective-permute-start(bf16[512,512]{1,0:T(8,128)(2,1)} %slice.40), channel_id=1, source_target_pairs={{0,6},{2,0},{4,2},{6,4},{1,7},{3,1},{5,3},{7,5},{8,14},{10,8},{12,... | collective-permute-start | bytes 1572872 | tf_op jit(solution)/shard_map/ppermute | solution.py:220
  93.2 0.8 copy-done.6
  94.0 1.0 copy-done.7
  95.1 9.9 %shard_map.107.refs_12_ = f32[1024,512]{1,0:T(8,128)S(1)} custom-call(s32[16]{0:T(128)S(1)} %stack.130.at, bf16[512,8192]{1,0:T(8,128)(2,1)} %refs_3_.5, bf16[512,8192]{1,0:T(8,128)(2,1)} %refs_3_.5, bf16[512,8192]{1,0:T(8,128)(2,1)} %refs_3_.5, bf16[512,8192]{1,0:T(8,128)(2,1)} %refs_3_.5, ...), custom_call_target="tpu_custom_call" | custom-call | flops 4294967296 | bytes 16777216 | tf_op jit(solution)/shard_map/pallas_call | solution.py:274
  105.0 5.8 %shard_map.110 = bf16[1024,512]{1,0:T(8,128)(2,1)S(1)} custom-call(s32[8]{0:T(128)S(1)} %stack.139.at, bf16[512,8192]{1,0:T(8,128)(2,1)} %refs_3_.5, bf16[512,8192]{1,0:T(8,128)(2,1)} %refs_3_.5, bf16[512,8192]{1,0:T(8,128)(2,1)} %refs_3_.5, bf16[512,8192]{1,0:T(8,128)(2,1)} %refs_3_.5, ...), custom_call_target="tpu_custom_call" | custom-call | flops 2147483648 | bytes 8388608 | tf_op jit(solution)/shard_map/pallas_call | solution.py:274
  110.8 1.0 copy-done.2
  111.8 0.8 slice.44
  112.6 0.9 shard_map.108
  113.6 3.5 %all-to-all-start.5 = ((bf16[4,304,128]{2,1,0:T(8,128)(2,1)}), bf16[4,304,128]{2,1,0:T(8,128)(2,1)S(1)}, u32[]{:S(2)}, u32[]{:S(2)}) async-start(bf16[4,304,128]{2,1,0:T(8,128)(2,1)} %shard_map.108), calls=%async_computation.5 | async-start | bytes 622592 | tf_op jit(solution)/shard_map/all_to_all | solution.py:23
  117.1 8.1 %all-to-all-done.5.g = bf16[4,304,128]{2,1,0:T(8,128)(2,1)S(1)} async-done(((bf16[4,304,128]{2,1,0:T(8,128)(2,1)}), bf16[4,304,128]{2,1,0:T(8,128)(2,1)S(1)}, u32[]{:S(2)}, u32[]{:S(2)}) %all-to-all-start.5) | async-done | bytes 311328 | tf_op jit(solution)/shard_map/all_to_all | solution.py:23
  125.9 1.1 pad_maximum_fusion.1
  (90 shorter events, 6.2 us)
Async XLA Ops:
  0.6 12.9 %copy-start.9 = (bf16[512,1024]{1,0:T(8,128)(2,1)S(1)}, bf16[512,1024]{1,0:T(8,128)(2,1)}, u32[]{:S(2)}) copy-start(bf16[512,1024]{1,0:T(8,128)(2,1)} %param.14) | copy-start | bytes 3145732
  1.8 19.0 %collective-permute-start.3 = (bf16[256,512]{1,0:T(8,128)(2,1)S(1)}, bf16[256,512]{1,0:T(8,128)(2,1)}, u32[]{:S(2)}, u32[]{:S(2)}) collective-permute-start(bf16[256,512]{1,0:T(8,128)(2,1)S(1)} %get-tuple-element.559), channel_id=1, source_target_pairs={{0,8},{8,16},{16,24},{24,0},{1,9},{9,17},{17,25},{25,1},{2,10},{10... | collective-permute-start | bytes 786440 | tf_op jit(solution)/shard_map/ppermute | solution.py:220
  3.4 29.2 %collective-permute-start.4 = (bf16[256,512]{1,0:T(8,128)(2,1)S(1)}, bf16[256,512]{1,0:T(8,128)(2,1)}, u32[]{:S(2)}, u32[]{:S(2)}) collective-permute-start(bf16[256,512]{1,0:T(8,128)(2,1)S(1)} %get-tuple-element.559), channel_id=1, source_target_pairs={{0,16},{8,24},{16,0},{24,8},{1,17},{9,25},{17,1},{25,9},{2,18},{10... | collective-permute-start | bytes 786440 | tf_op jit(solution)/shard_map/ppermute | solution.py:220
  6.2 2.9 %collective-permute-start.1 = (bf16[256,512]{1,0:T(8,128)(2,1)S(1)}, bf16[256,512]{1,0:T(8,128)(2,1)S(1)}, u32[]{:S(2)}, u32[]{:S(2)}) collective-permute-start(bf16[256,512]{1,0:T(8,128)(2,1)S(1)} %get-tuple-element.560), channel_id=1, source_target_pairs={{0,1},{1,0},{2,3},{3,2},{4,5},{5,4},{6,7},{7,6},{8,9},{9,8},{10,11... | collective-permute-start | bytes 786440 | tf_op jit(solution)/shard_map/ppermute | solution.py:308
  6.2 2.9 %collective-permute-start.2 = (s32[512]{0:T(512)}, s32[512]{0:T(512)S(1)}, u32[]{:S(2)}, u32[]{:S(2)}) collective-permute-start(s32[512]{0:T(512)} %param.15), channel_id=1, source_target_pairs={{0,1},{1,0},{2,3},{3,2},{4,5},{5,4},{6,7},{7,6},{8,9},{9,8},{10,11... | collective-permute-start | bytes 6152 | tf_op jit(solution)/shard_map/ppermute | solution.py:309
  7.5 25.2 %collective-permute-start.5 = (bf16[256,512]{1,0:T(8,128)(2,1)S(1)}, bf16[256,512]{1,0:T(8,128)(2,1)}, u32[]{:S(2)}, u32[]{:S(2)}) collective-permute-start(bf16[256,512]{1,0:T(8,128)(2,1)S(1)} %get-tuple-element.559), channel_id=1, source_target_pairs={{0,24},{8,0},{16,8},{24,16},{1,25},{9,1},{17,9},{25,17},{2,26},{10... | collective-permute-start | bytes 786440 | tf_op jit(solution)/shard_map/ppermute | solution.py:220
  11.5 21.2 %collective-permute-start.6 = (bf16[256,512]{1,0:T(8,128)(2,1)S(1)}, bf16[256,512]{1,0:T(8,128)(2,1)}, u32[]{:S(2)}, u32[]{:S(2)}) collective-permute-start(bf16[256,512]{1,0:T(8,128)(2,1)S(1)} %collective-permute-done.1), channel_id=1, source_target_pairs={{0,2},{2,4},{4,6},{6,0},{1,3},{3,5},{5,7},{7,1},{8,10},{10,12},{12... | collective-permute-start | bytes 786440 | tf_op jit(solution)/shard_map/ppermute | solution.py:220
  13.7 2.5 %copy-start.10 = (bf16[512,1024]{1,0:T(8,128)(2,1)}, bf16[512,1024]{1,0:T(8,128)(2,1)S(1)}, u32[]{:S(2)}) copy-start(bf16[512,1024]{1,0:T(8,128)(2,1)S(1)} %multiply_convert_fusion) | copy-start | bytes 3145732
  13.7 2.5 %copy-start.18 = (bf16[1024,512]{1,0:T(8,128)(2,1)S(1)}, bf16[1024,512]{1,0:T(8,128)(2,1)}, u32[]{:S(2)}) copy-start(bf16[1024,512]{1,0:T(8,128)(2,1)} %param.13) | copy-start | bytes 3145732
  13.8 2.5 %copy-start.20 = (s32[512]{0:T(512)S(1)}, s32[512]{0:T(512)}, u32[]{:S(2)}) copy-start(s32[512]{0:T(512)} %param.15) | copy-start | bytes 6148
  17.1 15.6 %collective-permute-start.7 = (bf16[256,512]{1,0:T(8,128)(2,1)S(1)}, bf16[256,512]{1,0:T(8,128)(2,1)S(1)}, u32[]{:S(2)}, u32[]{:S(2)}) collective-permute-start(bf16[256,512]{1,0:T(8,128)(2,1)S(1)} %collective-permute-done.1), channel_id=1, source_target_pairs={{0,4},{2,6},{4,0},{6,2},{1,5},{3,7},{5,1},{7,3},{8,12},{10,14},{12... | collective-permute-start | bytes 786440 | tf_op jit(solution)/shard_map/ppermute | solution.py:220
  20.8 12.0 %collective-permute-start.8 = (bf16[256,512]{1,0:T(8,128)(2,1)S(1)}, bf16[256,512]{1,0:T(8,128)(2,1)S(1)}, u32[]{:S(2)}, u32[]{:S(2)}) collective-permute-start(bf16[256,512]{1,0:T(8,128)(2,1)S(1)} %collective-permute-done.1), channel_id=1, source_target_pairs={{0,6},{2,0},{4,2},{6,4},{1,7},{3,1},{5,3},{7,5},{8,14},{10,8},{12,... | collective-permute-start | bytes 786440 | tf_op jit(solution)/shard_map/ppermute | solution.py:220
  32.7 39.0 %copy-start.4 = (bf16[512,512]{1,0:T(8,128)(2,1)}, bf16[512,512]{1,0:T(8,128)(2,1)S(1)}, u32[]{:S(2)}) copy-start(bf16[512,512]{1,0:T(8,128)(2,1)S(1)} %get-tuple-element.422.refs_13_) | copy-start | bytes 1572868
  32.7 0.8 copy-start.14
  33.5 0.7 copy-start.16
  34.2 2.8 %collective-permute-start.9 = (bf16[4,128,1152]{2,1,0:T(8,128)(2,1)S(1)}, bf16[4,128,1152]{2,1,0:T(8,128)(2,1)S(1)}, u32[]{:S(2)}, u32[]{:S(2)}) collective-permute-start(bf16[4,128,1152]{2,1,0:T(8,128)(2,1)S(1)} %get-tuple-element.411), channel_id=1, source_target_pairs={{0,1},{1,0},{2,3},{3,2},{4,5},{5,4},{6,7},{7,6},{8,9},{9,8},{10,11... | collective-permute-start | bytes 3538952 | tf_op jit(solution)/shard_map/ppermute | solution.py:362
  37.1 19.8 %collective-permute-start.10 = (bf16[512,8192]{1,0:T(8,128)(2,1)}, bf16[512,8192]{1,0:T(8,128)(2,1)}, u32[]{:S(2)}, u32[]{:S(2)}) collective-permute-start(bf16[512,8192]{1,0:T(8,128)(2,1)} %refs_3_.5), channel_id=1, source_target_pairs={{0,1},{1,0},{2,3},{3,2},{4,5},{5,4},{6,7},{7,6},{8,9},{9,8},{10,11... | collective-permute-start | bytes 25165832 | tf_op jit(solution)/shard_map/ppermute | solution.py:374
  41.1 5.4 %copy-start.15 = (bf16[256,512]{1,0:T(8,128)(2,1)S(1)}, bf16[256,512]{1,0:T(8,128)(2,1)}, u32[]{:S(2)}) copy-start(bf16[256,512]{1,0:T(8,128)(2,1)} %copy-done.14) | copy-start | bytes 786436
  41.1 6.1 %copy-start.17 = (bf16[256,512]{1,0:T(8,128)(2,1)S(1)}, bf16[256,512]{1,0:T(8,128)(2,1)}, u32[]{:S(2)}) copy-start(bf16[256,512]{1,0:T(8,128)(2,1)} %copy-done.16) | copy-start | bytes 786436
  41.1 23.1 %all-to-all-start.3 = ((bf16[4,144,1152]{2,1,0:T(8,128)(2,1)}), bf16[4,144,1152]{2,1,0:T(8,128)(2,1)S(1)}, u32[]{:S(2)}, u32[]{:S(2)}) async-start(bf16[4,144,1152]{2,1,0:T(8,128)(2,1)} %shard_map.104), calls=%async_computation.3 | async-start | bytes 2654208 | tf_op jit(solution)/shard_map/all_to_all | solution.py:23
  44.7 11.8 %copy-start.21 = (s32[8]{0:T(128)S(1)}, s32[8]{0:T(128)}, u32[]{:S(2)}) copy-start(s32[8]{0:T(128)} %param.16) | copy-start | bytes 100
  47.9 27.0 %collective-permute-start.13 = (bf16[1024,512]{1,0:T(8,128)(2,1)}, bf16[1024,512]{1,0:T(8,128)(2,1)}, u32[]{:S(2)}, u32[]{:S(2)}) collective-permute-start(bf16[1024,512]{1,0:T(8,128)(2,1)} %constant_dynamic-update-slice_fusion.refs_9_), channel_id=1, source_target_pairs={{0,8},{8,16},{16,24},{24,0},{1,9},{9,17},{17,25},{25,1},{2,10},{10... | collective-permute-start | bytes 3145736 | tf_op jit(solution)/shard_map/ppermute | solution.py:220
  48.5 28.2 %collective-permute-start.14 = (bf16[1024,512]{1,0:T(8,128)(2,1)}, bf16[1024,512]{1,0:T(8,128)(2,1)}, u32[]{:S(2)}, u32[]{:S(2)}) collective-permute-start(bf16[1024,512]{1,0:T(8,128)(2,1)} %constant_dynamic-update-slice_fusion.refs_9_), channel_id=1, source_target_pairs={{0,24},{8,0},{16,8},{24,16},{1,25},{9,1},{17,9},{25,17},{2,26},{10... | collective-permute-start | bytes 3145736 | tf_op jit(solution)/shard_map/ppermute | solution.py:220
  53.3 32.9 %collective-permute-start.11 = (bf16[1024,512]{1,0:T(8,128)(2,1)}, bf16[1024,512]{1,0:T(8,128)(2,1)}, u32[]{:S(2)}, u32[]{:S(2)}) collective-permute-start(bf16[1024,512]{1,0:T(8,128)(2,1)} %pad_maximum_fusion.refs_8_), channel_id=1, source_target_pairs={{0,2},{2,4},{4,6},{6,0},{1,3},{3,5},{5,7},{7,1},{8,10},{10,12},{12... | collective-permute-start | bytes 3145736 | tf_op jit(solution)/shard_map/ppermute | solution.py:220
  55.3 32.8 %collective-permute-start.12 = (bf16[1024,512]{1,0:T(8,128)(2,1)}, bf16[1024,512]{1,0:T(8,128)(2,1)}, u32[]{:S(2)}, u32[]{:S(2)}) collective-permute-start(bf16[1024,512]{1,0:T(8,128)(2,1)} %pad_maximum_fusion.refs_8_), channel_id=1, source_target_pairs={{0,6},{2,0},{4,2},{6,4},{1,7},{3,1},{5,3},{7,5},{8,14},{10,8},{12,... | collective-permute-start | bytes 3145736 | tf_op jit(solution)/shard_map/ppermute | solution.py:220
  62.7 1.4 %copy-start = (f32[1024,512]{1,0:T(8,128)}, f32[1024,512]{1,0:T(8,128)S(1)}, u32[]{:S(2)}) copy-start(f32[1024,512]{1,0:T(8,128)S(1)} %shard_map.105.refs_12_) | copy-start | bytes 6291460
  67.2 37.8 %all-to-all-start.4 = ((bf16[4,144,1152]{2,1,0:T(8,128)(2,1)}), bf16[4,144,1152]{2,1,0:T(8,128)(2,1)S(1)}, u32[]{:S(2)}, u32[]{:S(2)}) async-start(bf16[4,144,1152]{2,1,0:T(8,128)(2,1)} %shard_map.106), calls=%async_computation.4 | async-start | bytes 2654208 | tf_op jit(solution)/shard_map/all_to_all | solution.py:23
  71.7 21.5 %collective-permute-start.15 = (bf16[512,512]{1,0:T(8,128)(2,1)S(1)}, bf16[512,512]{1,0:T(8,128)(2,1)S(1)}, u32[]{:S(2)}, u32[]{:S(2)}) collective-permute-start(bf16[512,512]{1,0:T(8,128)(2,1)S(1)} %get-tuple-element.422.refs_13_), channel_id=1, source_target_pairs={{0,1},{1,0},{2,3},{3,2},{4,5},{5,4},{6,7},{7,6},{8,9},{9,8},{10,11... | collective-permute-start | bytes 1572872 | tf_op jit(solution)/shard_map/ppermute | solution.py:375
  72.0 21.2 %copy-start.19 = (bf16[1024,512]{1,0:T(8,128)(2,1)S(1)}, bf16[1024,512]{1,0:T(8,128)(2,1)}, u32[]{:S(2)}) copy-start(bf16[1024,512]{1,0:T(8,128)(2,1)} %param.13) | copy-start | bytes 3145732
  76.7 17.3 %copy-start.1 = (f32[1024,512]{1,0:T(8,128)S(1)}, f32[1024,512]{1,0:T(8,128)}, u32[]{:S(2)}) copy-start(f32[1024,512]{1,0:T(8,128)} %copy-done) | copy-start | bytes 6291460
  76.7 17.3 %copy-start.5 = (bf16[512,512]{1,0:T(8,128)(2,1)S(1)}, bf16[512,512]{1,0:T(8,128)(2,1)}, u32[]{:S(2)}) copy-start(bf16[512,512]{1,0:T(8,128)(2,1)} %copy-done.4) | copy-start | bytes 1572868
  76.7 28.3 %collective-permute-start.18 = (bf16[512,512]{1,0:T(8,128)(2,1)}, bf16[512,512]{1,0:T(8,128)(2,1)}, u32[]{:S(2)}, u32[]{:S(2)}) collective-permute-start(bf16[512,512]{1,0:T(8,128)(2,1)} %slice.41), channel_id=1, source_target_pairs={{0,8},{8,16},{16,24},{24,0},{1,9},{9,17},{17,25},{25,1},{2,10},{10... | collective-permute-start | bytes 1572872 | tf_op jit(solution)/shard_map/ppermute | solution.py:220
  78.8 26.2 %collective-permute-start.19 = (bf16[512,512]{1,0:T(8,128)(2,1)}, bf16[512,512]{1,0:T(8,128)(2,1)}, u32[]{:S(2)}, u32[]{:S(2)}) collective-permute-start(bf16[512,512]{1,0:T(8,128)(2,1)} %slice.42), channel_id=1, source_target_pairs={{0,24},{8,0},{16,8},{24,16},{1,25},{9,1},{17,9},{25,17},{2,26},{10... | collective-permute-start | bytes 1572872 | tf_op jit(solution)/shard_map/ppermute | solution.py:220
  88.1 16.9 %collective-permute-start.16 = (bf16[512,512]{1,0:T(8,128)(2,1)}, bf16[512,512]{1,0:T(8,128)(2,1)}, u32[]{:S(2)}, u32[]{:S(2)}) collective-permute-start(bf16[512,512]{1,0:T(8,128)(2,1)} %slice.39), channel_id=1, source_target_pairs={{0,2},{2,4},{4,6},{6,0},{1,3},{3,5},{5,7},{7,1},{8,10},{10,12},{12... | collective-permute-start | bytes 1572872 | tf_op jit(solution)/shard_map/ppermute | solution.py:220
  89.9 15.1 %collective-permute-start.17 = (bf16[512,512]{1,0:T(8,128)(2,1)}, bf16[512,512]{1,0:T(8,128)(2,1)}, u32[]{:S(2)}, u32[]{:S(2)}) collective-permute-start(bf16[512,512]{1,0:T(8,128)(2,1)} %slice.40), channel_id=1, source_target_pairs={{0,6},{2,0},{4,2},{6,4},{1,7},{3,1},{5,3},{7,5},{8,14},{10,8},{12,... | collective-permute-start | bytes 1572872 | tf_op jit(solution)/shard_map/ppermute | solution.py:220
  93.2 0.8 copy-start.6
  94.0 1.0 copy-start.7
  110.8 1.0 copy-start.2
  112.6 13.1 %copy-start.3 = (bf16[1024,512]{1,0:T(8,128)(2,1)S(1)}, bf16[1024,512]{1,0:T(8,128)(2,1)}, u32[]{:S(2)}) copy-start(bf16[1024,512]{1,0:T(8,128)(2,1)} %copy-done.2) | copy-start | bytes 3145732
  112.6 13.1 %collective-permute-start.20 = (bf16[512,512]{1,0:T(8,128)(2,1)}, bf16[512,512]{1,0:T(8,128)(2,1)S(1)}, u32[]{:S(2)}, u32[]{:S(2)}) collective-permute-start(bf16[512,512]{1,0:T(8,128)(2,1)} %slice.44), channel_id=1, source_target_pairs={{0,1},{1,0},{2,3},{3,2},{4,5},{5,4},{6,7},{7,6},{8,9},{9,8},{10,11... | collective-permute-start | bytes 1572872 | tf_op jit(solution)/shard_map/ppermute | solution.py:390
  113.6 11.6 %all-to-all-start.5 = ((bf16[4,304,128]{2,1,0:T(8,128)(2,1)}), bf16[4,304,128]{2,1,0:T(8,128)(2,1)S(1)}, u32[]{:S(2)}, u32[]{:S(2)}) async-start(bf16[4,304,128]{2,1,0:T(8,128)(2,1)} %shard_map.108), calls=%async_computation.5 | async-start | bytes 622592 | tf_op jit(solution)/shard_map/all_to_all | solution.py:23
  125.8 1.4 %copy-start.11 = (bf16[512,1024]{1,0:T(8,128)(2,1)S(1)}, bf16[512,1024]{1,0:T(8,128)(2,1)}, u32[]{:S(2)}) copy-start(bf16[512,1024]{1,0:T(8,128)(2,1)} %copy-done.10) | copy-start | bytes 3145732
  127.8 0.7 copy-start.8
  127.9 0.6 copy-start.13

commit v5 on v4

--- a/solution.py
+++ b/solution.py
@@ -40,11 +40,11 @@
     return pl.BlockSpec(shape, lambda *i: (0,) * len(shape))
 
 
-def terms(tokens, down, low_t, scaled, tasks_col, pick_t, me_c, nx, nz):
+def terms(tokens, down, up, cotangent, tasks, token_weight, pick_t, col_task, v_from, me_c, nx, nz):
     n_tok, width = tokens.shape
     cols = down.shape[1]
-    sc = low_t.shape[0]
-    kv = scaled.shape[1]
+    sc = pick_t.shape[0]
+    kv = cotangent.shape[1]
     per = 4
     steps = nx * nz // per
     blk = width // steps
@@ -53,9 +53,17 @@
     u = half // nz
     lanes = nx * d + u
 
-    def body(me, tok, dn, low, sca, task, pick, hidden, theirs, mine, acc):
+    def body(me, tok, dn, up_ref, cot, task_col, task_row, tw, pick, picked, v_ref, hidden, theirs, mine, acc, sca, low):
         i = pl.program_id(0)
         first = me[0] == 0
+
+        @pl.when(i == 0)
+        def _():
+            sca[...] = (cot[...].astype(F32) * tw[...]).astype(BF)
+            up_slot = dot(pick[...], up_ref[...], ((1,), (1,))).astype(BF)
+            g = dot(up_slot, sca[...], ((1,), (1,)))
+            low[...] = jnp.where(picked[...] == task_row[...], g, 0.0).astype(BF)
+
         t = tok[...]
         part = dot(t, dn[...])
 
@@ -67,25 +75,26 @@
         def _():
             acc[...] += part
 
-        r = dot(low[...], t)
+        r = dot(low[...], t).astype(BF)
         for k in range(per):
             x, z = (i * per + k) // nz, (i * per + k) % nz
             at = pl.ds(pl.multiple_of(x * d, d), d)
             a, b = r[:, 2 * k * d : (2 * k + 1) * d], r[:, (2 * k + 1) * d : (2 * k + 2) * d]
-            mine[z, :, at] = jnp.where(first, a, b).astype(BF)
-            theirs[z, :, at] = jnp.where(first, b, a).astype(BF)
+            mine[z, :, at] = jnp.where(first, a, b)
+            theirs[z, :, at] = jnp.where(first, b, a)
 
         @pl.when(i == steps - 1)
         def _():
             adapter = lax.broadcasted_iota(jnp.int32, (n_tok, cols), 1) // RANK
-            h = jnp.where(task[...] == adapter, acc[...], 0.0).astype(BF)
+            h = jnp.where(task_col[...] == adapter, acc[...], 0.0).astype(BF)
             hidden[...] = h
             h_t = dot(pick[...], h, ((1,), (1,))).astype(BF)
-            g = dot(h_t, sca[...])
+            order = lax.broadcasted_iota(jnp.int32, (kv, kv), 0) == v_ref[...]
+            g = dot(dot(h_t, sca[...]).astype(BF), jnp.where(order, 1.0, 0.0).astype(BF)).astype(BF)
             for k in range(nz):
                 a, b = g[:, k * u : (k + 1) * u], g[:, half + k * u : half + (k + 1) * u]
-                mine[k, :, nx * d :] = jnp.where(first, a, b).astype(BF)
-                theirs[k, :, nx * d :] = jnp.where(first, b, a).astype(BF)
+                mine[k, :, nx * d :] = jnp.where(first, a, b)
+                theirs[k, :, nx * d :] = jnp.where(first, b, a)
 
     return call(
         body,
@@ -99,17 +108,71 @@
             pl.BlockSpec(memory_space=pltpu.SMEM),
             pl.BlockSpec((n_tok, blk), lambda i: (0, i)),
             pl.BlockSpec((blk, cols), lambda i: (i, 0)),
-            whole((sc, n_tok)),
+            whole((kv, cols)),
             whole((n_tok, kv)),
             whole((n_tok, 1)),
+            whole((1, n_tok)),
+            whole((n_tok, 1)),
             whole((sc, cols)),
+            whole((sc, 1)),
+            whole((1, kv)),
         ],
         (whole((n_tok, cols)), whole((nz, sc, lanes)), whole((nz, sc, lanes))),
-        [pltpu.VMEM((n_tok, cols), F32)],
+        [pltpu.VMEM((n_tok, cols), F32), pltpu.VMEM((n_tok, kv), BF), pltpu.VMEM((sc, n_tok), BF)],
         flops=2 * n_tok * width * (cols + sc),
-        data=28 * MIB,
+        data=24 * MIB,
         vmem=48,
-    )(me_c, tokens, down, low_t, scaled, tasks_col, pick_t)
+    )(
+        me_c,
+        tokens,
+        down,
+        up,
+        cotangent,
+        tasks[:, None],
+        tasks[None, :],
+        token_weight,
+        pick_t,
+        col_task[:, None],
+        v_from[None, :],
+    )
+
+
+def join(*lists):
+    n = len(lists[0])
+    rows, lanes = lists[0][0].shape
+
+    def body(*refs):
+        for k in range(len(lists)):
+            for j in range(n):
+                refs[n * len(lists) + k][j * rows : (j + 1) * rows] = refs[k * n + j][...]
+
+    return call(
+        body,
+        tuple(jax.ShapeDtypeStruct((n * rows, lanes), BF) for _ in lists),
+        (1,),
+        [whole((rows, lanes))] * (n * len(lists)),
+        tuple(whole((n * rows, lanes)) for _ in lists),
+        data=4 * MIB,
+    )(*[a for one in lists for a in one])
+
+
+def halves(arrays, which):
+    rows, lanes = arrays[0].shape
+    steps = 2
+    blk = rows // 2 // steps
+
+    def body(*refs):
+        for k in range(len(arrays)):
+            refs[len(arrays) + k][...] = refs[k][...]
+
+    return call(
+        body,
+        tuple(jax.ShapeDtypeStruct((rows // 2, lanes), BF) for _ in arrays),
+        (steps,),
+        [pl.BlockSpec((blk, lanes), lambda i, w=w: (w * steps + i, 0)) for w in which],
+        tuple(pl.BlockSpec((blk, lanes), lambda i: (i, 0)) for _ in arrays),
+        data=4 * MIB,
+    )(*arrays)
 
 
 def pack(mine, theirs, note):
@@ -236,7 +299,7 @@
         tok_a, tok_b = refs[:per], refs[per : 2 * per]
         ws = refs[2 * per : 2 * per + len(flat)]
         more = refs[2 * per + len(flat) : 2 * per + len(flat) + len(extra)]
-        out = refs[2 * per + len(flat) + len(extra)]
+        outs = refs[2 * per + len(flat) + len(extra) :]
         acc = refs[-1]
         i = pl.program_id(0)
 
@@ -267,18 +330,19 @@
 
             @pl.when(i == steps - 1)
             def _():
-                out[...] = acc[...].astype(BF)
+                outs[0][...] = acc[:n_tok].astype(BF)
+                outs[1][...] = acc[n_tok:].astype(BF)
 
     tok_specs = [pl.BlockSpec((n_tok, blk), lambda i, s, k=k: (0, s[i * per + k])) for k in range(per)]
     shape = (2 * n_tok, n)
     return pl.pallas_call(
         body,
-        out_shape=jax.ShapeDtypeStruct(shape, BF if final else F32),
+        out_shape=(jax.ShapeDtypeStruct((n_tok, n), BF),) * 2 if final else jax.ShapeDtypeStruct(shape, F32),
         grid_spec=pltpu.PrefetchScalarGridSpec(
             num_scalar_prefetch=1,
             grid=(steps,),
             in_specs=tok_specs * 2 + [whole(w.shape) for w in flat] + [whole(e.shape) for e in extra],
-            out_specs=whole(shape),
+            out_specs=(whole((n_tok, n)),) * 2 if final else whole(shape),
             scratch_shapes=[pltpu.VMEM(shape, F32)] if final else [],
         ),
         compiler_params=pltpu.CompilerParams(vmem_limit_bytes=40 * MIB),
@@ -329,15 +393,14 @@
     row = jnp.arange(cols, dtype=jnp.int32)
 
     token_count = jnp.sum(jnp.where(hit, counts.astype(F32)[None, :], 0.0), axis=1)
-    scaled = (cotangent.astype(F32) * (SCALE / token_count)[:, None]).astype(BF)
-    v_in = jnp.arange(kv, dtype=jnp.int32)
+    token_weight = (SCALE / token_count)[:, None]
+    v_out = jnp.arange(kv, dtype=jnp.int32)
     v_from = (
-        (v_in // v_rows % nx) * (nz * 2 * v_rows)
-        + (v_in // (v_rows * nx) % nz) * (2 * v_rows)
-        + v_in // (v_rows * nx * nz) * v_rows
-        + v_in % v_rows
+        (v_out // v_rows % nx) * (nz * 2 * v_rows)
+        + (v_out // (v_rows * nx) % nz) * (2 * v_rows)
+        + v_out // (v_rows * nx * nz) * v_rows
+        + v_out % v_rows
     )
-    scaled_by_core = dot(scaled, (v_in[:, None] == v_from[None, :]).astype(BF)).astype(BF)
 
     owned_col = jnp.repeat(owned.astype(F32), RANK)[:, None]
 
@@ -347,11 +410,19 @@
         more = (jnp.sum(present.astype(jnp.int32)) > first + SLOTS).astype(F32)
         pick_t = ((row // RANK)[None, :] == col_task[:, None]) & ((row % RANK)[None, :] == col_rank[:, None])
         pick_t = pick_t.astype(BF)
-        mask_slot_t = (tasks[None, :] == col_task[:, None]).astype(F32)
-        up_slot_t = dot(pick_t, up, ((1,), (1,))).astype(BF)
-        low_t = (dot(up_slot_t, scaled, ((1,), (1,))) * mask_slot_t).astype(BF)
         hidden, theirs, mine = terms(
-            tokens, down, low_t, scaled_by_core, tasks[:, None], pick_t, me_c.astype(jnp.int32)[None], nx, nz
+            tokens,
+            down,
+            up,
+            cotangent,
+            tasks,
+            token_weight,
+            pick_t,
+            col_task,
+            v_from,
+            me_c.astype(jnp.int32)[None],
+            nx,
+            nz,
         )
         note_row = lax.broadcasted_iota(jnp.int32, (INFO, lanes), 0)
         note = jnp.where(note_row == 0, jnp.pad(col_task.astype(F32), (0, lanes - sc))[None, :], more)
@@ -360,13 +431,12 @@
     hidden, theirs, mine, note = local_terms(jnp.int32(0))
     first_hop, theirs = lax.optimization_barrier((first_hop, theirs))
     got = lax.ppermute(theirs, "c", SWAP)
-    near_a = jnp.concatenate([block_a] + first_hop[: nx - 1])
-    near_b = jnp.concatenate([block_b] + first_hop[nx - 1 :])
-    cut_a, cut_b = near_a.shape[0] // 2, near_b.shape[0] // 2
+    near_a, near_b = join([block_a] + first_hop[: nx - 1], [block_b] + first_hop[nx - 1 :])
     a_down, a_up = shifted(near_a, "z", 1), shifted(near_a, "z", nz - 1)
     b_down, b_up = shifted(near_b, "x", 1), shifted(near_b, "x", nx - 1)
-    a_far = [shifted(a_down[:cut_a], "z", 1), shifted(a_up[cut_a:], "z", nz - 1)]
-    b_far = [shifted(b_down[:cut_b], "x", 1), shifted(b_up[cut_b:], "x", nx - 1)]
+    pass_on = halves([a_down, a_up, b_down, b_up], [0, 1, 0, 1])
+    a_far = [shifted(pass_on[0], "z", 1), shifted(pass_on[1], "z", nz - 1)]
+    b_far = [shifted(pass_on[2], "x", 1), shifted(pass_on[3], "x", nx - 1)]
 
     from_z = exchange(pack(mine, got, note), "z")
 
@@ -376,6 +446,9 @@
     acc = add_blocks(tokens, other, [[near_a], [near_b]], at(blocks_a(0), blocks_b(0)))
     from_z, acc = lax.optimization_barrier((from_z, acc))
     from_y = exchange(spread(from_z, owned_col, ny), "y")
+    by_x = turn(from_y, nx, d_rows)
+    by_x, acc = lax.optimization_barrier((by_x, acc))
+    grad_down, grad_up, flags = finish(exchange(by_x, "x"), d_rows)
     acc = add_blocks(
         tokens,
         other,
@@ -384,13 +457,10 @@
         before=acc,
         lora=(hidden, other_hidden, lax.dynamic_slice_in_dim(up, me_c * half, half, 0)),
     )
-    from_y, acc = lax.optimization_barrier((from_y, acc))
-    grad_down, grad_up, flags = finish(exchange(turn(from_y, nx, d_rows), "x"), d_rows)
-    tile = add_blocks(tokens, other, [a_far, b_far], at(blocks_a(2), blocks_b(2)), before=acc, final=True)
-    back = lax.ppermute(tile[n_tok:], "c", SWAP)
-    low_half = jnp.where(me_c == 0, tile[:n_tok], back)
-    high_half = jnp.where(me_c == 0, back, tile[:n_tok])
-    keys = jnp.concatenate([low_half, high_half], axis=1)
+    acc, flags = lax.optimization_barrier((acc, flags))
+    tile, sent = add_blocks(tokens, other, [a_far, b_far], at(blocks_a(2), blocks_b(2)), before=acc, final=True)
+    back = lax.ppermute(sent, "c", SWAP)
+    keys = jnp.concatenate([jnp.where(me_c == 0, tile, back), jnp.where(me_c == 0, back, tile)], axis=1)
 
     flag, keys = lax.optimization_barrier((flags[0, 0], keys))
 

time: 130 us -> 127 us (0.977)
  other arithmetic: 6.84 us -> 2.49 us
  Pallas kernels: 38.1 us -> 42.2 us
  matrix products: 3.18 us -> 0 us
    slice x5 -> x0, local copies, waits for them, and re-layouts: 8.49 us -> none  [the longest x1 2.04 us: per_device(): b_up[cut_b:]]
    unnamed x45 -> x66, local copies, waits for them, and re-layouts: 9.72 us -> 17.7 us
    all_to_all x3, waiting for transfers between devices: 8.21 us -> 0.64 us  [exchange(): return lax.all_to_all(a, axis, 0, 0, tiled=True)]
    ppermute x14, waiting for transfers between devices: 7.21 us -> 12.9 us  [shifted(): return lax.ppermute(a, axis, [(i, (i + step) % n) for i in range(n)])]
    pallas_call x3 -> x5, Pallas kernels: 21.5 us -> 25.6 us  [the longest x3 21.6 us: add_blocks(): pl.pallas_call(body, out_shape=(jax.ShapeDtypeStruct((n_tok, n), BF),) *...]
    dot_general x2 -> x0, matrix products: 3.18 us -> none  [dot(): return lax.dot_general(a, b, (dims, ((), ())), preferred_element_type=F32)]
    concatenate x2 -> x1, other arithmetic: 3.24 us -> 1.13 us  [per_device(): jnp.concatenate([jnp.where(me_c == 0, tile, back), jnp.where(me_c == 0, b...]
    pallas_call x1, Pallas kernels: 10.9 us -> 12.5 us  [terms(): call(body, (jax.ShapeDtypeStruct((n_tok, cols), BF), jax.ShapeDtypeStruct...]
  transfers between devices with their start and end apart: 23 -> 23, of which waited for: 5 -> 4; matrix products, arithmetic and copies ran while one was open for 17% -> 4% of each run, Pallas kernels for 25% -> 29%
where the time goes in v5:
time: 127 us; the launch traced here: 125 us
  Pallas kernels  42.2 us (33%)
  starting transfers between devices  37.8 us (30%)
  local copies, waits for them, and re-layouts  22.5 us (18%)
  waiting for transfers between devices  17.8 us (14%)
  other arithmetic  2.49 us (2%)
  between operations  1.89 us (1%)
    ppermute x14, starting transfers between devices, shifted(): return lax.ppermute(a, axis, [(i, (i + step) % n) for i in range(n)])  25.5 us
    pallas_call x3, Pallas kernels, add_blocks(): pl.pallas_call(body, out_shape=(jax.ShapeDtypeStruct((n_tok, n), BF),) *...  21.6 us
    unnamed x66, local copies, waits for them, and re-layouts  17.7 us
    ppermute x14, waiting for transfers between devices, shifted(): return lax.ppermute(a, axis, [(i, (i + step) % n) for i in range(n)])  12.9 us
    pallas_call x1, Pallas kernels, terms(): call(body, (jax.ShapeDtypeStruct((n_tok, cols), BF), jax.ShapeDtypeStruct...  12.5 us
    all_to_all x3, starting transfers between devices, exchange(): return lax.all_to_all(a, axis, 0, 0, tiled=True)  11.6 us
    ppermute x1, waiting for transfers between devices, per_device(): got = lax.ppermute(theirs, 'c', SWAP)  2.84 us
    pallas_call x1, Pallas kernels, halves(): call(body, tuple((jax.ShapeDtypeStruct((rows // 2, lanes), BF) for _ in a...  2.58 us
  transfers between devices with their start and end apart: 23, of which 4 were waited for; matrix products, arithmetic and copies ran while one was open for 4% of the time, Pallas kernels for 29%

profile of v5, /device:TPU:0, one launch (start us, length us, event | category | flops | bytes accessed | tf_op | source)
XLA Modules:
  0.0 125.3 jit_solution(16710606058920082953)
XLA Ops:
  0.7 1.1 constant_dynamic-slice_fusion.1
  1.7 1.6 %collective-permute-start.3 = (bf16[256,512]{1,0:T(8,128)(2,1)S(1)}, bf16[256,512]{1,0:T(8,128)(2,1)S(1)}, u32[]{:S(2)}, u32[]{:S(2)}) collective-permute-start(bf16[256,512]{1,0:T(8,128)(2,1)S(1)} %get-tuple-element.627.refs_0_), channel_id=1, source_target_pairs={{0,8},{8,16},{16,24},{24,0},{1,9},{9,17},{17,25},{25,1},{2,10},{10... | collective-permute-start | bytes 786440 | tf_op jit(solution)/shard_map/ppermute | solution.py:283
  3.4 2.7 %collective-permute-start.4 = (bf16[256,512]{1,0:T(8,128)(2,1)S(1)}, bf16[256,512]{1,0:T(8,128)(2,1)S(1)}, u32[]{:S(2)}, u32[]{:S(2)}) collective-permute-start(bf16[256,512]{1,0:T(8,128)(2,1)S(1)} %get-tuple-element.627.refs_0_), channel_id=1, source_target_pairs={{0,16},{8,24},{16,0},{24,8},{1,17},{9,25},{17,1},{25,9},{2,18},{10... | collective-permute-start | bytes 786440 | tf_op jit(solution)/shard_map/ppermute | solution.py:283
  6.7 0.8 copy.24.task_col
  7.5 1.5 %collective-permute-start.5 = (bf16[256,512]{1,0:T(8,128)(2,1)S(1)}, bf16[256,512]{1,0:T(8,128)(2,1)S(1)}, u32[]{:S(2)}, u32[]{:S(2)}) collective-permute-start(bf16[256,512]{1,0:T(8,128)(2,1)S(1)} %get-tuple-element.627.refs_0_), channel_id=1, source_target_pairs={{0,24},{8,0},{16,8},{24,16},{1,25},{9,1},{17,9},{25,17},{2,26},{10... | collective-permute-start | bytes 786440 | tf_op jit(solution)/shard_map/ppermute | solution.py:283
  9.8 2.0 %collective-permute-start.6 = (bf16[256,512]{1,0:T(8,128)(2,1)S(1)}, bf16[256,512]{1,0:T(8,128)(2,1)S(1)}, u32[]{:S(2)}, u32[]{:S(2)}) collective-permute-start(bf16[256,512]{1,0:T(8,128)(2,1)S(1)} %collective-permute-done.1.refs_4_), channel_id=1, source_target_pairs={{0,2},{2,4},{4,6},{6,0},{1,3},{3,5},{5,7},{7,1},{8,10},{10,12},{12... | collective-permute-start | bytes 786440 | tf_op jit(solution)/shard_map/ppermute | solution.py:283
  11.9 3.7 %collective-permute-start.7 = (bf16[256,512]{1,0:T(8,128)(2,1)S(1)}, bf16[256,512]{1,0:T(8,128)(2,1)S(1)}, u32[]{:S(2)}, u32[]{:S(2)}) collective-permute-start(bf16[256,512]{1,0:T(8,128)(2,1)S(1)} %collective-permute-done.1.refs_4_), channel_id=1, source_target_pairs={{0,4},{2,6},{4,0},{6,2},{1,5},{3,7},{5,1},{7,3},{8,12},{10,14},{12... | collective-permute-start | bytes 786440 | tf_op jit(solution)/shard_map/ppermute | solution.py:283
  15.5 0.7 copy-done.10
  16.2 1.0 collective-permute-start.8
  17.2 12.5 %shard_map.103 = (bf16[512,512]{1,0:T(8,128)(2,1)S(1)}, bf16[4,128,1152]{2,1,0:T(8,128)(2,1)S(1)}, bf16[4,128,1152]{2,1,0:T(8,128)(2,1)S(1)}) custom-call(s32[1]{0:T(128)} %bitcast.16.me, bf16[512,8192]{1,0:T(8,128)(2,1)} %refs_3_.5, bf16[8192,512]{1,0:T(8,128)(2,1)} %dn.1, bf16[1024,512]{1,0:T(8,128)(2,1)} %up_ref.1, bf16[512,1024]{1,0:T(8,128)(2,1)} %cot, ...), custom_call_target="tpu_custom_call" | custom-call | flops 5368709120 | bytes 25165824 | tf_op jit(solution)/shard_map/pallas_call | solution.py:99
  29.8 0.8 copy-done.8
  30.6 0.7 copy-done.12
  31.3 0.7 copy-done.16
  32.0 0.7 copy-done.18
  32.7 0.7 copy-done.20
  33.4 0.7 copy-done.22
  34.1 2.8 %collective-permute-done.9.b = bf16[4,128,1152]{2,1,0:T(8,128)(2,1)S(1)} collective-permute-done((bf16[4,128,1152]{2,1,0:T(8,128)(2,1)S(1)}, bf16[4,128,1152]{2,1,0:T(8,128)(2,1)S(1)}, u32[]{:S(2)}, u32[]{:S(2)}) %collective-permute-start.9) | collective-permute-done | bytes 1179680 | tf_op jit(solution)/shard_map/ppermute | solution.py:433
  38.4 1.7 %shard_map.105 = bf16[4,144,1152]{2,1,0:T(8,128)(2,1)} custom-call(bf16[4,128,1152]{2,1,0:T(8,128)(2,1)S(1)} %get-tuple-element.447.a, bf16[4,128,1152]{2,1,0:T(8,128)(2,1)S(1)} %collective-permute-done.9.b, bf16[16,1152]{1,0:T(8,128)(2,1)S(1)} %select_convert_fusion.1.c), custom_call_target="tpu_custom_call" | custom-call | bytes 10485760 | tf_op jit(solution)/shard_map/pallas_call | solution.py:186
  40.2 3.7 %all-to-all-start.3 = ((bf16[4,144,1152]{2,1,0:T(8,128)(2,1)}), bf16[4,144,1152]{2,1,0:T(8,128)(2,1)S(1)}, u32[]{:S(2)}, u32[]{:S(2)}) async-start(bf16[4,144,1152]{2,1,0:T(8,128)(2,1)} %shard_map.105), calls=%async_computation.3 | async-start | bytes 2654208 | tf_op jit(solution)/shard_map/all_to_all | solution.py:23
  44.1 0.9 broadcast_in_dim_reshape.8.ow
  45.2 0.9 copy-done.15
  46.1 0.9 copy-done.19
  47.1 0.9 copy-done.21
  48.0 0.9 copy-done.23
  49.0 1.4 %shard_map.104 = (bf16[1024,512]{1,0:T(8,128)(2,1)}, bf16[1024,512]{1,0:T(8,128)(2,1)}) custom-call(bf16[256,512]{1,0:T(8,128)(2,1)S(1)} %copy-done.7, bf16[256,512]{1,0:T(8,128)(2,1)S(1)} %copy-done.11, bf16[256,512]{1,0:T(8,128)(2,1)S(1)} %copy-done.13, bf16[256,512]{1,0:T(8,128)(2,1)S(1)} %copy-done.17, bf16[256,512]{1,0:T(8,128)(2,1)S(1)} %copy-done.15, ...), custom_call_target="tpu_custom_call" | custom-call | bytes 4194304 | tf_op jit(solution)/shard_map/pallas_call | solution.py:149
  50.4 1.8 %collective-permute-start.11 = (bf16[1024,512]{1,0:T(8,128)(2,1)}, bf16[1024,512]{1,0:T(8,128)(2,1)}, u32[]{:S(2)}, u32[]{:S(2)}) collective-permute-start(bf16[1024,512]{1,0:T(8,128)(2,1)} %get-tuple-element.445.refs_8_), channel_id=1, source_target_pairs={{0,2},{2,4},{4,6},{6,0},{1,3},{3,5},{5,7},{7,1},{8,10},{10,12},{12... | collective-permute-start | bytes 3145736 | tf_op jit(solution)/shard_map/ppermute | solution.py:283
  52.3 1.4 %collective-permute-start.12 = (bf16[1024,512]{1,0:T(8,128)(2,1)}, bf16[1024,512]{1,0:T(8,128)(2,1)}, u32[]{:S(2)}, u32[]{:S(2)}) collective-permute-start(bf16[1024,512]{1,0:T(8,128)(2,1)} %get-tuple-element.445.refs_8_), channel_id=1, source_target_pairs={{0,6},{2,0},{4,2},{6,4},{1,7},{3,1},{5,3},{7,5},{8,14},{10,8},{12,... | collective-permute-start | bytes 3145736 | tf_op jit(solution)/shard_map/ppermute | solution.py:283
  54.3 2.6 %collective-permute-start.14 = (bf16[1024,512]{1,0:T(8,128)(2,1)}, bf16[1024,512]{1,0:T(8,128)(2,1)}, u32[]{:S(2)}, u32[]{:S(2)}) collective-permute-start(bf16[1024,512]{1,0:T(8,128)(2,1)} %get-tuple-element.446.refs_9_), channel_id=1, source_target_pairs={{0,24},{8,0},{16,8},{24,16},{1,25},{9,1},{17,9},{25,17},{2,26},{10... | collective-permute-start | bytes 3145736 | tf_op jit(solution)/shard_map/ppermute | solution.py:283
  56.9 5.8 %shard_map.106.refs_12_ = f32[1024,512]{1,0:T(8,128)S(1)} custom-call(s32[8]{0:T(128)S(1)} %stack.130.at, bf16[512,8192]{1,0:T(8,128)(2,1)} %refs_3_.5, bf16[512,8192]{1,0:T(8,128)(2,1)} %refs_3_.5, bf16[512,8192]{1,0:T(8,128)(2,1)} %refs_3_.5, bf16[512,8192]{1,0:T(8,128)(2,1)} %refs_3_.5, ...), custom_call_target="tpu_custom_call" | custom-call | flops 2147483648 | bytes 8388608 | tf_op jit(solution)/shard_map/pallas_call | solution.py:338
  63.4 0.9 copy-done.5
  64.3 2.1 %shard_map.107 = bf16[4,144,1152]{2,1,0:T(8,128)(2,1)S(1)} custom-call(bf16[4,144,1152]{2,1,0:T(8,128)(2,1)S(1)} %all-to-all-done.3.g, f32[512,1]{1,0:T(8,128)S(1)} %copy-done.5), custom_call_target="tpu_custom_call" | custom-call | flops 603979776 | bytes 5242880 | tf_op jit(solution)/shard_map/pallas_call | solution.py:218
  66.4 1.1 copy-done.2
  67.5 4.5 %all-to-all-start.4 = ((bf16[4,144,1152]{2,1,0:T(8,128)(2,1)}), bf16[4,144,1152]{2,1,0:T(8,128)(2,1)S(1)}, u32[]{:S(2)}, u32[]{:S(2)}) async-start(bf16[4,144,1152]{2,1,0:T(8,128)(2,1)} %copy-done.2), calls=%async_computation.4 | async-start | bytes 2654208 | tf_op jit(solution)/shard_map/all_to_all | solution.py:23
  72.1 12.9 %collective-permute-done.11.refs_8_.refs_0_ = bf16[1024,512]{1,0:T(8,128)(2,1)} collective-permute-done((bf16[1024,512]{1,0:T(8,128)(2,1)}, bf16[1024,512]{1,0:T(8,128)(2,1)}, u32[]{:S(2)}, u32[]{:S(2)}) %collective-permute-start.11) | collective-permute-done | bytes 1048608 | tf_op jit(solution)/shard_map/ppermute | solution.py:283
  85.1 2.6 %shard_map.111 = (bf16[512,512]{1,0:T(8,128)(2,1)}, bf16[512,512]{1,0:T(8,128)(2,1)}, bf16[512,512]{1,0:T(8,128)(2,1)}, bf16[512,512]{1,0:T(8,128)(2,1)}) custom-call(bf16[1024,512]{1,0:T(8,128)(2,1)} %collective-permute-done.11.refs_8_.refs_0_, bf16[1024,512]{1,0:T(8,128)(2,1)} %collective-permute-done.12.refs_9_.refs_1_, ...), custom_call_target="tpu_custom_call" | custom-call | bytes 4194304 | tf_op jit(solution)/shard_map/pallas_call | solution.py:168
  88.3 2.6 %collective-permute-start.17 = (bf16[512,512]{1,0:T(8,128)(2,1)}, bf16[512,512]{1,0:T(8,128)(2,1)}, u32[]{:S(2)}, u32[]{:S(2)}) collective-permute-start(bf16[512,512]{1,0:T(8,128)(2,1)} %get-tuple-element.456), channel_id=1, source_target_pairs={{0,6},{2,0},{4,2},{6,4},{1,7},{3,1},{5,3},{7,5},{8,14},{10,8},{12,... | collective-permute-start | bytes 1572872 | tf_op jit(solution)/shard_map/ppermute | solution.py:283
  91.5 2.6 %collective-permute-start.19 = (bf16[512,512]{1,0:T(8,128)(2,1)}, bf16[512,512]{1,0:T(8,128)(2,1)}, u32[]{:S(2)}, u32[]{:S(2)}) collective-permute-start(bf16[512,512]{1,0:T(8,128)(2,1)} %get-tuple-element.458), channel_id=1, source_target_pairs={{0,24},{8,0},{16,8},{24,16},{1,25},{9,1},{17,9},{25,17},{2,26},{10... | collective-permute-start | bytes 1572872 | tf_op jit(solution)/shard_map/ppermute | solution.py:283
  94.1 0.8 constant_dynamic-slice_fusion.refs_15_
  95.2 0.7 copy-done.4
  95.9 3.5 %all-to-all-start.5 = ((bf16[4,304,128]{2,1,0:T(8,128)(2,1)}), bf16[4,304,128]{2,1,0:T(8,128)(2,1)S(1)}, u32[]{:S(2)}, u32[]{:S(2)}) async-start(bf16[4,304,128]{2,1,0:T(8,128)(2,1)} %copy-done.4), calls=%async_computation.5 | async-start | bytes 622592 | tf_op jit(solution)/shard_map/all_to_all | solution.py:23
  99.4 1.0 copy-done.3
  100.4 1.0 copy-done.9
  101.5 10.0 %shard_map.109.refs_12_ = f32[1024,512]{1,0:T(8,128)S(1)} custom-call(s32[16]{0:T(128)S(1)} %stack.121.at, bf16[512,8192]{1,0:T(8,128)(2,1)} %refs_3_.5, bf16[512,8192]{1,0:T(8,128)(2,1)} %refs_3_.5, bf16[512,8192]{1,0:T(8,128)(2,1)} %refs_3_.5, bf16[512,8192]{1,0:T(8,128)(2,1)} %refs_3_.5, ...), custom_call_target="tpu_custom_call" | custom-call | flops 4294967296 | bytes 16777216 | tf_op jit(solution)/shard_map/pallas_call | solution.py:338
  111.5 1.3 %copy-done = f32[1024,512]{1,0:T(8,128)} copy-done((f32[1024,512]{1,0:T(8,128)}, f32[1024,512]{1,0:T(8,128)S(1)}, u32[]{:S(2)}) %copy-start) | copy-done | bytes 2097176
  112.9 1.6 %copy-done.1 = f32[1024,512]{1,0:T(8,128)S(1)} copy-done((f32[1024,512]{1,0:T(8,128)S(1)}, f32[1024,512]{1,0:T(8,128)}, u32[]{:S(2)}) %copy-start.1) | copy-done | bytes 2097176
  114.5 5.8 %shard_map.112 = (bf16[512,512]{1,0:T(8,128)(2,1)S(1)}, bf16[512,512]{1,0:T(8,128)(2,1)S(1)}) custom-call(s32[8]{0:T(128)S(1)} %stack.139.at, bf16[512,8192]{1,0:T(8,128)(2,1)} %refs_3_.5, bf16[512,8192]{1,0:T(8,128)(2,1)} %refs_3_.5, bf16[512,8192]{1,0:T(8,128)(2,1)} %refs_3_.5, bf16[512,8192]{1,0:T(8,128)(2,1)} %refs_3_.5, ...), custom_call_target="tpu_custom_call" | custom-call | flops 2147483648 | bytes 8388608 | tf_op jit(solution)/shard_map/pallas_call | solution.py:338
  120.9 1.3 %collective-permute-done.20 = bf16[512,512]{1,0:T(8,128)(2,1)S(1)} collective-permute-done((bf16[512,512]{1,0:T(8,128)(2,1)S(1)}, bf16[512,512]{1,0:T(8,128)(2,1)S(1)}, u32[]{:S(2)}, u32[]{:S(2)}) %collective-permute-start.20) | collective-permute-done | bytes 524320 | tf_op jit(solution)/shard_map/ppermute | solution.py:462
  122.3 1.1 pad_maximum_fusion
  (106 shorter events, 7.9 us)
Async XLA Ops:
  0.6 8.4 %copy-start.31 = (s32[512]{0:T(512)S(1)}, s32[512]{0:T(512)}, u32[]{:S(2)}) copy-start(s32[512]{0:T(512)} %param.15) | copy-start | bytes 6148
  0.6 8.4 %copy-start.32 = (s32[8]{0:T(128)S(1)}, s32[8]{0:T(128)}, u32[]{:S(2)}) copy-start(s32[8]{0:T(128)} %param.17) | copy-start | bytes 100
  1.7 28.0 %copy-start.6 = (bf16[256,512]{1,0:T(8,128)(2,1)}, bf16[256,512]{1,0:T(8,128)(2,1)S(1)}, u32[]{:S(2)}) copy-start(bf16[256,512]{1,0:T(8,128)(2,1)S(1)} %get-tuple-element.627.refs_0_) | copy-start | bytes 786436
  1.7 13.8 %collective-permute-start.3 = (bf16[256,512]{1,0:T(8,128)(2,1)S(1)}, bf16[256,512]{1,0:T(8,128)(2,1)S(1)}, u32[]{:S(2)}, u32[]{:S(2)}) collective-permute-start(bf16[256,512]{1,0:T(8,128)(2,1)S(1)} %get-tuple-element.627.refs_0_), channel_id=1, source_target_pairs={{0,8},{8,16},{16,24},{24,0},{1,9},{9,17},{17,25},{25,1},{2,10},{10... | collective-permute-start | bytes 786440 | tf_op jit(solution)/shard_map/ppermute | solution.py:283
  3.4 27.2 %collective-permute-start.4 = (bf16[256,512]{1,0:T(8,128)(2,1)S(1)}, bf16[256,512]{1,0:T(8,128)(2,1)S(1)}, u32[]{:S(2)}, u32[]{:S(2)}) collective-permute-start(bf16[256,512]{1,0:T(8,128)(2,1)S(1)} %get-tuple-element.627.refs_0_), channel_id=1, source_target_pairs={{0,16},{8,24},{16,0},{24,8},{1,17},{9,25},{17,1},{25,9},{2,18},{10... | collective-permute-start | bytes 786440 | tf_op jit(solution)/shard_map/ppermute | solution.py:283
  6.1 2.9 %collective-permute-start.1 = (bf16[256,512]{1,0:T(8,128)(2,1)S(1)}, bf16[256,512]{1,0:T(8,128)(2,1)S(1)}, u32[]{:S(2)}, u32[]{:S(2)}) collective-permute-start(bf16[256,512]{1,0:T(8,128)(2,1)S(1)} %get-tuple-element.628), channel_id=1, source_target_pairs={{0,1},{1,0},{2,3},{3,2},{4,5},{5,4},{6,7},{7,6},{8,9},{9,8},{10,11... | collective-permute-start | bytes 786440 | tf_op jit(solution)/shard_map/ppermute | solution.py:372
  6.1 2.9 %collective-permute-start.2 = (s32[512]{0:T(512)}, s32[512]{0:T(512)S(1)}, u32[]{:S(2)}, u32[]{:S(2)}) collective-permute-start(s32[512]{0:T(512)} %param.15), channel_id=1, source_target_pairs={{0,1},{1,0},{2,3},{3,2},{4,5},{5,4},{6,7},{7,6},{8,9},{9,8},{10,11... | collective-permute-start | bytes 6152 | tf_op jit(solution)/shard_map/ppermute | solution.py:373
  7.5 23.8 %collective-permute-start.5 = (bf16[256,512]{1,0:T(8,128)(2,1)S(1)}, bf16[256,512]{1,0:T(8,128)(2,1)S(1)}, u32[]{:S(2)}, u32[]{:S(2)}) collective-permute-start(bf16[256,512]{1,0:T(8,128)(2,1)S(1)} %get-tuple-element.627.refs_0_), channel_id=1, source_target_pairs={{0,24},{8,0},{16,8},{24,16},{1,25},{9,1},{17,9},{25,17},{2,26},{10... | collective-permute-start | bytes 786440 | tf_op jit(solution)/shard_map/ppermute | solution.py:283
  9.0 20.7 %copy-start.14 = (bf16[256,512]{1,0:T(8,128)(2,1)}, bf16[256,512]{1,0:T(8,128)(2,1)S(1)}, u32[]{:S(2)}) copy-start(bf16[256,512]{1,0:T(8,128)(2,1)S(1)} %collective-permute-done.1.refs_4_) | copy-start | bytes 786436
  9.6 20.1 %copy-start.26 = (f32[512,1]{1,0:T(8,128)}, f32[512,1]{1,0:T(8,128)S(1)}, u32[]{:S(2)}) copy-start(f32[512,1]{1,0:T(8,128)S(1)} %copy.25.tw) | copy-start | bytes 6148
  9.8 22.2 %collective-permute-start.6 = (bf16[256,512]{1,0:T(8,128)(2,1)S(1)}, bf16[256,512]{1,0:T(8,128)(2,1)S(1)}, u32[]{:S(2)}, u32[]{:S(2)}) collective-permute-start(bf16[256,512]{1,0:T(8,128)(2,1)S(1)} %collective-permute-done.1.refs_4_), channel_id=1, source_target_pairs={{0,2},{2,4},{4,6},{6,0},{1,3},{3,5},{5,7},{7,1},{8,10},{10,12},{12... | collective-permute-start | bytes 786440 | tf_op jit(solution)/shard_map/ppermute | solution.py:283
  11.9 20.8 %collective-permute-start.7 = (bf16[256,512]{1,0:T(8,128)(2,1)S(1)}, bf16[256,512]{1,0:T(8,128)(2,1)S(1)}, u32[]{:S(2)}, u32[]{:S(2)}) collective-permute-start(bf16[256,512]{1,0:T(8,128)(2,1)S(1)} %collective-permute-done.1.refs_4_), channel_id=1, source_target_pairs={{0,4},{2,6},{4,0},{6,2},{1,5},{3,7},{5,1},{7,3},{8,12},{10,14},{12... | collective-permute-start | bytes 786440 | tf_op jit(solution)/shard_map/ppermute | solution.py:283
  16.2 17.1 %collective-permute-start.8 = (bf16[256,512]{1,0:T(8,128)(2,1)S(1)}, bf16[256,512]{1,0:T(8,128)(2,1)S(1)}, u32[]{:S(2)}, u32[]{:S(2)}) collective-permute-start(bf16[256,512]{1,0:T(8,128)(2,1)S(1)} %collective-permute-done.1.refs_4_), channel_id=1, source_target_pairs={{0,6},{2,0},{4,2},{6,4},{1,7},{3,1},{5,3},{7,5},{8,14},{10,8},{12,... | collective-permute-start | bytes 786440 | tf_op jit(solution)/shard_map/ppermute | solution.py:283
  29.8 0.8 copy-start.8
  34.1 2.8 %collective-permute-start.9 = (bf16[4,128,1152]{2,1,0:T(8,128)(2,1)S(1)}, bf16[4,128,1152]{2,1,0:T(8,128)(2,1)S(1)}, u32[]{:S(2)}, u32[]{:S(2)}) collective-permute-start(bf16[4,128,1152]{2,1,0:T(8,128)(2,1)S(1)} %get-tuple-element.437), channel_id=1, source_target_pairs={{0,1},{1,0},{2,3},{3,2},{4,5},{5,4},{6,7},{7,6},{8,9},{9,8},{10,11... | collective-permute-start | bytes 3538952 | tf_op jit(solution)/shard_map/ppermute | solution.py:433
  36.9 20.0 %collective-permute-start.10 = (bf16[512,8192]{1,0:T(8,128)(2,1)}, bf16[512,8192]{1,0:T(8,128)(2,1)}, u32[]{:S(2)}, u32[]{:S(2)}) collective-permute-start(bf16[512,8192]{1,0:T(8,128)(2,1)} %refs_3_.5), channel_id=1, source_target_pairs={{0,1},{1,0},{2,3},{3,2},{4,5},{5,4},{6,7},{7,6},{8,9},{9,8},{10,11... | collective-permute-start | bytes 25165832 | tf_op jit(solution)/shard_map/ppermute | solution.py:444
  40.2 3.9 %copy-start.33 = (s32[8]{0:T(128)S(1)}, s32[8]{0:T(128)}, u32[]{:S(2)}) copy-start(s32[8]{0:T(128)} %param.16) | copy-start | bytes 100
  40.2 5.0 %copy-start.7 = (bf16[256,512]{1,0:T(8,128)(2,1)S(1)}, bf16[256,512]{1,0:T(8,128)(2,1)}, u32[]{:S(2)}) copy-start(bf16[256,512]{1,0:T(8,128)(2,1)} %copy-done.6) | copy-start | bytes 786436
  40.2 5.0 %copy-start.11 = (bf16[256,512]{1,0:T(8,128)(2,1)S(1)}, bf16[256,512]{1,0:T(8,128)(2,1)}, u32[]{:S(2)}) copy-start(bf16[256,512]{1,0:T(8,128)(2,1)} %copy-done.10) | copy-start | bytes 786436
  40.2 5.0 %copy-start.13 = (bf16[256,512]{1,0:T(8,128)(2,1)S(1)}, bf16[256,512]{1,0:T(8,128)(2,1)}, u32[]{:S(2)}) copy-start(bf16[256,512]{1,0:T(8,128)(2,1)} %copy-done.12) | copy-start | bytes 786436
  40.2 5.0 %copy-start.17 = (bf16[256,512]{1,0:T(8,128)(2,1)S(1)}, bf16[256,512]{1,0:T(8,128)(2,1)}, u32[]{:S(2)}) copy-start(bf16[256,512]{1,0:T(8,128)(2,1)} %copy-done.16) | copy-start | bytes 786436
  40.2 23.2 %all-to-all-start.3 = ((bf16[4,144,1152]{2,1,0:T(8,128)(2,1)}), bf16[4,144,1152]{2,1,0:T(8,128)(2,1)S(1)}, u32[]{:S(2)}, u32[]{:S(2)}) async-start(bf16[4,144,1152]{2,1,0:T(8,128)(2,1)} %shard_map.105), calls=%async_computation.3 | async-start | bytes 2654208 | tf_op jit(solution)/shard_map/all_to_all | solution.py:23
  45.2 1.0 copy-start.15
  46.1 0.9 copy-start.19
  47.1 0.9 copy-start.21
  48.0 0.9 copy-start.23
  50.4 34.6 %collective-permute-start.11 = (bf16[1024,512]{1,0:T(8,128)(2,1)}, bf16[1024,512]{1,0:T(8,128)(2,1)}, u32[]{:S(2)}, u32[]{:S(2)}) collective-permute-start(bf16[1024,512]{1,0:T(8,128)(2,1)} %get-tuple-element.445.refs_8_), channel_id=1, source_target_pairs={{0,2},{2,4},{4,6},{6,0},{1,3},{3,5},{5,7},{7,1},{8,10},{10,12},{12... | collective-permute-start | bytes 3145736 | tf_op jit(solution)/shard_map/ppermute | solution.py:283
  52.3 32.8 %collective-permute-start.12 = (bf16[1024,512]{1,0:T(8,128)(2,1)}, bf16[1024,512]{1,0:T(8,128)(2,1)}, u32[]{:S(2)}, u32[]{:S(2)}) collective-permute-start(bf16[1024,512]{1,0:T(8,128)(2,1)} %get-tuple-element.445.refs_8_), channel_id=1, source_target_pairs={{0,6},{2,0},{4,2},{6,4},{1,7},{3,1},{5,3},{7,5},{8,14},{10,8},{12,... | collective-permute-start | bytes 3145736 | tf_op jit(solution)/shard_map/ppermute | solution.py:283
  53.7 31.4 %collective-permute-start.13 = (bf16[1024,512]{1,0:T(8,128)(2,1)}, bf16[1024,512]{1,0:T(8,128)(2,1)}, u32[]{:S(2)}, u32[]{:S(2)}) collective-permute-start(bf16[1024,512]{1,0:T(8,128)(2,1)} %get-tuple-element.446.refs_9_), channel_id=1, source_target_pairs={{0,8},{8,16},{16,24},{24,0},{1,9},{9,17},{17,25},{25,1},{2,10},{10... | collective-permute-start | bytes 3145736 | tf_op jit(solution)/shard_map/ppermute | solution.py:283
  54.3 30.8 %collective-permute-start.14 = (bf16[1024,512]{1,0:T(8,128)(2,1)}, bf16[1024,512]{1,0:T(8,128)(2,1)}, u32[]{:S(2)}, u32[]{:S(2)}) collective-permute-start(bf16[1024,512]{1,0:T(8,128)(2,1)} %get-tuple-element.446.refs_9_), channel_id=1, source_target_pairs={{0,24},{8,0},{16,8},{24,16},{1,25},{9,1},{17,9},{25,17},{2,26},{10... | collective-permute-start | bytes 3145736 | tf_op jit(solution)/shard_map/ppermute | solution.py:283
  63.4 1.0 copy-start.5
  66.4 1.1 copy-start.2
  67.5 27.5 %all-to-all-start.4 = ((bf16[4,144,1152]{2,1,0:T(8,128)(2,1)}), bf16[4,144,1152]{2,1,0:T(8,128)(2,1)S(1)}, u32[]{:S(2)}, u32[]{:S(2)}) async-start(bf16[4,144,1152]{2,1,0:T(8,128)(2,1)} %copy-done.2), calls=%async_computation.4 | async-start | bytes 2654208 | tf_op jit(solution)/shard_map/all_to_all | solution.py:23
  71.9 27.4 %collective-permute-start.15 = (bf16[512,512]{1,0:T(8,128)(2,1)}, bf16[512,512]{1,0:T(8,128)(2,1)}, u32[]{:S(2)}, u32[]{:S(2)}) collective-permute-start(bf16[512,512]{1,0:T(8,128)(2,1)} %copy-done.8), channel_id=1, source_target_pairs={{0,1},{1,0},{2,3},{3,2},{4,5},{5,4},{6,7},{7,6},{8,9},{9,8},{10,11... | collective-permute-start | bytes 1572872 | tf_op jit(solution)/shard_map/ppermute | solution.py:445
  72.1 22.0 %copy-start.28 = (bf16[1024,512]{1,0:T(8,128)(2,1)S(1)}, bf16[1024,512]{1,0:T(8,128)(2,1)}, u32[]{:S(2)}) copy-start(bf16[1024,512]{1,0:T(8,128)(2,1)} %up_ref.1) | copy-start | bytes 3145732
  87.6 25.2 %collective-permute-start.16 = (bf16[512,512]{1,0:T(8,128)(2,1)}, bf16[512,512]{1,0:T(8,128)(2,1)}, u32[]{:S(2)}, u32[]{:S(2)}) collective-permute-start(bf16[512,512]{1,0:T(8,128)(2,1)} %get-tuple-element.455), channel_id=1, source_target_pairs={{0,2},{2,4},{4,6},{6,0},{1,3},{3,5},{5,7},{7,1},{8,10},{10,12},{12... | collective-permute-start | bytes 1572872 | tf_op jit(solution)/shard_map/ppermute | solution.py:283
  88.3 24.6 %collective-permute-start.17 = (bf16[512,512]{1,0:T(8,128)(2,1)}, bf16[512,512]{1,0:T(8,128)(2,1)}, u32[]{:S(2)}, u32[]{:S(2)}) collective-permute-start(bf16[512,512]{1,0:T(8,128)(2,1)} %get-tuple-element.456), channel_id=1, source_target_pairs={{0,6},{2,0},{4,2},{6,4},{1,7},{3,1},{5,3},{7,5},{8,14},{10,8},{12,... | collective-permute-start | bytes 1572872 | tf_op jit(solution)/shard_map/ppermute | solution.py:283
  90.9 22.0 %collective-permute-start.18 = (bf16[512,512]{1,0:T(8,128)(2,1)}, bf16[512,512]{1,0:T(8,128)(2,1)}, u32[]{:S(2)}, u32[]{:S(2)}) collective-permute-start(bf16[512,512]{1,0:T(8,128)(2,1)} %get-tuple-element.457), channel_id=1, source_target_pairs={{0,8},{8,16},{16,24},{24,0},{1,9},{9,17},{17,25},{25,1},{2,10},{10... | collective-permute-start | bytes 1572872 | tf_op jit(solution)/shard_map/ppermute | solution.py:283
  91.5 21.4 %collective-permute-start.19 = (bf16[512,512]{1,0:T(8,128)(2,1)}, bf16[512,512]{1,0:T(8,128)(2,1)}, u32[]{:S(2)}, u32[]{:S(2)}) collective-permute-start(bf16[512,512]{1,0:T(8,128)(2,1)} %get-tuple-element.458), channel_id=1, source_target_pairs={{0,24},{8,0},{16,8},{24,16},{1,25},{9,1},{17,9},{25,17},{2,26},{10... | collective-permute-start | bytes 1572872 | tf_op jit(solution)/shard_map/ppermute | solution.py:283
  95.2 0.7 copy-start.4
  95.9 16.9 %all-to-all-start.5 = ((bf16[4,304,128]{2,1,0:T(8,128)(2,1)}), bf16[4,304,128]{2,1,0:T(8,128)(2,1)S(1)}, u32[]{:S(2)}, u32[]{:S(2)}) async-start(bf16[4,304,128]{2,1,0:T(8,128)(2,1)} %copy-done.4), calls=%async_computation.5 | async-start | bytes 622592 | tf_op jit(solution)/shard_map/all_to_all | solution.py:23
  99.4 1.0 copy-start.3
  100.4 1.0 copy-start.9
  111.5 1.3 %copy-start = (f32[1024,512]{1,0:T(8,128)}, f32[1024,512]{1,0:T(8,128)S(1)}, u32[]{:S(2)}) copy-start(f32[1024,512]{1,0:T(8,128)S(1)} %shard_map.109.refs_12_) | copy-start | bytes 6291460
  112.9 1.6 %copy-start.1 = (f32[1024,512]{1,0:T(8,128)S(1)}, f32[1024,512]{1,0:T(8,128)}, u32[]{:S(2)}) copy-start(f32[1024,512]{1,0:T(8,128)} %copy-done) | copy-start | bytes 6291460
  120.3 2.0 %collective-permute-start.20 = (bf16[512,512]{1,0:T(8,128)(2,1)S(1)}, bf16[512,512]{1,0:T(8,128)(2,1)S(1)}, u32[]{:S(2)}, u32[]{:S(2)}) collective-permute-start(bf16[512,512]{1,0:T(8,128)(2,1)S(1)} %get-tuple-element.461), channel_id=1, source_target_pairs={{0,1},{1,0},{2,3},{3,2},{4,5},{5,4},{6,7},{7,6},{8,9},{9,8},{10,11... | collective-permute-start | bytes 1572872 | tf_op jit(solution)/shard_map/ppermute | solution.py:462
  122.3 1.1 copy-start.27
  122.3 1.7 %copy-start.29 = (bf16[1024,512]{1,0:T(8,128)(2,1)S(1)}, bf16[1024,512]{1,0:T(8,128)(2,1)}, u32[]{:S(2)}) copy-start(bf16[1024,512]{1,0:T(8,128)(2,1)} %up_ref.1) | copy-start | bytes 3145732
  (8 other events, 5.5 us)

commit v6 on v5

--- a/solution.py
+++ b/solution.py
@@ -23,7 +23,7 @@
     return lax.all_to_all(a, axis, 0, 0, tiled=True)
 
 
-def call(body, out, grid, in_specs, out_specs, scratch=(), flops=0, data=0, vmem=40):
+def call(body, out, grid, in_specs, out_specs, scratch=(), flops=0, data=0, vmem=12):
     return pl.pallas_call(
         body,
         out_shape=out,
@@ -38,6 +38,10 @@
 
 def whole(shape):
     return pl.BlockSpec(shape, lambda *i: (0,) * len(shape))
+
+
+def once(shape):
+    return pl.BlockSpec(shape, lambda *i: (0,) * len(shape), pipeline_mode=pl.Buffered(1))
 
 
 def terms(tokens, down, up, cotangent, tasks, token_weight, pick_t, col_task, v_from, me_c, nx, nz):
@@ -108,20 +112,20 @@
             pl.BlockSpec(memory_space=pltpu.SMEM),
             pl.BlockSpec((n_tok, blk), lambda i: (0, i)),
             pl.BlockSpec((blk, cols), lambda i: (i, 0)),
-            whole((kv, cols)),
-            whole((n_tok, kv)),
-            whole((n_tok, 1)),
-            whole((1, n_tok)),
-            whole((n_tok, 1)),
-            whole((sc, cols)),
-            whole((sc, 1)),
-            whole((1, kv)),
+            once((kv, cols)),
+            once((n_tok, kv)),
+            once((n_tok, 1)),
+            once((1, n_tok)),
+            once((n_tok, 1)),
+            once((sc, cols)),
+            once((sc, 1)),
+            once((1, kv)),
         ],
         (whole((n_tok, cols)), whole((nz, sc, lanes)), whole((nz, sc, lanes))),
         [pltpu.VMEM((n_tok, cols), F32), pltpu.VMEM((n_tok, kv), BF), pltpu.VMEM((sc, n_tok), BF)],
         flops=2 * n_tok * width * (cols + sc),
         data=24 * MIB,
-        vmem=48,
+        vmem=28,
     )(
         me_c,
         tokens,
@@ -150,7 +154,7 @@
         body,
         tuple(jax.ShapeDtypeStruct((n * rows, lanes), BF) for _ in lists),
         (1,),
-        [whole((rows, lanes))] * (n * len(lists)),
+        [once((rows, lanes))] * (n * len(lists)),
         tuple(whole((n * rows, lanes)) for _ in lists),
         data=4 * MIB,
     )(*[a for one in lists for a in one])
@@ -219,7 +223,7 @@
         body,
         jax.ShapeDtypeStruct((ny, own + INFO, lanes), BF),
         (ny,),
-        [whole((n, rows, lanes)), pl.BlockSpec((own, 1), lambda i: (i, 0))],
+        [once((n, rows, lanes)), pl.BlockSpec((own, 1), lambda i: (i, 0))],
         pl.BlockSpec((1, own + INFO, lanes), lambda i: (i, 0, 0)),
         flops=2 * cols * n * sc * lanes,
         data=5 * MIB,
@@ -292,8 +296,11 @@
     blk = rows // per
     flat = [w for group in groups for w in group]
     extra = [] if before is None else [before]
+    extra_specs = [once(e.shape) for e in extra]
     if lora is not None:
         extra += list(lora)
+        extra_specs += [once(e.shape) for e in lora[:2]]
+        extra_specs.append(pl.BlockSpec((n, lora[2].shape[1]), lambda i, s: (s[steps * per], 0)))
 
     def body(at, *refs):
         tok_a, tok_b = refs[:per], refs[per : 2 * per]
@@ -341,11 +348,11 @@
         grid_spec=pltpu.PrefetchScalarGridSpec(
             num_scalar_prefetch=1,
             grid=(steps,),
-            in_specs=tok_specs * 2 + [whole(w.shape) for w in flat] + [whole(e.shape) for e in extra],
+            in_specs=tok_specs * 2 + [once(w.shape) for w in flat] + extra_specs,
             out_specs=(whole((n_tok, n)),) * 2 if final else whole(shape),
             scratch_shapes=[pltpu.VMEM(shape, F32)] if final else [],
         ),
-        compiler_params=pltpu.CompilerParams(vmem_limit_bytes=40 * MIB),
+        compiler_params=pltpu.CompilerParams(vmem_limit_bytes=22 * MIB),
         cost_estimate=pl.CostEstimate(
             flops=4 * n_tok * rows * n * steps, bytes_accessed=8 * n_tok * rows * steps, transcendentals=0
         ),
@@ -430,8 +437,9 @@
 
     hidden, theirs, mine, note = local_terms(jnp.int32(0))
     first_hop, theirs = lax.optimization_barrier((first_hop, theirs))
+    near_a, near_b = join([block_a] + first_hop[: nx - 1], [block_b] + first_hop[nx - 1 :])
+    near_a, near_b, theirs = lax.optimization_barrier((near_a, near_b, theirs))
     got = lax.ppermute(theirs, "c", SWAP)
-    near_a, near_b = join([block_a] + first_hop[: nx - 1], [block_b] + first_hop[nx - 1 :])
     a_down, a_up = shifted(near_a, "z", 1), shifted(near_a, "z", nz - 1)
     b_down, b_up = shifted(near_b, "x", 1), shifted(near_b, "x", nx - 1)
     pass_on = halves([a_down, a_up, b_down, b_up], [0, 1, 0, 1])
@@ -443,7 +451,13 @@
     sent_tokens, sent_hidden, _ = lax.optimization_barrier((tokens, hidden, got))
     other = lax.ppermute(sent_tokens, "c", SWAP)
     other_hidden = lax.ppermute(sent_hidden, "c", SWAP)
-    acc = add_blocks(tokens, other, [[near_a], [near_b]], at(blocks_a(0), blocks_b(0)))
+    acc = add_blocks(
+        tokens,
+        other,
+        [[near_a], [near_b]],
+        at(blocks_a(0), blocks_b(0), [me_c]),
+        lora=(hidden, other_hidden, up),
+    )
     from_z, acc = lax.optimization_barrier((from_z, acc))
     from_y = exchange(spread(from_z, owned_col, ny), "y")
     by_x = turn(from_y, nx, d_rows)
@@ -455,7 +469,6 @@
         [[a_down], [a_up], [b_down], [b_up]],
         at(blocks_a(-1), blocks_a(1), blocks_b(-1), blocks_b(1)),
         before=acc,
-        lora=(hidden, other_hidden, lax.dynamic_slice_in_dim(up, me_c * half, half, 0)),
     )
     acc, flags = lax.optimization_barrier((acc, flags))
     tile, sent = add_blocks(tokens, other, [a_far, b_far], at(blocks_a(2), blocks_b(2)), before=acc, final=True)

time: 127 us -> 120 us (0.945)
  local copies, waits for them, and re-layouts: 22.5 us -> 13.7 us
  waiting for transfers between devices: 17.8 us -> 20.6 us
    unnamed x66 -> x36, local copies, waits for them, and re-layouts: 17.7 us -> 9.81 us
    ppermute x1, waiting for transfers between devices: 0.01 us -> 1.52 us  [per_device(): other_hidden = lax.ppermute(sent_hidden, 'c', SWAP)]
  transfers between devices with their start and end apart: 23 -> 23, of which waited for: 4 -> 5; matrix products, arithmetic and copies ran while one was open for 4% -> 4% of each run, Pallas kernels for 29% -> 30%
where the time goes in v6:
time: 120 us; the launch traced here: 119 us
  Pallas kernels  42.3 us (35%)
  starting transfers between devices  37.1 us (31%)
  waiting for transfers between devices  20.6 us (17%)
  local copies, waits for them, and re-layouts  13.7 us (11%)
  other arithmetic  2.46 us (2%)
  between operations  1.68 us (1%)
    ppermute x14, starting transfers between devices, shifted(): return lax.ppermute(a, axis, [(i, (i + step) % n) for i in range(n)])  24.3 us
    pallas_call x3, Pallas kernels, add_blocks(): pl.pallas_call(body, out_shape=(jax.ShapeDtypeStruct((n_tok, n), BF),) *...  21.6 us
    ppermute x14, waiting for transfers between devices, shifted(): return lax.ppermute(a, axis, [(i, (i + step) % n) for i in range(n)])  13.1 us
    pallas_call x1, Pallas kernels, terms(): call(body, (jax.ShapeDtypeStruct((n_tok, cols), BF), jax.ShapeDtypeStruct...  12.5 us
    all_to_all x3, starting transfers between devices, exchange(): return lax.all_to_all(a, axis, 0, 0, tiled=True)  11.6 us
    unnamed x36, local copies, waits for them, and re-layouts  9.81 us
    ppermute x1, waiting for transfers between devices, per_device(): got = lax.ppermute(theirs, 'c', SWAP)  2.84 us
    pallas_call x1, Pallas kernels, halves(): call(body, tuple((jax.ShapeDtypeStruct((rows // 2, lanes), BF) for _ in a...  2.58 us
  transfers between devices with their start and end apart: 23, of which 5 were waited for; matrix products, arithmetic and copies ran while one was open for 4% of the time, Pallas kernels for 30%

profile of v6, /device:TPU:0, one launch (start us, length us, event | category | flops | bytes accessed | tf_op | source)
XLA Modules:
  0.0 118.5 jit_solution(11568377648793472194)
XLA Ops:
  0.7 1.1 constant_dynamic-slice_fusion
  1.7 1.6 %collective-permute-start.3 = (bf16[256,512]{1,0:T(8,128)(2,1)S(1)}, bf16[256,512]{1,0:T(8,128)(2,1)S(1)}, u32[]{:S(2)}, u32[]{:S(2)}) collective-permute-start(bf16[256,512]{1,0:T(8,128)(2,1)S(1)} %get-tuple-element.633.refs_0_), channel_id=1, source_target_pairs={{0,8},{8,16},{16,24},{24,0},{1,9},{9,17},{17,25},{25,1},{2,10},{10... | collective-permute-start | bytes 786440 | tf_op jit(solution)/shard_map/ppermute | solution.py:287
  3.4 2.7 %collective-permute-start.4 = (bf16[256,512]{1,0:T(8,128)(2,1)S(1)}, bf16[256,512]{1,0:T(8,128)(2,1)S(1)}, u32[]{:S(2)}, u32[]{:S(2)}) collective-permute-start(bf16[256,512]{1,0:T(8,128)(2,1)S(1)} %get-tuple-element.633.refs_0_), channel_id=1, source_target_pairs={{0,16},{8,24},{16,0},{24,8},{1,17},{9,25},{17,1},{25,9},{2,18},{10... | collective-permute-start | bytes 786440 | tf_op jit(solution)/shard_map/ppermute | solution.py:287
  6.1 0.5 collective-permute-start.2
  6.7 0.8 copy.24.task_col
  7.5 1.5 %collective-permute-start.5 = (bf16[256,512]{1,0:T(8,128)(2,1)S(1)}, bf16[256,512]{1,0:T(8,128)(2,1)S(1)}, u32[]{:S(2)}, u32[]{:S(2)}) collective-permute-start(bf16[256,512]{1,0:T(8,128)(2,1)S(1)} %get-tuple-element.633.refs_0_), channel_id=1, source_target_pairs={{0,24},{8,0},{16,8},{24,16},{1,25},{9,1},{17,9},{25,17},{2,26},{10... | collective-permute-start | bytes 786440 | tf_op jit(solution)/shard_map/ppermute | solution.py:287
  9.7 2.0 %collective-permute-start.6 = (bf16[256,512]{1,0:T(8,128)(2,1)S(1)}, bf16[256,512]{1,0:T(8,128)(2,1)S(1)}, u32[]{:S(2)}, u32[]{:S(2)}) collective-permute-start(bf16[256,512]{1,0:T(8,128)(2,1)S(1)} %collective-permute-done.1.refs_4_), channel_id=1, source_target_pairs={{0,2},{2,4},{4,6},{6,0},{1,3},{3,5},{5,7},{7,1},{8,10},{10,12},{12... | collective-permute-start | bytes 786440 | tf_op jit(solution)/shard_map/ppermute | solution.py:287
  11.8 3.7 %collective-permute-start.7 = (bf16[256,512]{1,0:T(8,128)(2,1)S(1)}, bf16[256,512]{1,0:T(8,128)(2,1)S(1)}, u32[]{:S(2)}, u32[]{:S(2)}) collective-permute-start(bf16[256,512]{1,0:T(8,128)(2,1)S(1)} %collective-permute-done.1.refs_4_), channel_id=1, source_target_pairs={{0,4},{2,6},{4,0},{6,2},{1,5},{3,7},{5,1},{7,3},{8,12},{10,14},{12... | collective-permute-start | bytes 786440 | tf_op jit(solution)/shard_map/ppermute | solution.py:287
  15.5 1.0 collective-permute-start.8
  16.5 12.5 %shard_map.103 = (bf16[512,512]{1,0:T(8,128)(2,1)S(1)}, bf16[4,128,1152]{2,1,0:T(8,128)(2,1)S(1)}, bf16[4,128,1152]{2,1,0:T(8,128)(2,1)S(1)}) custom-call(s32[1]{0:T(128)} %bitcast.16.me, bf16[512,8192]{1,0:T(8,128)(2,1)} %refs_3_.5, bf16[8192,512]{1,0:T(8,128)(2,1)} %dn.1, bf16[1024,512]{1,0:T(8,128)(2,1)} %refs_12_.1, bf16[512,1024]{1,0:T(8,128)(2,1)} %cot, ...), custom_call_target="tpu_custom_call" | custom-call | flops 5368709120 | bytes 25165824 | tf_op jit(solution)/shard_map/pallas_call | solution.py:103
  29.1 1.4 %shard_map.104 = (bf16[1024,512]{1,0:T(8,128)(2,1)}, bf16[1024,512]{1,0:T(8,128)(2,1)}) custom-call(bf16[256,512]{1,0:T(8,128)(2,1)S(1)} %get-tuple-element.633.refs_0_, bf16[256,512]{1,0:T(8,128)(2,1)S(1)} %collective-permute-done.3.refs_1_, bf16[256,512]{1,0:T(8,128)(2,1)S(1)} %collective-permute-done.4.refs_2_, ...), custom_call_target="tpu_custom_call" | custom-call | bytes 4194304 | tf_op jit(solution)/shard_map/pallas_call | solution.py:153
  30.5 2.8 %collective-permute-done.9.b = bf16[4,128,1152]{2,1,0:T(8,128)(2,1)S(1)} collective-permute-done((bf16[4,128,1152]{2,1,0:T(8,128)(2,1)S(1)}, bf16[4,128,1152]{2,1,0:T(8,128)(2,1)S(1)}, u32[]{:S(2)}, u32[]{:S(2)}) %collective-permute-start.9) | collective-permute-done | bytes 1179680 | tf_op jit(solution)/shard_map/ppermute | solution.py:442
  33.5 0.6 convert_reduce_fusion.2
  34.9 1.8 %shard_map.105 = bf16[4,144,1152]{2,1,0:T(8,128)(2,1)} custom-call(bf16[4,128,1152]{2,1,0:T(8,128)(2,1)S(1)} %get-tuple-element.453.a, bf16[4,128,1152]{2,1,0:T(8,128)(2,1)S(1)} %collective-permute-done.9.b, bf16[16,1152]{1,0:T(8,128)(2,1)S(1)} %select_convert_fusion.1.c), custom_call_target="tpu_custom_call" | custom-call | bytes 10485760 | tf_op jit(solution)/shard_map/pallas_call | solution.py:190
  36.7 3.7 %all-to-all-start.3 = ((bf16[4,144,1152]{2,1,0:T(8,128)(2,1)}), bf16[4,144,1152]{2,1,0:T(8,128)(2,1)S(1)}, u32[]{:S(2)}, u32[]{:S(2)}) async-start(bf16[4,144,1152]{2,1,0:T(8,128)(2,1)} %shard_map.105), calls=%async_computation.3 | async-start | bytes 2654208 | tf_op jit(solution)/shard_map/all_to_all | solution.py:23
  40.4 0.5 collective-permute-start.15
  40.9 0.9 broadcast_in_dim_reshape.8.ow
  41.9 1.6 %collective-permute-start.11 = (bf16[1024,512]{1,0:T(8,128)(2,1)}, bf16[1024,512]{1,0:T(8,128)(2,1)}, u32[]{:S(2)}, u32[]{:S(2)}) collective-permute-start(bf16[1024,512]{1,0:T(8,128)(2,1)} %get-tuple-element.451.refs_8_), channel_id=1, source_target_pairs={{0,2},{2,4},{4,6},{6,0},{1,3},{3,5},{5,7},{7,1},{8,10},{10,12},{12... | collective-permute-start | bytes 3145736 | tf_op jit(solution)/shard_map/ppermute | solution.py:287
  43.6 1.6 %collective-permute-start.12 = (bf16[1024,512]{1,0:T(8,128)(2,1)}, bf16[1024,512]{1,0:T(8,128)(2,1)}, u32[]{:S(2)}, u32[]{:S(2)}) collective-permute-start(bf16[1024,512]{1,0:T(8,128)(2,1)} %get-tuple-element.451.refs_8_), channel_id=1, source_target_pairs={{0,6},{2,0},{4,2},{6,4},{1,7},{3,1},{5,3},{7,5},{8,14},{10,8},{12,... | collective-permute-start | bytes 3145736 | tf_op jit(solution)/shard_map/ppermute | solution.py:287
  45.2 0.6 collective-permute-start.13
  45.8 1.5 %collective-permute-done.15.refs_11_ = bf16[512,512]{1,0:T(8,128)(2,1)S(1)} collective-permute-done((bf16[512,512]{1,0:T(8,128)(2,1)S(1)}, bf16[512,512]{1,0:T(8,128)(2,1)S(1)}, u32[]{:S(2)}, u32[]{:S(2)}) %collective-permute-start.15) | collective-permute-done | bytes 524320 | tf_op jit(solution)/shard_map/ppermute | solution.py:453
  47.3 0.8 copy-done.8
  48.1 1.4 %collective-permute-start.14 = (bf16[1024,512]{1,0:T(8,128)(2,1)}, bf16[1024,512]{1,0:T(8,128)(2,1)}, u32[]{:S(2)}, u32[]{:S(2)}) collective-permute-start(bf16[1024,512]{1,0:T(8,128)(2,1)} %get-tuple-element.452.refs_9_), channel_id=1, source_target_pairs={{0,24},{8,0},{16,8},{24,16},{1,25},{9,1},{17,9},{25,17},{2,26},{10... | collective-permute-start | bytes 3145736 | tf_op jit(solution)/shard_map/ppermute | solution.py:287
  49.5 1.0 copy-done.7
  50.5 1.0 copy-done.9
  51.6 6.5 %shard_map.106.refs_12_ = f32[1024,512]{1,0:T(8,128)S(1)} custom-call(s32[9]{0:T(128)S(1)} %stack.131.at, bf16[512,8192]{1,0:T(8,128)(2,1)} %refs_3_.5, bf16[512,8192]{1,0:T(8,128)(2,1)} %refs_3_.5, bf16[512,8192]{1,0:T(8,128)(2,1)} %refs_3_.5, bf16[512,8192]{1,0:T(8,128)(2,1)} %refs_3_.5, ...), custom_call_target="tpu_custom_call" | custom-call | flops 2147483648 | bytes 8388608 | tf_op jit(solution)/shard_map/pallas_call | solution.py:345
  58.1 1.8 %all-to-all-done.3.g = bf16[4,144,1152]{2,1,0:T(8,128)(2,1)S(1)} async-done(((bf16[4,144,1152]{2,1,0:T(8,128)(2,1)}), bf16[4,144,1152]{2,1,0:T(8,128)(2,1)S(1)}, u32[]{:S(2)}, u32[]{:S(2)}) %all-to-all-start.3) | async-done | bytes 1327136 | tf_op jit(solution)/shard_map/all_to_all | solution.py:23
  59.9 0.9 copy-done.4
  60.8 2.1 %shard_map.107 = bf16[4,144,1152]{2,1,0:T(8,128)(2,1)S(1)} custom-call(bf16[4,144,1152]{2,1,0:T(8,128)(2,1)S(1)} %all-to-all-done.3.g, f32[512,1]{1,0:T(8,128)S(1)} %copy-done.4), custom_call_target="tpu_custom_call" | custom-call | flops 603979776 | bytes 5242880 | tf_op jit(solution)/shard_map/pallas_call | solution.py:222
  62.9 1.1 copy-done.2
  64.0 4.5 %all-to-all-start.4 = ((bf16[4,144,1152]{2,1,0:T(8,128)(2,1)}), bf16[4,144,1152]{2,1,0:T(8,128)(2,1)S(1)}, u32[]{:S(2)}, u32[]{:S(2)}) async-start(bf16[4,144,1152]{2,1,0:T(8,128)(2,1)} %copy-done.2), calls=%async_computation.4 | async-start | bytes 2654208 | tf_op jit(solution)/shard_map/all_to_all | solution.py:23
  68.5 13.1 %collective-permute-done.11.refs_8_.refs_0_ = bf16[1024,512]{1,0:T(8,128)(2,1)} collective-permute-done((bf16[1024,512]{1,0:T(8,128)(2,1)}, bf16[1024,512]{1,0:T(8,128)(2,1)}, u32[]{:S(2)}, u32[]{:S(2)}) %collective-permute-start.11) | collective-permute-done | bytes 1048608 | tf_op jit(solution)/shard_map/ppermute | solution.py:287
  81.6 2.6 %shard_map.111 = (bf16[512,512]{1,0:T(8,128)(2,1)}, bf16[512,512]{1,0:T(8,128)(2,1)}, bf16[512,512]{1,0:T(8,128)(2,1)}, bf16[512,512]{1,0:T(8,128)(2,1)}) custom-call(bf16[1024,512]{1,0:T(8,128)(2,1)} %collective-permute-done.11.refs_8_.refs_0_, bf16[1024,512]{1,0:T(8,128)(2,1)} %collective-permute-done.12.refs_9_.refs_1_, ...), custom_call_target="tpu_custom_call" | custom-call | bytes 4194304 | tf_op jit(solution)/shard_map/pallas_call | solution.py:172
  84.5 3.0 %collective-permute-start.17 = (bf16[512,512]{1,0:T(8,128)(2,1)}, bf16[512,512]{1,0:T(8,128)(2,1)}, u32[]{:S(2)}, u32[]{:S(2)}) collective-permute-start(bf16[512,512]{1,0:T(8,128)(2,1)} %get-tuple-element.462), channel_id=1, source_target_pairs={{0,6},{2,0},{4,2},{6,4},{1,7},{3,1},{5,3},{7,5},{8,14},{10,8},{12,... | collective-permute-start | bytes 1572872 | tf_op jit(solution)/shard_map/ppermute | solution.py:287
  87.5 0.6 collective-permute-start.18
  88.1 2.6 %collective-permute-start.19 = (bf16[512,512]{1,0:T(8,128)(2,1)}, bf16[512,512]{1,0:T(8,128)(2,1)}, u32[]{:S(2)}, u32[]{:S(2)}) collective-permute-start(bf16[512,512]{1,0:T(8,128)(2,1)} %get-tuple-element.464), channel_id=1, source_target_pairs={{0,24},{8,0},{16,8},{24,16},{1,25},{9,1},{17,9},{25,17},{2,26},{10... | collective-permute-start | bytes 1572872 | tf_op jit(solution)/shard_map/ppermute | solution.py:287
  91.2 0.7 copy-done.3
  91.9 3.5 %all-to-all-start.5 = ((bf16[4,304,128]{2,1,0:T(8,128)(2,1)}), bf16[4,304,128]{2,1,0:T(8,128)(2,1)S(1)}, u32[]{:S(2)}, u32[]{:S(2)}) async-start(bf16[4,304,128]{2,1,0:T(8,128)(2,1)} %copy-done.3), calls=%async_computation.5 | async-start | bytes 622592 | tf_op jit(solution)/shard_map/all_to_all | solution.py:23
  95.3 9.3 %shard_map.109.refs_12_ = f32[1024,512]{1,0:T(8,128)S(1)} custom-call(s32[16]{0:T(128)S(1)} %stack.122.at, bf16[512,8192]{1,0:T(8,128)(2,1)} %refs_3_.5, bf16[512,8192]{1,0:T(8,128)(2,1)} %refs_3_.5, bf16[512,8192]{1,0:T(8,128)(2,1)} %refs_3_.5, bf16[512,8192]{1,0:T(8,128)(2,1)} %refs_3_.5, ...), custom_call_target="tpu_custom_call" | custom-call | flops 4294967296 | bytes 16777216 | tf_op jit(solution)/shard_map/pallas_call | solution.py:345
  104.7 1.4 %copy-done = f32[1024,512]{1,0:T(8,128)} copy-done((f32[1024,512]{1,0:T(8,128)}, f32[1024,512]{1,0:T(8,128)S(1)}, u32[]{:S(2)}) %copy-start) | copy-done | bytes 2097176
  106.1 1.6 %copy-done.1 = f32[1024,512]{1,0:T(8,128)S(1)} copy-done((f32[1024,512]{1,0:T(8,128)S(1)}, f32[1024,512]{1,0:T(8,128)}, u32[]{:S(2)}) %copy-start.1) | copy-done | bytes 2097176
  107.7 5.8 %shard_map.112 = (bf16[512,512]{1,0:T(8,128)(2,1)S(1)}, bf16[512,512]{1,0:T(8,128)(2,1)S(1)}) custom-call(s32[8]{0:T(128)S(1)} %stack.140.at, bf16[512,8192]{1,0:T(8,128)(2,1)} %refs_3_.5, bf16[512,8192]{1,0:T(8,128)(2,1)} %refs_3_.5, bf16[512,8192]{1,0:T(8,128)(2,1)} %refs_3_.5, bf16[512,8192]{1,0:T(8,128)(2,1)} %refs_3_.5, ...), custom_call_target="tpu_custom_call" | custom-call | flops 2147483648 | bytes 8388608 | tf_op jit(solution)/shard_map/pallas_call | solution.py:345
  113.6 0.5 slice.11
  114.1 1.4 %collective-permute-done.20 = bf16[512,512]{1,0:T(8,128)(2,1)S(1)} collective-permute-done((bf16[512,512]{1,0:T(8,128)(2,1)S(1)}, bf16[512,512]{1,0:T(8,128)(2,1)S(1)}, u32[]{:S(2)}, u32[]{:S(2)}) %collective-permute-start.20) | collective-permute-done | bytes 524320 | tf_op jit(solution)/shard_map/ppermute | solution.py:475
  115.6 1.1 pad_maximum_fusion
  116.7 0.5 copy-done.11
  117.2 0.6 while.20
  117.9 0.6 copy-done.10
  (75 shorter events, 2.3 us)
Async XLA Ops:
  0.6 8.4 %copy-start.16 = (s32[512]{0:T(512)S(1)}, s32[512]{0:T(512)}, u32[]{:S(2)}) copy-start(s32[512]{0:T(512)} %param.15) | copy-start | bytes 6148
  0.6 8.4 %copy-start.17 = (s32[8]{0:T(128)S(1)}, s32[8]{0:T(128)}, u32[]{:S(2)}) copy-start(s32[8]{0:T(128)} %param.17) | copy-start | bytes 100
  1.7 13.8 %collective-permute-start.3 = (bf16[256,512]{1,0:T(8,128)(2,1)S(1)}, bf16[256,512]{1,0:T(8,128)(2,1)S(1)}, u32[]{:S(2)}, u32[]{:S(2)}) collective-permute-start(bf16[256,512]{1,0:T(8,128)(2,1)S(1)} %get-tuple-element.633.refs_0_), channel_id=1, source_target_pairs={{0,8},{8,16},{16,24},{24,0},{1,9},{9,17},{17,25},{25,1},{2,10},{10... | collective-permute-start | bytes 786440 | tf_op jit(solution)/shard_map/ppermute | solution.py:287
  3.4 25.7 %collective-permute-start.4 = (bf16[256,512]{1,0:T(8,128)(2,1)S(1)}, bf16[256,512]{1,0:T(8,128)(2,1)S(1)}, u32[]{:S(2)}, u32[]{:S(2)}) collective-permute-start(bf16[256,512]{1,0:T(8,128)(2,1)S(1)} %get-tuple-element.633.refs_0_), channel_id=1, source_target_pairs={{0,16},{8,24},{16,0},{24,8},{1,17},{9,25},{17,1},{25,9},{2,18},{10... | collective-permute-start | bytes 786440 | tf_op jit(solution)/shard_map/ppermute | solution.py:287
  6.1 2.9 %collective-permute-start.1 = (bf16[256,512]{1,0:T(8,128)(2,1)S(1)}, bf16[256,512]{1,0:T(8,128)(2,1)S(1)}, u32[]{:S(2)}, u32[]{:S(2)}) collective-permute-start(bf16[256,512]{1,0:T(8,128)(2,1)S(1)} %get-tuple-element.634), channel_id=1, source_target_pairs={{0,1},{1,0},{2,3},{3,2},{4,5},{5,4},{6,7},{7,6},{8,9},{9,8},{10,11... | collective-permute-start | bytes 786440 | tf_op jit(solution)/shard_map/ppermute | solution.py:379
  6.1 2.9 %collective-permute-start.2 = (s32[512]{0:T(512)}, s32[512]{0:T(512)S(1)}, u32[]{:S(2)}, u32[]{:S(2)}) collective-permute-start(s32[512]{0:T(512)} %param.15), channel_id=1, source_target_pairs={{0,1},{1,0},{2,3},{3,2},{4,5},{5,4},{6,7},{7,6},{8,9},{9,8},{10,11... | collective-permute-start | bytes 6152 | tf_op jit(solution)/shard_map/ppermute | solution.py:380
  7.5 21.6 %collective-permute-start.5 = (bf16[256,512]{1,0:T(8,128)(2,1)S(1)}, bf16[256,512]{1,0:T(8,128)(2,1)S(1)}, u32[]{:S(2)}, u32[]{:S(2)}) collective-permute-start(bf16[256,512]{1,0:T(8,128)(2,1)S(1)} %get-tuple-element.633.refs_0_), channel_id=1, source_target_pairs={{0,24},{8,0},{16,8},{24,16},{1,25},{9,1},{17,9},{25,17},{2,26},{10... | collective-permute-start | bytes 786440 | tf_op jit(solution)/shard_map/ppermute | solution.py:287
  9.6 19.4 %copy-start.14 = (f32[512,1]{1,0:T(8,128)}, f32[512,1]{1,0:T(8,128)S(1)}, u32[]{:S(2)}) copy-start(f32[512,1]{1,0:T(8,128)S(1)} %copy.25.tw) | copy-start | bytes 6148
  9.7 19.3 %collective-permute-start.6 = (bf16[256,512]{1,0:T(8,128)(2,1)S(1)}, bf16[256,512]{1,0:T(8,128)(2,1)S(1)}, u32[]{:S(2)}, u32[]{:S(2)}) collective-permute-start(bf16[256,512]{1,0:T(8,128)(2,1)S(1)} %collective-permute-done.1.refs_4_), channel_id=1, source_target_pairs={{0,2},{2,4},{4,6},{6,0},{1,3},{3,5},{5,7},{7,1},{8,10},{10,12},{12... | collective-permute-start | bytes 786440 | tf_op jit(solution)/shard_map/ppermute | solution.py:287
  11.8 17.2 %collective-permute-start.7 = (bf16[256,512]{1,0:T(8,128)(2,1)S(1)}, bf16[256,512]{1,0:T(8,128)(2,1)S(1)}, u32[]{:S(2)}, u32[]{:S(2)}) collective-permute-start(bf16[256,512]{1,0:T(8,128)(2,1)S(1)} %collective-permute-done.1.refs_4_), channel_id=1, source_target_pairs={{0,4},{2,6},{4,0},{6,2},{1,5},{3,7},{5,1},{7,3},{8,12},{10,14},{12... | collective-permute-start | bytes 786440 | tf_op jit(solution)/shard_map/ppermute | solution.py:287
  15.5 13.6 %collective-permute-start.8 = (bf16[256,512]{1,0:T(8,128)(2,1)S(1)}, bf16[256,512]{1,0:T(8,128)(2,1)S(1)}, u32[]{:S(2)}, u32[]{:S(2)}) collective-permute-start(bf16[256,512]{1,0:T(8,128)(2,1)S(1)} %collective-permute-done.1.refs_4_), channel_id=1, source_target_pairs={{0,6},{2,0},{4,2},{6,4},{1,7},{3,1},{5,3},{7,5},{8,14},{10,8},{12,... | collective-permute-start | bytes 786440 | tf_op jit(solution)/shard_map/ppermute | solution.py:287
  29.0 4.4 %copy-start.5 = (bf16[512,512]{1,0:T(8,128)(2,1)}, bf16[512,512]{1,0:T(8,128)(2,1)S(1)}, u32[]{:S(2)}) copy-start(bf16[512,512]{1,0:T(8,128)(2,1)S(1)} %get-tuple-element.454.refs_10_) | copy-start | bytes 1572868
  30.5 2.8 %collective-permute-start.9 = (bf16[4,128,1152]{2,1,0:T(8,128)(2,1)S(1)}, bf16[4,128,1152]{2,1,0:T(8,128)(2,1)S(1)}, u32[]{:S(2)}, u32[]{:S(2)}) collective-permute-start(bf16[4,128,1152]{2,1,0:T(8,128)(2,1)S(1)} %get-tuple-element.449), channel_id=1, source_target_pairs={{0,1},{1,0},{2,3},{3,2},{4,5},{5,4},{6,7},{7,6},{8,9},{9,8},{10,11... | collective-permute-start | bytes 3538952 | tf_op jit(solution)/shard_map/ppermute | solution.py:442
  33.4 16.1 %collective-permute-start.10 = (bf16[512,8192]{1,0:T(8,128)(2,1)}, bf16[512,8192]{1,0:T(8,128)(2,1)}, u32[]{:S(2)}, u32[]{:S(2)}) collective-permute-start(bf16[512,8192]{1,0:T(8,128)(2,1)} %refs_3_.5), channel_id=1, source_target_pairs={{0,1},{1,0},{2,3},{3,2},{4,5},{5,4},{6,7},{7,6},{8,9},{9,8},{10,11... | collective-permute-start | bytes 25165832 | tf_op jit(solution)/shard_map/ppermute | solution.py:452
  36.7 3.7 %copy-start.6 = (bf16[512,512]{1,0:T(8,128)(2,1)S(1)}, bf16[512,512]{1,0:T(8,128)(2,1)}, u32[]{:S(2)}) copy-start(bf16[512,512]{1,0:T(8,128)(2,1)} %copy-done.5) | copy-start | bytes 1572868
  36.7 4.1 %copy-start.18 = (s32[8]{0:T(128)S(1)}, s32[8]{0:T(128)}, u32[]{:S(2)}) copy-start(s32[8]{0:T(128)} %param.16) | copy-start | bytes 100
  36.7 23.1 %all-to-all-start.3 = ((bf16[4,144,1152]{2,1,0:T(8,128)(2,1)}), bf16[4,144,1152]{2,1,0:T(8,128)(2,1)S(1)}, u32[]{:S(2)}, u32[]{:S(2)}) async-start(bf16[4,144,1152]{2,1,0:T(8,128)(2,1)} %shard_map.105), calls=%async_computation.3 | async-start | bytes 2654208 | tf_op jit(solution)/shard_map/all_to_all | solution.py:23
  40.4 6.9 %collective-permute-start.15 = (bf16[512,512]{1,0:T(8,128)(2,1)S(1)}, bf16[512,512]{1,0:T(8,128)(2,1)S(1)}, u32[]{:S(2)}, u32[]{:S(2)}) collective-permute-start(bf16[512,512]{1,0:T(8,128)(2,1)S(1)} %copy-done.6), channel_id=1, source_target_pairs={{0,1},{1,0},{2,3},{3,2},{4,5},{5,4},{6,7},{7,6},{8,9},{9,8},{10,11... | collective-permute-start | bytes 1572872 | tf_op jit(solution)/shard_map/ppermute | solution.py:453
  41.9 39.6 %collective-permute-start.11 = (bf16[1024,512]{1,0:T(8,128)(2,1)}, bf16[1024,512]{1,0:T(8,128)(2,1)}, u32[]{:S(2)}, u32[]{:S(2)}) collective-permute-start(bf16[1024,512]{1,0:T(8,128)(2,1)} %get-tuple-element.451.refs_8_), channel_id=1, source_target_pairs={{0,2},{2,4},{4,6},{6,0},{1,3},{3,5},{5,7},{7,1},{8,10},{10,12},{12... | collective-permute-start | bytes 3145736 | tf_op jit(solution)/shard_map/ppermute | solution.py:287
  43.6 38.0 %collective-permute-start.12 = (bf16[1024,512]{1,0:T(8,128)(2,1)}, bf16[1024,512]{1,0:T(8,128)(2,1)}, u32[]{:S(2)}, u32[]{:S(2)}) collective-permute-start(bf16[1024,512]{1,0:T(8,128)(2,1)} %get-tuple-element.451.refs_8_), channel_id=1, source_target_pairs={{0,6},{2,0},{4,2},{6,4},{1,7},{3,1},{5,3},{7,5},{8,14},{10,8},{12,... | collective-permute-start | bytes 3145736 | tf_op jit(solution)/shard_map/ppermute | solution.py:287
  45.2 36.4 %collective-permute-start.13 = (bf16[1024,512]{1,0:T(8,128)(2,1)}, bf16[1024,512]{1,0:T(8,128)(2,1)}, u32[]{:S(2)}, u32[]{:S(2)}) collective-permute-start(bf16[1024,512]{1,0:T(8,128)(2,1)} %get-tuple-element.452.refs_9_), channel_id=1, source_target_pairs={{0,8},{8,16},{16,24},{24,0},{1,9},{9,17},{17,25},{25,1},{2,10},{10... | collective-permute-start | bytes 3145736 | tf_op jit(solution)/shard_map/ppermute | solution.py:287
  47.3 0.8 copy-start.8
  48.1 33.5 %collective-permute-start.14 = (bf16[1024,512]{1,0:T(8,128)(2,1)}, bf16[1024,512]{1,0:T(8,128)(2,1)}, u32[]{:S(2)}, u32[]{:S(2)}) collective-permute-start(bf16[1024,512]{1,0:T(8,128)(2,1)} %get-tuple-element.452.refs_9_), channel_id=1, source_target_pairs={{0,24},{8,0},{16,8},{24,16},{1,25},{9,1},{17,9},{25,17},{2,26},{10... | collective-permute-start | bytes 3145736 | tf_op jit(solution)/shard_map/ppermute | solution.py:287
  49.5 1.0 copy-start.7
  50.5 1.0 copy-start.9
  59.9 1.0 copy-start.4
  62.9 1.1 copy-start.2
  64.0 26.9 %all-to-all-start.4 = ((bf16[4,144,1152]{2,1,0:T(8,128)(2,1)}), bf16[4,144,1152]{2,1,0:T(8,128)(2,1)S(1)}, u32[]{:S(2)}, u32[]{:S(2)}) async-start(bf16[4,144,1152]{2,1,0:T(8,128)(2,1)} %copy-done.2), calls=%async_computation.4 | async-start | bytes 2654208 | tf_op jit(solution)/shard_map/all_to_all | solution.py:23
  84.1 22.0 %collective-permute-start.16 = (bf16[512,512]{1,0:T(8,128)(2,1)}, bf16[512,512]{1,0:T(8,128)(2,1)}, u32[]{:S(2)}, u32[]{:S(2)}) collective-permute-start(bf16[512,512]{1,0:T(8,128)(2,1)} %get-tuple-element.461), channel_id=1, source_target_pairs={{0,2},{2,4},{4,6},{6,0},{1,3},{3,5},{5,7},{7,1},{8,10},{10,12},{12... | collective-permute-start | bytes 1572872 | tf_op jit(solution)/shard_map/ppermute | solution.py:287
  84.5 21.6 %collective-permute-start.17 = (bf16[512,512]{1,0:T(8,128)(2,1)}, bf16[512,512]{1,0:T(8,128)(2,1)}, u32[]{:S(2)}, u32[]{:S(2)}) collective-permute-start(bf16[512,512]{1,0:T(8,128)(2,1)} %get-tuple-element.462), channel_id=1, source_target_pairs={{0,6},{2,0},{4,2},{6,4},{1,7},{3,1},{5,3},{7,5},{8,14},{10,8},{12,... | collective-permute-start | bytes 1572872 | tf_op jit(solution)/shard_map/ppermute | solution.py:287
  87.5 18.6 %collective-permute-start.18 = (bf16[512,512]{1,0:T(8,128)(2,1)}, bf16[512,512]{1,0:T(8,128)(2,1)}, u32[]{:S(2)}, u32[]{:S(2)}) collective-permute-start(bf16[512,512]{1,0:T(8,128)(2,1)} %get-tuple-element.463), channel_id=1, source_target_pairs={{0,8},{8,16},{16,24},{24,0},{1,9},{9,17},{17,25},{25,1},{2,10},{10... | collective-permute-start | bytes 1572872 | tf_op jit(solution)/shard_map/ppermute | solution.py:287
  88.1 18.0 %collective-permute-start.19 = (bf16[512,512]{1,0:T(8,128)(2,1)}, bf16[512,512]{1,0:T(8,128)(2,1)}, u32[]{:S(2)}, u32[]{:S(2)}) collective-permute-start(bf16[512,512]{1,0:T(8,128)(2,1)} %get-tuple-element.464), channel_id=1, source_target_pairs={{0,24},{8,0},{16,8},{24,16},{1,25},{9,1},{17,9},{25,17},{2,26},{10... | collective-permute-start | bytes 1572872 | tf_op jit(solution)/shard_map/ppermute | solution.py:287
  91.1 0.7 copy-start.3
  91.9 14.2 %all-to-all-start.5 = ((bf16[4,304,128]{2,1,0:T(8,128)(2,1)}), bf16[4,304,128]{2,1,0:T(8,128)(2,1)S(1)}, u32[]{:S(2)}, u32[]{:S(2)}) async-start(bf16[4,304,128]{2,1,0:T(8,128)(2,1)} %copy-done.3), calls=%async_computation.5 | async-start | bytes 622592 | tf_op jit(solution)/shard_map/all_to_all | solution.py:23
  104.7 1.4 %copy-start = (f32[1024,512]{1,0:T(8,128)}, f32[1024,512]{1,0:T(8,128)S(1)}, u32[]{:S(2)}) copy-start(f32[1024,512]{1,0:T(8,128)S(1)} %shard_map.109.refs_12_) | copy-start | bytes 6291460
  106.1 1.6 %copy-start.1 = (f32[1024,512]{1,0:T(8,128)S(1)}, f32[1024,512]{1,0:T(8,128)}, u32[]{:S(2)}) copy-start(f32[1024,512]{1,0:T(8,128)} %copy-done) | copy-start | bytes 6291460
  113.5 2.0 %collective-permute-start.20 = (bf16[512,512]{1,0:T(8,128)(2,1)S(1)}, bf16[512,512]{1,0:T(8,128)(2,1)S(1)}, u32[]{:S(2)}, u32[]{:S(2)}) collective-permute-start(bf16[512,512]{1,0:T(8,128)(2,1)S(1)} %get-tuple-element.467), channel_id=1, source_target_pairs={{0,1},{1,0},{2,3},{3,2},{4,5},{5,4},{6,7},{7,6},{8,9},{9,8},{10,11... | collective-permute-start | bytes 1572872 | tf_op jit(solution)/shard_map/ppermute | solution.py:475
  115.6 1.6 %copy-start.11 = (bf16[1024,512]{1,0:T(8,128)(2,1)S(1)}, bf16[1024,512]{1,0:T(8,128)(2,1)}, u32[]{:S(2)}) copy-start(bf16[1024,512]{1,0:T(8,128)(2,1)} %refs_12_.1) | copy-start | bytes 3145732
  115.6 1.6 %copy-start.15 = (f32[512,1]{1,0:T(8,128)S(1)}, f32[512,1]{1,0:T(8,128)}, u32[]{:S(2)}) copy-start(f32[512,1]{1,0:T(8,128)} %copy-done.14) | copy-start | bytes 6148
  117.9 0.7 copy-start.10
  117.9 0.6 copy-start.13

commit v7 on v6

--- a/solution.py
+++ b/solution.py
@@ -354,7 +354,7 @@
         ),
         compiler_params=pltpu.CompilerParams(vmem_limit_bytes=22 * MIB),
         cost_estimate=pl.CostEstimate(
-            flops=4 * n_tok * rows * n * steps, bytes_accessed=8 * n_tok * rows * steps, transcendentals=0
+            flops=20 * n_tok * rows * n * steps, bytes_accessed=8 * n_tok * rows * steps, transcendentals=0
         ),
     )(where_from, *([own] * per), *([other] * per), *flat, *extra)
 
@@ -378,6 +378,7 @@
     block_a = columns(weight, me_c)
     block_b = lax.ppermute(columns(weight, 1 - me_c), "c", SWAP)
     partner_tasks = lax.ppermute(tasks, "c", SWAP)
+    other = lax.ppermute(tokens, "c", SWAP)
     block_b, partner_tasks, cotangent, counts = lax.optimization_barrier((block_b, partner_tasks, cotangent, counts))
     first_hop = [shifted(block_a, "x", k) for k in range(1, nx)] + [shifted(block_b, "z", k) for k in range(1, nz)]
     def blocks_a(step):
@@ -436,9 +437,9 @@
         return hidden, theirs, mine, note.astype(BF)
 
     hidden, theirs, mine, note = local_terms(jnp.int32(0))
-    first_hop, theirs = lax.optimization_barrier((first_hop, theirs))
+    first_hop, theirs, other = lax.optimization_barrier((first_hop, theirs, other))
     near_a, near_b = join([block_a] + first_hop[: nx - 1], [block_b] + first_hop[nx - 1 :])
-    near_a, near_b, theirs = lax.optimization_barrier((near_a, near_b, theirs))
+    near_a, near_b, theirs, other = lax.optimization_barrier((near_a, near_b, theirs, other))
     got = lax.ppermute(theirs, "c", SWAP)
     a_down, a_up = shifted(near_a, "z", 1), shifted(near_a, "z", nz - 1)
     b_down, b_up = shifted(near_b, "x", 1), shifted(near_b, "x", nx - 1)
@@ -448,8 +449,7 @@
 
     from_z = exchange(pack(mine, got, note), "z")
 
-    sent_tokens, sent_hidden, _ = lax.optimization_barrier((tokens, hidden, got))
-    other = lax.ppermute(sent_tokens, "c", SWAP)
+    sent_hidden, _ = lax.optimization_barrier((hidden, got))
     other_hidden = lax.ppermute(sent_hidden, "c", SWAP)
     acc = add_blocks(
         tokens,

time: 120 us -> 141 us (1.18)
  waiting for transfers between devices: 20.6 us -> 40.6 us
  local copies, waits for them, and re-layouts: 13.7 us -> 9.61 us
  Pallas kernels: 42.3 us -> 44.7 us
  starting transfers between devices: 37.1 us -> 39.3 us
    all_to_all x3, waiting for transfers between devices: 1.76 us -> 30.8 us  [exchange(): return lax.all_to_all(a, axis, 0, 0, tiled=True)]
    ppermute x14, waiting for transfers between devices: 13.1 us -> 0.04 us  [shifted(): return lax.ppermute(a, axis, [(i, (i + step) % n) for i in range(n)])]
    ppermute x1, waiting for transfers between devices: 0.01 us -> 6.43 us  [per_device(): partner_tasks = lax.ppermute(tasks, 'c', SWAP)]
    unnamed x36 -> x24, local copies, waits for them, and re-layouts: 9.81 us -> 5.7 us
    ppermute x14, starting transfers between devices: 24.3 us -> 27 us  [shifted(): return lax.ppermute(a, axis, [(i, (i + step) % n) for i in range(n)])]
    ppermute x1, waiting for transfers between devices: 1.52 us -> 0.01 us  [per_device(): other_hidden = lax.ppermute(sent_hidden, 'c', SWAP)]
  transfers between devices with their start and end apart: 23 -> 23, of which waited for: 5 -> 5; matrix products, arithmetic and copies ran while one was open for 4% -> 4% of each run, Pallas kernels for 30% -> 27%
where the time goes in v7:
time: 141 us; the launch traced here: 139 us
  Pallas kernels  44.7 us (32%)
  waiting for transfers between devices  40.6 us (29%)
  starting transfers between devices  39.3 us (28%)
  local copies, waits for them, and re-layouts  9.61 us (7%)
  other arithmetic  2.48 us (2%)
  between operations  1.66 us (1%)
    all_to_all x3, waiting for transfers between devices, exchange(): return lax.all_to_all(a, axis, 0, 0, tiled=True)  30.8 us
    ppermute x14, starting transfers between devices, shifted(): return lax.ppermute(a, axis, [(i, (i + step) % n) for i in range(n)])  27 us
    pallas_call x3, Pallas kernels, add_blocks(): pl.pallas_call(body, out_shape=(jax.ShapeDtypeStruct((n_tok, n), BF),) *...  22 us
    pallas_call x1, Pallas kernels, terms(): call(body, (jax.ShapeDtypeStruct((n_tok, cols), BF), jax.ShapeDtypeStruct...  13.6 us
    all_to_all x3, starting transfers between devices, exchange(): return lax.all_to_all(a, axis, 0, 0, tiled=True)  11.5 us
    ppermute x1, waiting for transfers between devices, per_device(): partner_tasks = lax.ppermute(tasks, 'c', SWAP)  6.43 us
    unnamed x24, local copies, waits for them, and re-layouts  5.7 us
    pallas_call x1, Pallas kernels, spread(): call(body, jax.ShapeDtypeStruct((ny, own + INFO, lanes), BF), (ny,), [onc...  3.03 us
  transfers between devices with their start and end apart: 23, of which 5 were waited for; matrix products, arithmetic and copies ran while one was open for 4% of the time, Pallas kernels for 27%

profile of v7, /device:TPU:0, one launch (start us, length us, event | category | flops | bytes accessed | tf_op | source)
XLA Modules:
  0.0 138.9 jit_solution(16594738735119253377)
XLA Ops:
  0.8 1.1 constant_dynamic-slice_fusion
  1.8 1.6 %collective-permute-start.1 = (bf16[256,512]{1,0:T(8,128)(2,1)S(1)}, bf16[256,512]{1,0:T(8,128)(2,1)S(1)}, u32[]{:S(2)}, u32[]{:S(2)}) collective-permute-start(bf16[256,512]{1,0:T(8,128)(2,1)S(1)} %get-tuple-element.636.refs_0_), channel_id=1, source_target_pairs={{0,8},{8,16},{16,24},{24,0},{1,9},{9,17},{17,25},{25,1},{2,10},{10... | collective-permute-start | bytes 786440 | tf_op jit(solution)/shard_map/ppermute | solution.py:287
  3.5 0.2 collective-permute-start.4
  3.7 0.3 collective-permute-start.5
  4.0 0.8 copy.24.task_col
  4.9 2.8 %collective-permute-start.2 = (bf16[256,512]{1,0:T(8,128)(2,1)S(1)}, bf16[256,512]{1,0:T(8,128)(2,1)S(1)}, u32[]{:S(2)}, u32[]{:S(2)}) collective-permute-start(bf16[256,512]{1,0:T(8,128)(2,1)S(1)} %get-tuple-element.636.refs_0_), channel_id=1, source_target_pairs={{0,16},{8,24},{16,0},{24,8},{1,17},{9,25},{17,1},{25,9},{2,18},{10... | collective-permute-start | bytes 786440 | tf_op jit(solution)/shard_map/ppermute | solution.py:287
  7.7 6.4 %collective-permute-done.5 = s32[512]{0:T(512)S(1)} collective-permute-done((s32[512]{0:T(512)}, s32[512]{0:T(512)S(1)}, u32[]{:S(2)}, u32[]{:S(2)}) %collective-permute-start.5) | collective-permute-done | bytes 2080 | tf_op jit(solution)/shard_map/ppermute | solution.py:380
  14.1 2.8 %collective-permute-start.3 = (bf16[256,512]{1,0:T(8,128)(2,1)S(1)}, bf16[256,512]{1,0:T(8,128)(2,1)S(1)}, u32[]{:S(2)}, u32[]{:S(2)}) collective-permute-start(bf16[256,512]{1,0:T(8,128)(2,1)S(1)} %get-tuple-element.636.refs_0_), channel_id=1, source_target_pairs={{0,24},{8,0},{16,8},{24,16},{1,25},{9,1},{17,9},{25,17},{2,26},{10... | collective-permute-start | bytes 786440 | tf_op jit(solution)/shard_map/ppermute | solution.py:287
  17.0 0.1 fusion.46
  17.1 0.1 convert_reduce_fusion.1
  17.4 0.1 copy.25.tw
  17.8 2.0 %collective-permute-start.6 = (bf16[256,512]{1,0:T(8,128)(2,1)S(1)}, bf16[256,512]{1,0:T(8,128)(2,1)S(1)}, u32[]{:S(2)}, u32[]{:S(2)}) collective-permute-start(bf16[256,512]{1,0:T(8,128)(2,1)S(1)} %collective-permute-done.4.refs_4_), channel_id=1, source_target_pairs={{0,2},{2,4},{4,6},{6,0},{1,3},{3,5},{5,7},{7,1},{8,10},{10,12},{12... | collective-permute-start | bytes 786440 | tf_op jit(solution)/shard_map/ppermute | solution.py:287
  19.8 3.6 %collective-permute-start.7 = (bf16[256,512]{1,0:T(8,128)(2,1)S(1)}, bf16[256,512]{1,0:T(8,128)(2,1)S(1)}, u32[]{:S(2)}, u32[]{:S(2)}) collective-permute-start(bf16[256,512]{1,0:T(8,128)(2,1)S(1)} %collective-permute-done.4.refs_4_), channel_id=1, source_target_pairs={{0,4},{2,6},{4,0},{6,2},{1,5},{3,7},{5,1},{7,3},{8,12},{10,14},{12... | collective-permute-start | bytes 786440 | tf_op jit(solution)/shard_map/ppermute | solution.py:287
  23.4 1.0 collective-permute-start.8
  24.4 13.6 %shard_map.103 = (bf16[512,512]{1,0:T(8,128)(2,1)}, bf16[4,128,1152]{2,1,0:T(8,128)(2,1)}, bf16[4,128,1152]{2,1,0:T(8,128)(2,1)S(1)}) custom-call(s32[1]{0:T(128)} %bitcast.16.me, bf16[512,8192]{1,0:T(8,128)(2,1)} %refs_3_.5, bf16[8192,512]{1,0:T(8,128)(2,1)} %dn.1, bf16[1024,512]{1,0:T(8,128)(2,1)} %refs_12_.1, bf16[512,1024]{1,0:T(8,128)(2,1)} %cot, ...), custom_call_target="tpu_custom_call" | custom-call | flops 5368709120 | bytes 25165824 | tf_op jit(solution)/shard_map/pallas_call | solution.py:103
  38.1 1.5 %shard_map.104 = (bf16[1024,512]{1,0:T(8,128)(2,1)}, bf16[1024,512]{1,0:T(8,128)(2,1)}) custom-call(bf16[256,512]{1,0:T(8,128)(2,1)S(1)} %get-tuple-element.636.refs_0_, bf16[256,512]{1,0:T(8,128)(2,1)S(1)} %collective-permute-done.1.refs_1_, bf16[256,512]{1,0:T(8,128)(2,1)S(1)} %collective-permute-done.2.refs_2_, ...), custom_call_target="tpu_custom_call" | custom-call | bytes 4194304 | tf_op jit(solution)/shard_map/pallas_call | solution.py:153
  39.6 0.9 broadcast_in_dim_reshape.8.ow
  40.6 1.9 %collective-permute-done.14.b = bf16[4,128,1152]{2,1,0:T(8,128)(2,1)S(1)} collective-permute-done((bf16[4,128,1152]{2,1,0:T(8,128)(2,1)}, bf16[4,128,1152]{2,1,0:T(8,128)(2,1)S(1)}, u32[]{:S(2)}, u32[]{:S(2)}) %collective-permute-start.14) | collective-permute-done | bytes 1179680 | tf_op jit(solution)/shard_map/ppermute | solution.py:443
  42.6 0.1 collective-permute-start.15
  42.7 0.6 convert_reduce_fusion.2
  44.1 1.1 collective-permute-start.10
  45.2 2.2 %collective-permute-start.11 = (bf16[1024,512]{1,0:T(8,128)(2,1)}, bf16[1024,512]{1,0:T(8,128)(2,1)}, u32[]{:S(2)}, u32[]{:S(2)}) collective-permute-start(bf16[1024,512]{1,0:T(8,128)(2,1)} %get-tuple-element.451.refs_8_), channel_id=1, source_target_pairs={{0,6},{2,0},{4,2},{6,4},{1,7},{3,1},{5,3},{7,5},{8,14},{10,8},{12,... | collective-permute-start | bytes 3145736 | tf_op jit(solution)/shard_map/ppermute | solution.py:287
  47.4 1.7 %shard_map.105 = bf16[4,144,1152]{2,1,0:T(8,128)(2,1)} custom-call(bf16[4,128,1152]{2,1,0:T(8,128)(2,1)S(1)} %get-tuple-element.453.a, bf16[4,128,1152]{2,1,0:T(8,128)(2,1)S(1)} %collective-permute-done.14.b, bf16[16,1152]{1,0:T(8,128)(2,1)S(1)} %select_convert_fusion.1.c), custom_call_target="tpu_custom_call" | custom-call | bytes 10485760 | tf_op jit(solution)/shard_map/pallas_call | solution.py:190
  49.2 3.2 %collective-permute-start.13 = (bf16[1024,512]{1,0:T(8,128)(2,1)}, bf16[1024,512]{1,0:T(8,128)(2,1)}, u32[]{:S(2)}, u32[]{:S(2)}) collective-permute-start(bf16[1024,512]{1,0:T(8,128)(2,1)} %get-tuple-element.452.refs_9_), channel_id=1, source_target_pairs={{0,24},{8,0},{16,8},{24,16},{1,25},{9,1},{17,9},{25,17},{2,26},{10... | collective-permute-start | bytes 3145736 | tf_op jit(solution)/shard_map/ppermute | solution.py:287
  52.4 3.5 %all-to-all-start.3 = ((bf16[4,144,1152]{2,1,0:T(8,128)(2,1)}), bf16[4,144,1152]{2,1,0:T(8,128)(2,1)S(1)}, u32[]{:S(2)}, u32[]{:S(2)}) async-start(bf16[4,144,1152]{2,1,0:T(8,128)(2,1)} %shard_map.105), calls=%async_computation.3 | async-start | bytes 2654208 | tf_op jit(solution)/shard_map/all_to_all | solution.py:23
  55.9 6.9 %shard_map.106.refs_12_ = f32[1024,512]{1,0:T(8,128)S(1)} custom-call(s32[9]{0:T(128)S(1)} %stack.131.at, bf16[512,8192]{1,0:T(8,128)(2,1)} %refs_3_.5, bf16[512,8192]{1,0:T(8,128)(2,1)} %refs_3_.5, bf16[512,8192]{1,0:T(8,128)(2,1)} %refs_3_.5, bf16[512,8192]{1,0:T(8,128)(2,1)} %refs_3_.5, ...), custom_call_target="tpu_custom_call" | custom-call | flops 10737418240 | bytes 8388608 | tf_op jit(solution)/shard_map/pallas_call | solution.py:345
  62.8 22.4 %all-to-all-done.3.g = bf16[4,144,1152]{2,1,0:T(8,128)(2,1)S(1)} async-done(((bf16[4,144,1152]{2,1,0:T(8,128)(2,1)}), bf16[4,144,1152]{2,1,0:T(8,128)(2,1)S(1)}, u32[]{:S(2)}, u32[]{:S(2)}) %all-to-all-start.3) | async-done | bytes 1327136 | tf_op jit(solution)/shard_map/all_to_all | solution.py:23
  85.2 0.9 copy-done.3
  86.2 3.0 %shard_map.107 = bf16[4,144,1152]{2,1,0:T(8,128)(2,1)} custom-call(bf16[4,144,1152]{2,1,0:T(8,128)(2,1)S(1)} %all-to-all-done.3.g, f32[512,1]{1,0:T(8,128)S(1)} %copy-done.3), custom_call_target="tpu_custom_call" | custom-call | flops 603979776 | bytes 5242880 | tf_op jit(solution)/shard_map/pallas_call | solution.py:222
  89.2 4.5 %all-to-all-start.4 = ((bf16[4,144,1152]{2,1,0:T(8,128)(2,1)}), bf16[4,144,1152]{2,1,0:T(8,128)(2,1)S(1)}, u32[]{:S(2)}, u32[]{:S(2)}) async-start(bf16[4,144,1152]{2,1,0:T(8,128)(2,1)} %shard_map.107), calls=%async_computation.4 | async-start | bytes 2654208 | tf_op jit(solution)/shard_map/all_to_all | solution.py:23
  93.9 2.6 %shard_map.111 = (bf16[512,512]{1,0:T(8,128)(2,1)}, bf16[512,512]{1,0:T(8,128)(2,1)}, bf16[512,512]{1,0:T(8,128)(2,1)}, bf16[512,512]{1,0:T(8,128)(2,1)}) custom-call(bf16[1024,512]{1,0:T(8,128)(2,1)} %collective-permute-done.10.refs_8_.refs_0_, bf16[1024,512]{1,0:T(8,128)(2,1)} %collective-permute-done.11.refs_9_.refs_1_, ...), custom_call_target="tpu_custom_call" | custom-call | bytes 4194304 | tf_op jit(solution)/shard_map/pallas_call | solution.py:172
  96.5 1.0 collective-permute-start.16
  97.5 2.3 %collective-permute-start.17 = (bf16[512,512]{1,0:T(8,128)(2,1)}, bf16[512,512]{1,0:T(8,128)(2,1)}, u32[]{:S(2)}, u32[]{:S(2)}) collective-permute-start(bf16[512,512]{1,0:T(8,128)(2,1)} %get-tuple-element.464), channel_id=1, source_target_pairs={{0,6},{2,0},{4,2},{6,4},{1,7},{3,1},{5,3},{7,5},{8,14},{10,8},{12,... | collective-permute-start | bytes 1572872 | tf_op jit(solution)/shard_map/ppermute | solution.py:287
  99.9 3.2 %collective-permute-start.19 = (bf16[512,512]{1,0:T(8,128)(2,1)}, bf16[512,512]{1,0:T(8,128)(2,1)}, u32[]{:S(2)}, u32[]{:S(2)}) collective-permute-start(bf16[512,512]{1,0:T(8,128)(2,1)} %get-tuple-element.466), channel_id=1, source_target_pairs={{0,24},{8,0},{16,8},{24,16},{1,25},{9,1},{17,9},{25,17},{2,26},{10... | collective-permute-start | bytes 1572872 | tf_op jit(solution)/shard_map/ppermute | solution.py:287
  103.1 8.4 %all-to-all-done.4.g = bf16[4,144,1152]{2,1,0:T(8,128)(2,1)S(1)} async-done(((bf16[4,144,1152]{2,1,0:T(8,128)(2,1)}), bf16[4,144,1152]{2,1,0:T(8,128)(2,1)S(1)}, u32[]{:S(2)}, u32[]{:S(2)}) %all-to-all-start.4) | async-done | bytes 1327136 | tf_op jit(solution)/shard_map/all_to_all | solution.py:23
  111.5 0.2 shard_map.108
  111.7 0.7 copy-done.2
  112.4 3.5 %all-to-all-start.5 = ((bf16[4,304,128]{2,1,0:T(8,128)(2,1)}), bf16[4,304,128]{2,1,0:T(8,128)(2,1)S(1)}, u32[]{:S(2)}, u32[]{:S(2)}) async-start(bf16[4,304,128]{2,1,0:T(8,128)(2,1)} %copy-done.2), calls=%async_computation.5 | async-start | bytes 622592 | tf_op jit(solution)/shard_map/all_to_all | solution.py:23
  115.9 9.3 %shard_map.109.refs_12_ = f32[1024,512]{1,0:T(8,128)S(1)} custom-call(s32[16]{0:T(128)S(1)} %stack.122.at, bf16[512,8192]{1,0:T(8,128)(2,1)} %refs_3_.5, bf16[512,8192]{1,0:T(8,128)(2,1)} %refs_3_.5, bf16[512,8192]{1,0:T(8,128)(2,1)} %refs_3_.5, bf16[512,8192]{1,0:T(8,128)(2,1)} %refs_3_.5, ...), custom_call_target="tpu_custom_call" | custom-call | flops 21474836480 | bytes 16777216 | tf_op jit(solution)/shard_map/pallas_call | solution.py:345
  125.2 1.3 copy-done
  126.6 1.6 %copy-done.1 = f32[1024,512]{1,0:T(8,128)S(1)} copy-done((f32[1024,512]{1,0:T(8,128)S(1)}, f32[1024,512]{1,0:T(8,128)}, u32[]{:S(2)}) %copy-start.1) | copy-done | bytes 2097176
  128.2 5.8 %shard_map.112 = (bf16[512,512]{1,0:T(8,128)(2,1)S(1)}, bf16[512,512]{1,0:T(8,128)(2,1)S(1)}) custom-call(s32[8]{0:T(128)S(1)} %stack.140.at, bf16[512,8192]{1,0:T(8,128)(2,1)} %refs_3_.5, bf16[512,8192]{1,0:T(8,128)(2,1)} %refs_3_.5, bf16[512,8192]{1,0:T(8,128)(2,1)} %refs_3_.5, bf16[512,8192]{1,0:T(8,128)(2,1)} %refs_3_.5, ...), custom_call_target="tpu_custom_call" | custom-call | flops 10737418240 | bytes 8388608 | tf_op jit(solution)/shard_map/pallas_call | solution.py:345
  134.1 0.5 slice.11
  134.6 1.4 %collective-permute-done.20 = bf16[512,512]{1,0:T(8,128)(2,1)S(1)} collective-permute-done((bf16[512,512]{1,0:T(8,128)(2,1)S(1)}, bf16[512,512]{1,0:T(8,128)(2,1)S(1)}, u32[]{:S(2)}, u32[]{:S(2)}) %collective-permute-start.20) | collective-permute-done | bytes 524320 | tf_op jit(solution)/shard_map/ppermute | solution.py:475
  136.1 1.1 pad_maximum_fusion
  137.2 0.4 copy-done.5
  137.7 0.6 while.20
  138.3 0.6 copy-done.4
  (63 shorter events, 1.4 us)
Async XLA Ops:
  0.6 16.3 %copy-start.10 = (s32[512]{0:T(512)S(1)}, s32[512]{0:T(512)}, u32[]{:S(2)}) copy-start(s32[512]{0:T(512)} %param.15) | copy-start | bytes 6148
  0.6 16.3 %copy-start.11 = (s32[8]{0:T(128)S(1)}, s32[8]{0:T(128)}, u32[]{:S(2)}) copy-start(s32[8]{0:T(128)} %param.17) | copy-start | bytes 100
  0.7 37.4 %collective-permute-start.9 = (bf16[512,8192]{1,0:T(8,128)(2,1)}, bf16[512,8192]{1,0:T(8,128)(2,1)}, u32[]{:S(2)}, u32[]{:S(2)}) collective-permute-start(bf16[512,8192]{1,0:T(8,128)(2,1)} %refs_3_.5), channel_id=1, source_target_pairs={{0,1},{1,0},{2,3},{3,2},{4,5},{5,4},{6,7},{7,6},{8,9},{9,8},{10,11... | collective-permute-start | bytes 25165832 | tf_op jit(solution)/shard_map/ppermute | solution.py:381
  1.8 17.9 %collective-permute-start.1 = (bf16[256,512]{1,0:T(8,128)(2,1)S(1)}, bf16[256,512]{1,0:T(8,128)(2,1)S(1)}, u32[]{:S(2)}, u32[]{:S(2)}) collective-permute-start(bf16[256,512]{1,0:T(8,128)(2,1)S(1)} %get-tuple-element.636.refs_0_), channel_id=1, source_target_pairs={{0,8},{8,16},{16,24},{24,0},{1,9},{9,17},{17,25},{25,1},{2,10},{10... | collective-permute-start | bytes 786440 | tf_op jit(solution)/shard_map/ppermute | solution.py:287
  3.5 13.5 %collective-permute-start.4 = (bf16[256,512]{1,0:T(8,128)(2,1)S(1)}, bf16[256,512]{1,0:T(8,128)(2,1)S(1)}, u32[]{:S(2)}, u32[]{:S(2)}) collective-permute-start(bf16[256,512]{1,0:T(8,128)(2,1)S(1)} %get-tuple-element.635), channel_id=1, source_target_pairs={{0,1},{1,0},{2,3},{3,2},{4,5},{5,4},{6,7},{7,6},{8,9},{9,8},{10,11... | collective-permute-start | bytes 786440 | tf_op jit(solution)/shard_map/ppermute | solution.py:379
  3.7 10.4 %collective-permute-start.5 = (s32[512]{0:T(512)}, s32[512]{0:T(512)S(1)}, u32[]{:S(2)}, u32[]{:S(2)}) collective-permute-start(s32[512]{0:T(512)} %param.15), channel_id=1, source_target_pairs={{0,1},{1,0},{2,3},{3,2},{4,5},{5,4},{6,7},{7,6},{8,9},{9,8},{10,11... | collective-permute-start | bytes 6152 | tf_op jit(solution)/shard_map/ppermute | solution.py:380
  4.9 18.5 %collective-permute-start.2 = (bf16[256,512]{1,0:T(8,128)(2,1)S(1)}, bf16[256,512]{1,0:T(8,128)(2,1)S(1)}, u32[]{:S(2)}, u32[]{:S(2)}) collective-permute-start(bf16[256,512]{1,0:T(8,128)(2,1)S(1)} %get-tuple-element.636.refs_0_), channel_id=1, source_target_pairs={{0,16},{8,24},{16,0},{24,8},{1,17},{9,25},{17,1},{25,9},{2,18},{10... | collective-permute-start | bytes 786440 | tf_op jit(solution)/shard_map/ppermute | solution.py:287
  14.1 23.9 %collective-permute-start.3 = (bf16[256,512]{1,0:T(8,128)(2,1)S(1)}, bf16[256,512]{1,0:T(8,128)(2,1)S(1)}, u32[]{:S(2)}, u32[]{:S(2)}) collective-permute-start(bf16[256,512]{1,0:T(8,128)(2,1)S(1)} %get-tuple-element.636.refs_0_), channel_id=1, source_target_pairs={{0,24},{8,0},{16,8},{24,16},{1,25},{9,1},{17,9},{25,17},{2,26},{10... | collective-permute-start | bytes 786440 | tf_op jit(solution)/shard_map/ppermute | solution.py:287
  17.5 20.5 %copy-start.8 = (f32[512,1]{1,0:T(8,128)}, f32[512,1]{1,0:T(8,128)S(1)}, u32[]{:S(2)}) copy-start(f32[512,1]{1,0:T(8,128)S(1)} %copy.25.tw) | copy-start | bytes 6148
  17.8 20.3 %collective-permute-start.6 = (bf16[256,512]{1,0:T(8,128)(2,1)S(1)}, bf16[256,512]{1,0:T(8,128)(2,1)S(1)}, u32[]{:S(2)}, u32[]{:S(2)}) collective-permute-start(bf16[256,512]{1,0:T(8,128)(2,1)S(1)} %collective-permute-done.4.refs_4_), channel_id=1, source_target_pairs={{0,2},{2,4},{4,6},{6,0},{1,3},{3,5},{5,7},{7,1},{8,10},{10,12},{12... | collective-permute-start | bytes 786440 | tf_op jit(solution)/shard_map/ppermute | solution.py:287
  19.8 18.3 %collective-permute-start.7 = (bf16[256,512]{1,0:T(8,128)(2,1)S(1)}, bf16[256,512]{1,0:T(8,128)(2,1)S(1)}, u32[]{:S(2)}, u32[]{:S(2)}) collective-permute-start(bf16[256,512]{1,0:T(8,128)(2,1)S(1)} %collective-permute-done.4.refs_4_), channel_id=1, source_target_pairs={{0,4},{2,6},{4,0},{6,2},{1,5},{3,7},{5,1},{7,3},{8,12},{10,14},{12... | collective-permute-start | bytes 786440 | tf_op jit(solution)/shard_map/ppermute | solution.py:287
  23.4 14.7 %collective-permute-start.8 = (bf16[256,512]{1,0:T(8,128)(2,1)S(1)}, bf16[256,512]{1,0:T(8,128)(2,1)S(1)}, u32[]{:S(2)}, u32[]{:S(2)}) collective-permute-start(bf16[256,512]{1,0:T(8,128)(2,1)S(1)} %collective-permute-done.4.refs_4_), channel_id=1, source_target_pairs={{0,6},{2,0},{4,2},{6,4},{1,7},{3,1},{5,3},{7,5},{8,14},{10,8},{12,... | collective-permute-start | bytes 786440 | tf_op jit(solution)/shard_map/ppermute | solution.py:287
  38.0 1.5 %copy-start.12 = (s32[8]{0:T(128)S(1)}, s32[8]{0:T(128)}, u32[]{:S(2)}) copy-start(s32[8]{0:T(128)} %param.16) | copy-start | bytes 100
  39.5 3.1 %collective-permute-start.14 = (bf16[4,128,1152]{2,1,0:T(8,128)(2,1)}, bf16[4,128,1152]{2,1,0:T(8,128)(2,1)S(1)}, u32[]{:S(2)}, u32[]{:S(2)}) collective-permute-start(bf16[4,128,1152]{2,1,0:T(8,128)(2,1)} %get-tuple-element.454), channel_id=1, source_target_pairs={{0,1},{1,0},{2,3},{3,2},{4,5},{5,4},{6,7},{7,6},{8,9},{9,8},{10,11... | collective-permute-start | bytes 3538952 | tf_op jit(solution)/shard_map/ppermute | solution.py:443
  42.6 13.3 %collective-permute-start.15 = (bf16[512,512]{1,0:T(8,128)(2,1)}, bf16[512,512]{1,0:T(8,128)(2,1)}, u32[]{:S(2)}, u32[]{:S(2)}) collective-permute-start(bf16[512,512]{1,0:T(8,128)(2,1)} %get-tuple-element.456.refs_10_), channel_id=1, source_target_pairs={{0,1},{1,0},{2,3},{3,2},{4,5},{5,4},{6,7},{7,6},{8,9},{9,8},{10,11... | collective-permute-start | bytes 1572872 | tf_op jit(solution)/shard_map/ppermute | solution.py:453
  44.1 49.8 %collective-permute-start.10 = (bf16[1024,512]{1,0:T(8,128)(2,1)}, bf16[1024,512]{1,0:T(8,128)(2,1)}, u32[]{:S(2)}, u32[]{:S(2)}) collective-permute-start(bf16[1024,512]{1,0:T(8,128)(2,1)} %get-tuple-element.451.refs_8_), channel_id=1, source_target_pairs={{0,2},{2,4},{4,6},{6,0},{1,3},{3,5},{5,7},{7,1},{8,10},{10,12},{12... | collective-permute-start | bytes 3145736 | tf_op jit(solution)/shard_map/ppermute | solution.py:287
  45.2 48.7 %collective-permute-start.11 = (bf16[1024,512]{1,0:T(8,128)(2,1)}, bf16[1024,512]{1,0:T(8,128)(2,1)}, u32[]{:S(2)}, u32[]{:S(2)}) collective-permute-start(bf16[1024,512]{1,0:T(8,128)(2,1)} %get-tuple-element.451.refs_8_), channel_id=1, source_target_pairs={{0,6},{2,0},{4,2},{6,4},{1,7},{3,1},{5,3},{7,5},{8,14},{10,8},{12,... | collective-permute-start | bytes 3145736 | tf_op jit(solution)/shard_map/ppermute | solution.py:287
  47.4 46.5 %collective-permute-start.12 = (bf16[1024,512]{1,0:T(8,128)(2,1)}, bf16[1024,512]{1,0:T(8,128)(2,1)}, u32[]{:S(2)}, u32[]{:S(2)}) collective-permute-start(bf16[1024,512]{1,0:T(8,128)(2,1)} %get-tuple-element.452.refs_9_), channel_id=1, source_target_pairs={{0,8},{8,16},{16,24},{24,0},{1,9},{9,17},{17,25},{25,1},{2,10},{10... | collective-permute-start | bytes 3145736 | tf_op jit(solution)/shard_map/ppermute | solution.py:287
  49.2 44.8 %collective-permute-start.13 = (bf16[1024,512]{1,0:T(8,128)(2,1)}, bf16[1024,512]{1,0:T(8,128)(2,1)}, u32[]{:S(2)}, u32[]{:S(2)}) collective-permute-start(bf16[1024,512]{1,0:T(8,128)(2,1)} %get-tuple-element.452.refs_9_), channel_id=1, source_target_pairs={{0,24},{8,0},{16,8},{24,16},{1,25},{9,1},{17,9},{25,17},{2,26},{10... | collective-permute-start | bytes 3145736 | tf_op jit(solution)/shard_map/ppermute | solution.py:287
  52.4 32.9 %all-to-all-start.3 = ((bf16[4,144,1152]{2,1,0:T(8,128)(2,1)}), bf16[4,144,1152]{2,1,0:T(8,128)(2,1)S(1)}, u32[]{:S(2)}, u32[]{:S(2)}) async-start(bf16[4,144,1152]{2,1,0:T(8,128)(2,1)} %shard_map.105), calls=%async_computation.3 | async-start | bytes 2654208 | tf_op jit(solution)/shard_map/all_to_all | solution.py:23
  85.2 1.0 copy-start.3
  89.2 22.3 %all-to-all-start.4 = ((bf16[4,144,1152]{2,1,0:T(8,128)(2,1)}), bf16[4,144,1152]{2,1,0:T(8,128)(2,1)S(1)}, u32[]{:S(2)}, u32[]{:S(2)}) async-start(bf16[4,144,1152]{2,1,0:T(8,128)(2,1)} %shard_map.107), calls=%async_computation.4 | async-start | bytes 2654208 | tf_op jit(solution)/shard_map/all_to_all | solution.py:23
  96.5 30.0 %collective-permute-start.16 = (bf16[512,512]{1,0:T(8,128)(2,1)}, bf16[512,512]{1,0:T(8,128)(2,1)}, u32[]{:S(2)}, u32[]{:S(2)}) collective-permute-start(bf16[512,512]{1,0:T(8,128)(2,1)} %get-tuple-element.463), channel_id=1, source_target_pairs={{0,2},{2,4},{4,6},{6,0},{1,3},{3,5},{5,7},{7,1},{8,10},{10,12},{12... | collective-permute-start | bytes 1572872 | tf_op jit(solution)/shard_map/ppermute | solution.py:287
  97.5 29.0 %collective-permute-start.17 = (bf16[512,512]{1,0:T(8,128)(2,1)}, bf16[512,512]{1,0:T(8,128)(2,1)}, u32[]{:S(2)}, u32[]{:S(2)}) collective-permute-start(bf16[512,512]{1,0:T(8,128)(2,1)} %get-tuple-element.464), channel_id=1, source_target_pairs={{0,6},{2,0},{4,2},{6,4},{1,7},{3,1},{5,3},{7,5},{8,14},{10,8},{12,... | collective-permute-start | bytes 1572872 | tf_op jit(solution)/shard_map/ppermute | solution.py:287
  99.9 26.7 %collective-permute-start.18 = (bf16[512,512]{1,0:T(8,128)(2,1)}, bf16[512,512]{1,0:T(8,128)(2,1)}, u32[]{:S(2)}, u32[]{:S(2)}) collective-permute-start(bf16[512,512]{1,0:T(8,128)(2,1)} %get-tuple-element.465), channel_id=1, source_target_pairs={{0,8},{8,16},{16,24},{24,0},{1,9},{9,17},{17,25},{25,1},{2,10},{10... | collective-permute-start | bytes 1572872 | tf_op jit(solution)/shard_map/ppermute | solution.py:287
  99.9 26.7 %collective-permute-start.19 = (bf16[512,512]{1,0:T(8,128)(2,1)}, bf16[512,512]{1,0:T(8,128)(2,1)}, u32[]{:S(2)}, u32[]{:S(2)}) collective-permute-start(bf16[512,512]{1,0:T(8,128)(2,1)} %get-tuple-element.466), channel_id=1, source_target_pairs={{0,24},{8,0},{16,8},{24,16},{1,25},{9,1},{17,9},{25,17},{2,26},{10... | collective-permute-start | bytes 1572872 | tf_op jit(solution)/shard_map/ppermute | solution.py:287
  111.7 0.7 copy-start.2
  112.4 14.1 %all-to-all-start.5 = ((bf16[4,304,128]{2,1,0:T(8,128)(2,1)}), bf16[4,304,128]{2,1,0:T(8,128)(2,1)S(1)}, u32[]{:S(2)}, u32[]{:S(2)}) async-start(bf16[4,304,128]{2,1,0:T(8,128)(2,1)} %copy-done.2), calls=%async_computation.5 | async-start | bytes 622592 | tf_op jit(solution)/shard_map/all_to_all | solution.py:23
  125.2 1.3 copy-start
  126.6 1.6 %copy-start.1 = (f32[1024,512]{1,0:T(8,128)S(1)}, f32[1024,512]{1,0:T(8,128)}, u32[]{:S(2)}) copy-start(f32[1024,512]{1,0:T(8,128)} %copy-done) | copy-start | bytes 6291460
  134.0 2.0 %collective-permute-start.20 = (bf16[512,512]{1,0:T(8,128)(2,1)S(1)}, bf16[512,512]{1,0:T(8,128)(2,1)S(1)}, u32[]{:S(2)}, u32[]{:S(2)}) collective-permute-start(bf16[512,512]{1,0:T(8,128)(2,1)S(1)} %get-tuple-element.469), channel_id=1, source_target_pairs={{0,1},{1,0},{2,3},{3,2},{4,5},{5,4},{6,7},{7,6},{8,9},{9,8},{10,11... | collective-permute-start | bytes 1572872 | tf_op jit(solution)/shard_map/ppermute | solution.py:475
  136.1 1.5 %copy-start.5 = (bf16[1024,512]{1,0:T(8,128)(2,1)S(1)}, bf16[1024,512]{1,0:T(8,128)(2,1)}, u32[]{:S(2)}) copy-start(bf16[1024,512]{1,0:T(8,128)(2,1)} %refs_12_.1) | copy-start | bytes 3145732
  136.1 1.6 %copy-start.9 = (f32[512,1]{1,0:T(8,128)S(1)}, f32[512,1]{1,0:T(8,128)}, u32[]{:S(2)}) copy-start(f32[512,1]{1,0:T(8,128)} %copy-done.8) | copy-start | bytes 6148
  138.3 0.7 copy-start.4
  138.3 0.6 copy-start.7

commit v8 on v6

--- a/solution.py
+++ b/solution.py
@@ -438,19 +438,17 @@
     hidden, theirs, mine, note = local_terms(jnp.int32(0))
     first_hop, theirs = lax.optimization_barrier((first_hop, theirs))
     near_a, near_b = join([block_a] + first_hop[: nx - 1], [block_b] + first_hop[nx - 1 :])
-    near_a, near_b, theirs = lax.optimization_barrier((near_a, near_b, theirs))
+    near_a, near_b, theirs, sent_hidden = lax.optimization_barrier((near_a, near_b, theirs, hidden))
     got = lax.ppermute(theirs, "c", SWAP)
+    other_hidden = lax.ppermute(sent_hidden, "c", SWAP)
+    chip = pack(mine, got, note)
+    sent_tokens, _ = lax.optimization_barrier((tokens, got))
+    other = lax.ppermute(sent_tokens, "c", SWAP)
+    near_a, other, _ = lax.optimization_barrier((near_a, other, chip))
     a_down, a_up = shifted(near_a, "z", 1), shifted(near_a, "z", nz - 1)
     b_down, b_up = shifted(near_b, "x", 1), shifted(near_b, "x", nx - 1)
-    pass_on = halves([a_down, a_up, b_down, b_up], [0, 1, 0, 1])
-    a_far = [shifted(pass_on[0], "z", 1), shifted(pass_on[1], "z", nz - 1)]
-    b_far = [shifted(pass_on[2], "x", 1), shifted(pass_on[3], "x", nx - 1)]
-
-    from_z = exchange(pack(mine, got, note), "z")
-
-    sent_tokens, sent_hidden, _ = lax.optimization_barrier((tokens, hidden, got))
-    other = lax.ppermute(sent_tokens, "c", SWAP)
-    other_hidden = lax.ppermute(sent_hidden, "c", SWAP)
+    from_z = exchange(chip, "z")
+
     acc = add_blocks(
         tokens,
         other,
@@ -459,19 +457,21 @@
         lora=(hidden, other_hidden, up),
     )
     from_z, acc = lax.optimization_barrier((from_z, acc))
+    b_down, b_up, _ = lax.optimization_barrier((b_down, b_up, from_z))
     from_y = exchange(spread(from_z, owned_col, ny), "y")
+    b_pass = halves([b_down, b_up], [0, 1])
+    b_far = [shifted(b_pass[0], "x", 1), shifted(b_pass[1], "x", nx - 1)]
+    acc = add_blocks(tokens, other, [[b_down], [b_up]], at(blocks_b(-1), blocks_b(1)), before=acc)
+    a_down, a_up, acc = lax.optimization_barrier((a_down, a_up, acc))
+    a_pass = halves([a_down, a_up], [0, 1])
+    a_far = [shifted(a_pass[0], "z", 1), shifted(a_pass[1], "z", nz - 1)]
     by_x = turn(from_y, nx, d_rows)
     by_x, acc = lax.optimization_barrier((by_x, acc))
-    grad_down, grad_up, flags = finish(exchange(by_x, "x"), d_rows)
-    acc = add_blocks(
-        tokens,
-        other,
-        [[a_down], [a_up], [b_down], [b_up]],
-        at(blocks_a(-1), blocks_a(1), blocks_b(-1), blocks_b(1)),
-        before=acc,
-    )
-    acc, flags = lax.optimization_barrier((acc, flags))
+    from_x = exchange(by_x, "x")
+    acc = add_blocks(tokens, other, [[a_down], [a_up]], at(blocks_a(-1), blocks_a(1)), before=acc)
+    acc, from_x = lax.optimization_barrier((acc, from_x))
     tile, sent = add_blocks(tokens, other, [a_far, b_far], at(blocks_a(2), blocks_b(2)), before=acc, final=True)
+    grad_down, grad_up, flags = finish(from_x, d_rows)
     back = lax.ppermute(sent, "c", SWAP)
     keys = jnp.concatenate([jnp.where(me_c == 0, tile, back), jnp.where(me_c == 0, back, tile)], axis=1)
 

time: 120 us -> 117 us (0.975)
  waiting for transfers between devices: 20.6 us -> 15.2 us
  Pallas kernels: 42.3 us -> 46.2 us
    ppermute x14, waiting for transfers between devices: 13.1 us -> 5.64 us  [shifted(): return lax.ppermute(a, axis, [(i, (i + step) % n) for i in range(n)])]
    pallas_call x3 -> x4, Pallas kernels: 21.6 us -> 24 us  [add_blocks(): pl.pallas_call(body, out_shape=(jax.ShapeDtypeStruct((n_tok, n), BF),) *...]
    all_to_all x3, waiting for transfers between devices: 1.76 us -> 3.85 us  [exchange(): return lax.all_to_all(a, axis, 0, 0, tiled=True)]
    ppermute x1, waiting for transfers between devices: 1.52 us -> 0.01 us  [per_device(): other_hidden = lax.ppermute(sent_hidden, 'c', SWAP)]
    pallas_call x1 -> x2, Pallas kernels: 2.58 us -> 4.09 us  [halves(): call(body, tuple((jax.ShapeDtypeStruct((rows // 2, lanes), BF) for _ in a...]
    ppermute x1, waiting for transfers between devices: 0.01 us -> 1.49 us  [per_device(): other = lax.ppermute(sent_tokens, 'c', SWAP)]
    all_to_all x3, starting transfers between devices: 11.6 us -> 12.9 us  [exchange(): return lax.all_to_all(a, axis, 0, 0, tiled=True)]
    ppermute x14, starting transfers between devices: 24.3 us -> 23 us  [shifted(): return lax.ppermute(a, axis, [(i, (i + step) % n) for i in range(n)])]
  transfers between devices with their start and end apart: 23 -> 23, of which waited for: 5 -> 6; matrix products, arithmetic and copies ran while one was open for 4% -> 4% of each run, Pallas kernels for 30% -> 34%
where the time goes in v8:
time: 117 us; the launch traced here: 116 us
  Pallas kernels  46.2 us (39%)
  starting transfers between devices  36.7 us (31%)
  waiting for transfers between devices  15.2 us (13%)
  local copies, waits for them, and re-layouts  12.9 us (11%)
  other arithmetic  2.46 us (2%)
  between operations  1.75 us (1%)
    pallas_call x4, Pallas kernels, add_blocks(): pl.pallas_call(body, out_shape=(jax.ShapeDtypeStruct((n_tok, n), BF),) *...  24 us
    ppermute x14, starting transfers between devices, shifted(): return lax.ppermute(a, axis, [(i, (i + step) % n) for i in range(n)])  23 us
    all_to_all x3, starting transfers between devices, exchange(): return lax.all_to_all(a, axis, 0, 0, tiled=True)  12.9 us
    pallas_call x1, Pallas kernels, terms(): call(body, (jax.ShapeDtypeStruct((n_tok, cols), BF), jax.ShapeDtypeStruct...  12.6 us
    unnamed x26, local copies, waits for them, and re-layouts  8.85 us
    ppermute x14, waiting for transfers between devices, shifted(): return lax.ppermute(a, axis, [(i, (i + step) % n) for i in range(n)])  5.64 us
    pallas_call x2, Pallas kernels, halves(): call(body, tuple((jax.ShapeDtypeStruct((rows // 2, lanes), BF) for _ in a...  4.09 us
    all_to_all x3, waiting for transfers between devices, exchange(): return lax.all_to_all(a, axis, 0, 0, tiled=True)  3.85 us
  transfers between devices with their start and end apart: 23, of which 6 were waited for; matrix products, arithmetic and copies ran while one was open for 4% of the time, Pallas kernels for 34%

profile of v8, /device:TPU:0, one launch (start us, length us, event | category | flops | bytes accessed | tf_op | source)
XLA Modules:
  0.0 115.7 jit_solution(17963774763417580863)
XLA Ops:
  0.7 1.1 constant_dynamic-slice_fusion
  1.7 2.9 %collective-permute-start.3 = (bf16[256,512]{1,0:T(8,128)(2,1)S(1)}, bf16[256,512]{1,0:T(8,128)(2,1)S(1)}, u32[]{:S(2)}, u32[]{:S(2)}) collective-permute-start(bf16[256,512]{1,0:T(8,128)(2,1)S(1)} %get-tuple-element.648.refs_0_), channel_id=1, source_target_pairs={{0,24},{8,0},{16,8},{24,16},{1,25},{9,1},{17,9},{25,17},{2,26},{10... | collective-permute-start | bytes 786440 | tf_op jit(solution)/shard_map/ppermute | solution.py:287
  4.6 0.8 collective-permute-start.2
  5.4 0.5 collective-permute-start.4
  6.0 0.8 copy.24.task_col
  6.8 1.0 collective-permute-start.1
  8.4 0.9 copy.25.tw
  9.2 4.0 %collective-permute-start.8 = (bf16[256,512]{1,0:T(8,128)(2,1)S(1)}, bf16[256,512]{1,0:T(8,128)(2,1)S(1)}, u32[]{:S(2)}, u32[]{:S(2)}) collective-permute-start(bf16[256,512]{1,0:T(8,128)(2,1)S(1)} %collective-permute-done.4.refs_4_), channel_id=1, source_target_pairs={{0,6},{2,0},{4,2},{6,4},{1,7},{3,1},{5,3},{7,5},{8,14},{10,8},{12,... | collective-permute-start | bytes 786440 | tf_op jit(solution)/shard_map/ppermute | solution.py:287
  13.5 2.3 %collective-permute-done.3.refs_3_ = bf16[256,512]{1,0:T(8,128)(2,1)S(1)} collective-permute-done((bf16[256,512]{1,0:T(8,128)(2,1)S(1)}, bf16[256,512]{1,0:T(8,128)(2,1)S(1)}, u32[]{:S(2)}, u32[]{:S(2)}) %collective-permute-start.3) | collective-permute-done | bytes 262176 | tf_op jit(solution)/shard_map/ppermute | solution.py:287
  15.8 1.9 %collective-permute-start.6 = (bf16[256,512]{1,0:T(8,128)(2,1)S(1)}, bf16[256,512]{1,0:T(8,128)(2,1)S(1)}, u32[]{:S(2)}, u32[]{:S(2)}) collective-permute-start(bf16[256,512]{1,0:T(8,128)(2,1)S(1)} %collective-permute-done.4.refs_4_), channel_id=1, source_target_pairs={{0,2},{2,4},{4,6},{6,0},{1,3},{3,5},{5,7},{7,1},{8,10},{10,12},{12... | collective-permute-start | bytes 786440 | tf_op jit(solution)/shard_map/ppermute | solution.py:287
  17.8 12.6 %shard_map.103 = (bf16[512,512]{1,0:T(8,128)(2,1)S(1)}, bf16[4,128,1152]{2,1,0:T(8,128)(2,1)S(1)}, bf16[4,128,1152]{2,1,0:T(8,128)(2,1)S(1)}) custom-call(s32[1]{0:T(128)} %bitcast.8.me, bf16[512,8192]{1,0:T(8,128)(2,1)} %refs_3_.7, bf16[8192,512]{1,0:T(8,128)(2,1)} %dn.1, bf16[1024,512]{1,0:T(8,128)(2,1)} %refs_12_.1, bf16[512,1024]{1,0:T(8,128)(2,1)} %cot, ...), custom_call_target="tpu_custom_call" | custom-call | flops 5368709120 | bytes 25165824 | tf_op jit(solution)/shard_map/pallas_call | solution.py:103
  30.4 1.5 %shard_map.104 = (bf16[1024,512]{1,0:T(8,128)(2,1)}, bf16[1024,512]{1,0:T(8,128)(2,1)}) custom-call(bf16[256,512]{1,0:T(8,128)(2,1)S(1)} %get-tuple-element.648.refs_0_, bf16[256,512]{1,0:T(8,128)(2,1)S(1)} %collective-permute-done.1.refs_1_, bf16[256,512]{1,0:T(8,128)(2,1)S(1)} %collective-permute-done.2.refs_2_, ...), custom_call_target="tpu_custom_call" | custom-call | bytes 4194304 | tf_op jit(solution)/shard_map/pallas_call | solution.py:153
  31.9 2.8 %collective-permute-done.9.b = bf16[4,128,1152]{2,1,0:T(8,128)(2,1)S(1)} collective-permute-done((bf16[4,128,1152]{2,1,0:T(8,128)(2,1)S(1)}, bf16[4,128,1152]{2,1,0:T(8,128)(2,1)S(1)}, u32[]{:S(2)}, u32[]{:S(2)}) %collective-permute-start.9) | collective-permute-done | bytes 1179680 | tf_op jit(solution)/shard_map/ppermute | solution.py:442
  34.7 0.1 collective-permute-start.10
  34.9 0.6 convert_reduce_fusion.2
  36.3 1.7 %shard_map.105 = bf16[4,144,1152]{2,1,0:T(8,128)(2,1)} custom-call(bf16[4,128,1152]{2,1,0:T(8,128)(2,1)S(1)} %get-tuple-element.459.a, bf16[4,128,1152]{2,1,0:T(8,128)(2,1)S(1)} %collective-permute-done.9.b, bf16[16,1152]{1,0:T(8,128)(2,1)S(1)} %select_convert_fusion.1.c), custom_call_target="tpu_custom_call" | custom-call | bytes 10485760 | tf_op jit(solution)/shard_map/pallas_call | solution.py:190
  38.0 5.0 %all-to-all-start.3 = ((bf16[4,144,1152]{2,1,0:T(8,128)(2,1)}), bf16[4,144,1152]{2,1,0:T(8,128)(2,1)S(1)}, u32[]{:S(2)}, u32[]{:S(2)}) async-start(bf16[4,144,1152]{2,1,0:T(8,128)(2,1)} %shard_map.105), calls=%async_computation.3 | async-start | bytes 2654208 | tf_op jit(solution)/shard_map/all_to_all | solution.py:23
  43.1 3.7 %collective-permute-start.14 = (bf16[1024,512]{1,0:T(8,128)(2,1)}, bf16[1024,512]{1,0:T(8,128)(2,1)}, u32[]{:S(2)}, u32[]{:S(2)}) collective-permute-start(bf16[1024,512]{1,0:T(8,128)(2,1)} %get-tuple-element.462.refs_9_), channel_id=1, source_target_pairs={{0,24},{8,0},{16,8},{24,16},{1,25},{9,1},{17,9},{25,17},{2,26},{10... | collective-permute-start | bytes 3145736 | tf_op jit(solution)/shard_map/ppermute | solution.py:287
  46.7 1.5 %collective-permute-done.10.refs_4_.refs_5_.refs_6_.refs_7_ = bf16[512,8192]{1,0:T(8,128)(2,1)} collective-permute-done((bf16[512,8192]{1,0:T(8,128)(2,1)}, bf16[512,8192]{1,0:T(8,128)(2,1)}, u32[]{:S(2)}, u32[]{:S(2)}) %collective-permute-start.10) | collective-permute-done | bytes 8388640 | tf_op jit(solution)/shard_map/ppermute | solution.py:446
  48.2 2.1 %collective-permute-start.12 = (bf16[1024,512]{1,0:T(8,128)(2,1)}, bf16[1024,512]{1,0:T(8,128)(2,1)}, u32[]{:S(2)}, u32[]{:S(2)}) collective-permute-start(bf16[1024,512]{1,0:T(8,128)(2,1)} %get-tuple-element.461.refs_8_), channel_id=1, source_target_pairs={{0,6},{2,0},{4,2},{6,4},{1,7},{3,1},{5,3},{7,5},{8,14},{10,8},{12,... | collective-permute-start | bytes 3145736 | tf_op jit(solution)/shard_map/ppermute | solution.py:287
  50.4 0.2 broadcast_in_dim_reshape.8.ow
  50.7 6.6 %shard_map.106.refs_10_ = f32[1024,512]{1,0:T(8,128)S(1)} custom-call(s32[9]{0:T(128)S(1)} %stack.135.at, bf16[512,8192]{1,0:T(8,128)(2,1)} %refs_3_.7, bf16[512,8192]{1,0:T(8,128)(2,1)} %refs_3_.7, bf16[512,8192]{1,0:T(8,128)(2,1)} %refs_3_.7, bf16[512,8192]{1,0:T(8,128)(2,1)} %refs_3_.7, ...), custom_call_target="tpu_custom_call" | custom-call | flops 2147483648 | bytes 8388608 | tf_op jit(solution)/shard_map/pallas_call | solution.py:345
  57.3 1.4 %copy-done = f32[1024,512]{1,0:T(8,128)} copy-done((f32[1024,512]{1,0:T(8,128)}, f32[1024,512]{1,0:T(8,128)S(1)}, u32[]{:S(2)}) %copy-start) | copy-done | bytes 2097176
  58.7 3.8 %all-to-all-done.3.g = bf16[4,144,1152]{2,1,0:T(8,128)(2,1)S(1)} async-done(((bf16[4,144,1152]{2,1,0:T(8,128)(2,1)}), bf16[4,144,1152]{2,1,0:T(8,128)(2,1)S(1)}, u32[]{:S(2)}, u32[]{:S(2)}) %all-to-all-start.3) | async-done | bytes 1327136 | tf_op jit(solution)/shard_map/all_to_all | solution.py:23
  62.5 2.1 %shard_map.108 = bf16[4,144,1152]{2,1,0:T(8,128)(2,1)S(1)} custom-call(bf16[4,144,1152]{2,1,0:T(8,128)(2,1)S(1)} %all-to-all-done.3.g, f32[512,1]{1,0:T(8,128)S(1)} %broadcast_in_dim_reshape.8.ow), custom_call_target="tpu_custom_call" | custom-call | flops 603979776 | bytes 5242880 | tf_op jit(solution)/shard_map/pallas_call | solution.py:222
  64.6 1.0 copy-done.4
  65.7 4.5 %all-to-all-start.4 = ((bf16[4,144,1152]{2,1,0:T(8,128)(2,1)}), bf16[4,144,1152]{2,1,0:T(8,128)(2,1)S(1)}, u32[]{:S(2)}, u32[]{:S(2)}) async-start(bf16[4,144,1152]{2,1,0:T(8,128)(2,1)} %copy-done.4), calls=%async_computation.4 | async-start | bytes 2654208 | tf_op jit(solution)/shard_map/all_to_all | solution.py:23
  70.2 3.3 %collective-permute-done.13.refs_8_.refs_0_ = bf16[1024,512]{1,0:T(8,128)(2,1)} collective-permute-done((bf16[1024,512]{1,0:T(8,128)(2,1)}, bf16[1024,512]{1,0:T(8,128)(2,1)}, u32[]{:S(2)}, u32[]{:S(2)}) %collective-permute-start.13) | collective-permute-done | bytes 1048608 | tf_op jit(solution)/shard_map/ppermute | solution.py:287
  73.5 2.0 %shard_map.113 = (bf16[512,512]{1,0:T(8,128)(2,1)}, bf16[512,512]{1,0:T(8,128)(2,1)}) custom-call(bf16[1024,512]{1,0:T(8,128)(2,1)} %collective-permute-done.13.refs_8_.refs_0_, bf16[1024,512]{1,0:T(8,128)(2,1)} %collective-permute-done.14.refs_9_.refs_1_), custom_call_target="tpu_custom_call" | custom-call | bytes 4194304 | tf_op jit(solution)/shard_map/pallas_call | solution.py:172
  75.5 3.2 %collective-permute-start.19 = (bf16[512,512]{1,0:T(8,128)(2,1)}, bf16[512,512]{1,0:T(8,128)(2,1)}, u32[]{:S(2)}, u32[]{:S(2)}) collective-permute-start(bf16[512,512]{1,0:T(8,128)(2,1)} %get-tuple-element.478), channel_id=1, source_target_pairs={{0,24},{8,0},{16,8},{24,16},{1,25},{9,1},{17,9},{25,17},{2,26},{10... | collective-permute-start | bytes 1572872 | tf_op jit(solution)/shard_map/ppermute | solution.py:287
  78.8 1.6 %copy-done.1 = f32[1024,512]{1,0:T(8,128)S(1)} copy-done((f32[1024,512]{1,0:T(8,128)S(1)}, f32[1024,512]{1,0:T(8,128)}, u32[]{:S(2)}) %copy-start.1) | copy-done | bytes 2097176
  80.4 5.8 %shard_map.107.refs_10_ = f32[1024,512]{1,0:T(8,128)S(1)} custom-call(s32[8]{0:T(128)S(1)} %stack.126.at, bf16[512,8192]{1,0:T(8,128)(2,1)} %refs_3_.7, bf16[512,8192]{1,0:T(8,128)(2,1)} %refs_3_.7, bf16[512,8192]{1,0:T(8,128)(2,1)} %refs_3_.7, bf16[512,8192]{1,0:T(8,128)(2,1)} %refs_3_.7, ...), custom_call_target="tpu_custom_call" | custom-call | flops 2147483648 | bytes 8388608 | tf_op jit(solution)/shard_map/pallas_call | solution.py:345
  86.2 2.0 %shard_map.112 = (bf16[512,512]{1,0:T(8,128)(2,1)}, bf16[512,512]{1,0:T(8,128)(2,1)}) custom-call(bf16[1024,512]{1,0:T(8,128)(2,1)} %collective-permute-done.11.refs_8_.refs_0_, bf16[1024,512]{1,0:T(8,128)(2,1)} %collective-permute-done.12.refs_9_.refs_1_), custom_call_target="tpu_custom_call" | custom-call | bytes 4194304 | tf_op jit(solution)/shard_map/pallas_call | solution.py:172
  88.3 2.0 %collective-permute-start.16 = (bf16[512,512]{1,0:T(8,128)(2,1)}, bf16[512,512]{1,0:T(8,128)(2,1)}, u32[]{:S(2)}, u32[]{:S(2)}) collective-permute-start(bf16[512,512]{1,0:T(8,128)(2,1)} %get-tuple-element.475), channel_id=1, source_target_pairs={{0,2},{2,4},{4,6},{6,0},{1,3},{3,5},{5,7},{7,1},{8,10},{10,12},{12... | collective-permute-start | bytes 1572872 | tf_op jit(solution)/shard_map/ppermute | solution.py:287
  90.3 1.2 %collective-permute-start.17 = (bf16[512,512]{1,0:T(8,128)(2,1)}, bf16[512,512]{1,0:T(8,128)(2,1)}, u32[]{:S(2)}, u32[]{:S(2)}) collective-permute-start(bf16[512,512]{1,0:T(8,128)(2,1)} %get-tuple-element.476), channel_id=1, source_target_pairs={{0,6},{2,0},{4,2},{6,4},{1,7},{3,1},{5,3},{7,5},{8,14},{10,8},{12,... | collective-permute-start | bytes 1572872 | tf_op jit(solution)/shard_map/ppermute | solution.py:287
  91.5 0.2 shard_map.109
  91.7 0.7 copy-done.5
  92.4 3.5 %all-to-all-start.5 = ((bf16[4,304,128]{2,1,0:T(8,128)(2,1)}), bf16[4,304,128]{2,1,0:T(8,128)(2,1)S(1)}, u32[]{:S(2)}, u32[]{:S(2)}) async-start(bf16[4,304,128]{2,1,0:T(8,128)(2,1)} %copy-done.5), calls=%async_computation.5 | async-start | bytes 622592 | tf_op jit(solution)/shard_map/all_to_all | solution.py:23
  96.2 5.8 %shard_map.110.refs_12_ = f32[1024,512]{1,0:T(8,128)S(1)} custom-call(s32[8]{0:T(128)S(1)} %stack.117.at, bf16[512,8192]{1,0:T(8,128)(2,1)} %refs_3_.7, bf16[512,8192]{1,0:T(8,128)(2,1)} %refs_3_.7, bf16[512,8192]{1,0:T(8,128)(2,1)} %refs_3_.7, bf16[512,8192]{1,0:T(8,128)(2,1)} %refs_3_.7, ...), custom_call_target="tpu_custom_call" | custom-call | flops 2147483648 | bytes 8388608 | tf_op jit(solution)/shard_map/pallas_call | solution.py:345
  102.0 1.4 %copy-done.2 = f32[1024,512]{1,0:T(8,128)} copy-done((f32[1024,512]{1,0:T(8,128)}, f32[1024,512]{1,0:T(8,128)S(1)}, u32[]{:S(2)}) %copy-start.2) | copy-done | bytes 2097176
  103.4 1.6 %copy-done.3 = f32[1024,512]{1,0:T(8,128)S(1)} copy-done((f32[1024,512]{1,0:T(8,128)S(1)}, f32[1024,512]{1,0:T(8,128)}, u32[]{:S(2)}) %copy-start.3) | copy-done | bytes 2097176
  105.0 5.8 %shard_map.114 = (bf16[512,512]{1,0:T(8,128)(2,1)S(1)}, bf16[512,512]{1,0:T(8,128)(2,1)S(1)}) custom-call(s32[8]{0:T(128)S(1)} %stack.144.at, bf16[512,8192]{1,0:T(8,128)(2,1)} %refs_3_.7, bf16[512,8192]{1,0:T(8,128)(2,1)} %refs_3_.7, bf16[512,8192]{1,0:T(8,128)(2,1)} %refs_3_.7, bf16[512,8192]{1,0:T(8,128)(2,1)} %refs_3_.7, ...), custom_call_target="tpu_custom_call" | custom-call | flops 2147483648 | bytes 8388608 | tf_op jit(solution)/shard_map/pallas_call | solution.py:345
  110.9 0.5 slice.11
  111.4 1.3 %collective-permute-done.20 = bf16[512,512]{1,0:T(8,128)(2,1)S(1)} collective-permute-done((bf16[512,512]{1,0:T(8,128)(2,1)S(1)}, bf16[512,512]{1,0:T(8,128)(2,1)S(1)}, u32[]{:S(2)}, u32[]{:S(2)}) %collective-permute-start.20) | collective-permute-done | bytes 524320 | tf_op jit(solution)/shard_map/ppermute | solution.py:475
  112.9 1.1 pad_maximum_fusion
  114.0 0.5 copy-done.7
  114.5 0.6 while.20
  115.1 0.6 copy-done.6
  (68 shorter events, 1.7 us)
Async XLA Ops:
  0.6 7.2 %copy-start.11 = (s32[512]{0:T(512)S(1)}, s32[512]{0:T(512)}, u32[]{:S(2)}) copy-start(s32[512]{0:T(512)} %param.15) | copy-start | bytes 6148
  0.6 7.4 %copy-start.12 = (s32[8]{0:T(128)S(1)}, s32[8]{0:T(128)}, u32[]{:S(2)}) copy-start(s32[8]{0:T(128)} %param.17) | copy-start | bytes 100
  1.7 14.1 %collective-permute-start.3 = (bf16[256,512]{1,0:T(8,128)(2,1)S(1)}, bf16[256,512]{1,0:T(8,128)(2,1)S(1)}, u32[]{:S(2)}, u32[]{:S(2)}) collective-permute-start(bf16[256,512]{1,0:T(8,128)(2,1)S(1)} %get-tuple-element.648.refs_0_), channel_id=1, source_target_pairs={{0,24},{8,0},{16,8},{24,16},{1,25},{9,1},{17,9},{25,17},{2,26},{10... | collective-permute-start | bytes 786440 | tf_op jit(solution)/shard_map/ppermute | solution.py:287
  4.6 25.7 %collective-permute-start.2 = (bf16[256,512]{1,0:T(8,128)(2,1)S(1)}, bf16[256,512]{1,0:T(8,128)(2,1)S(1)}, u32[]{:S(2)}, u32[]{:S(2)}) collective-permute-start(bf16[256,512]{1,0:T(8,128)(2,1)S(1)} %get-tuple-element.648.refs_0_), channel_id=1, source_target_pairs={{0,16},{8,24},{16,0},{24,8},{1,17},{9,25},{17,1},{25,9},{2,18},{10... | collective-permute-start | bytes 786440 | tf_op jit(solution)/shard_map/ppermute | solution.py:287
  5.4 2.4 %collective-permute-start.5 = (s32[512]{0:T(512)}, s32[512]{0:T(512)S(1)}, u32[]{:S(2)}, u32[]{:S(2)}) collective-permute-start(s32[512]{0:T(512)} %param.15), channel_id=1, source_target_pairs={{0,1},{1,0},{2,3},{3,2},{4,5},{5,4},{6,7},{7,6},{8,9},{9,8},{10,11... | collective-permute-start | bytes 6152 | tf_op jit(solution)/shard_map/ppermute | solution.py:380
  5.4 2.4 %collective-permute-start.4 = (bf16[256,512]{1,0:T(8,128)(2,1)S(1)}, bf16[256,512]{1,0:T(8,128)(2,1)S(1)}, u32[]{:S(2)}, u32[]{:S(2)}) collective-permute-start(bf16[256,512]{1,0:T(8,128)(2,1)S(1)} %get-tuple-element.647), channel_id=1, source_target_pairs={{0,1},{1,0},{2,3},{3,2},{4,5},{5,4},{6,7},{7,6},{8,9},{9,8},{10,11... | collective-permute-start | bytes 786440 | tf_op jit(solution)/shard_map/ppermute | solution.py:379
  6.8 23.5 %collective-permute-start.1 = (bf16[256,512]{1,0:T(8,128)(2,1)S(1)}, bf16[256,512]{1,0:T(8,128)(2,1)S(1)}, u32[]{:S(2)}, u32[]{:S(2)}) collective-permute-start(bf16[256,512]{1,0:T(8,128)(2,1)S(1)} %get-tuple-element.648.refs_0_), channel_id=1, source_target_pairs={{0,8},{8,16},{16,24},{24,0},{1,9},{9,17},{17,25},{25,1},{2,10},{10... | collective-permute-start | bytes 786440 | tf_op jit(solution)/shard_map/ppermute | solution.py:287
  9.2 21.1 %collective-permute-start.8 = (bf16[256,512]{1,0:T(8,128)(2,1)S(1)}, bf16[256,512]{1,0:T(8,128)(2,1)S(1)}, u32[]{:S(2)}, u32[]{:S(2)}) collective-permute-start(bf16[256,512]{1,0:T(8,128)(2,1)S(1)} %collective-permute-done.4.refs_4_), channel_id=1, source_target_pairs={{0,6},{2,0},{4,2},{6,4},{1,7},{3,1},{5,3},{7,5},{8,14},{10,8},{12,... | collective-permute-start | bytes 786440 | tf_op jit(solution)/shard_map/ppermute | solution.py:287
  13.4 17.0 %collective-permute-start.7 = (bf16[256,512]{1,0:T(8,128)(2,1)S(1)}, bf16[256,512]{1,0:T(8,128)(2,1)S(1)}, u32[]{:S(2)}, u32[]{:S(2)}) collective-permute-start(bf16[256,512]{1,0:T(8,128)(2,1)S(1)} %collective-permute-done.4.refs_4_), channel_id=1, source_target_pairs={{0,4},{2,6},{4,0},{6,2},{1,5},{3,7},{5,1},{7,3},{8,12},{10,14},{12... | collective-permute-start | bytes 786440 | tf_op jit(solution)/shard_map/ppermute | solution.py:287
  15.8 14.6 %collective-permute-start.6 = (bf16[256,512]{1,0:T(8,128)(2,1)S(1)}, bf16[256,512]{1,0:T(8,128)(2,1)S(1)}, u32[]{:S(2)}, u32[]{:S(2)}) collective-permute-start(bf16[256,512]{1,0:T(8,128)(2,1)S(1)} %collective-permute-done.4.refs_4_), channel_id=1, source_target_pairs={{0,2},{2,4},{4,6},{6,0},{1,3},{3,5},{5,7},{7,1},{8,10},{10,12},{12... | collective-permute-start | bytes 786440 | tf_op jit(solution)/shard_map/ppermute | solution.py:287
  31.9 2.8 %collective-permute-start.9 = (bf16[4,128,1152]{2,1,0:T(8,128)(2,1)S(1)}, bf16[4,128,1152]{2,1,0:T(8,128)(2,1)S(1)}, u32[]{:S(2)}, u32[]{:S(2)}) collective-permute-start(bf16[4,128,1152]{2,1,0:T(8,128)(2,1)S(1)} %get-tuple-element.457), channel_id=1, source_target_pairs={{0,1},{1,0},{2,3},{3,2},{4,5},{5,4},{6,7},{7,6},{8,9},{9,8},{10,11... | collective-permute-start | bytes 3538952 | tf_op jit(solution)/shard_map/ppermute | solution.py:442
  34.7 13.5 %collective-permute-start.10 = (bf16[512,8192]{1,0:T(8,128)(2,1)}, bf16[512,8192]{1,0:T(8,128)(2,1)}, u32[]{:S(2)}, u32[]{:S(2)}) collective-permute-start(bf16[512,8192]{1,0:T(8,128)(2,1)} %refs_3_.7), channel_id=1, source_target_pairs={{0,1},{1,0},{2,3},{3,2},{4,5},{5,4},{6,7},{7,6},{8,9},{9,8},{10,11... | collective-permute-start | bytes 25165832 | tf_op jit(solution)/shard_map/ppermute | solution.py:446
  38.0 12.4 %copy-start.13 = (s32[8]{0:T(128)S(1)}, s32[8]{0:T(128)}, u32[]{:S(2)}) copy-start(s32[8]{0:T(128)} %param.16) | copy-start | bytes 100
  38.0 24.5 %all-to-all-start.3 = ((bf16[4,144,1152]{2,1,0:T(8,128)(2,1)}), bf16[4,144,1152]{2,1,0:T(8,128)(2,1)S(1)}, u32[]{:S(2)}, u32[]{:S(2)}) async-start(bf16[4,144,1152]{2,1,0:T(8,128)(2,1)} %shard_map.105), calls=%async_computation.3 | async-start | bytes 2654208 | tf_op jit(solution)/shard_map/all_to_all | solution.py:23
  43.0 7.7 %collective-permute-start.15 = (bf16[512,512]{1,0:T(8,128)(2,1)S(1)}, bf16[512,512]{1,0:T(8,128)(2,1)S(1)}, u32[]{:S(2)}, u32[]{:S(2)}) collective-permute-start(bf16[512,512]{1,0:T(8,128)(2,1)S(1)} %get-tuple-element.463.refs_10_), channel_id=1, source_target_pairs={{0,1},{1,0},{2,3},{3,2},{4,5},{5,4},{6,7},{7,6},{8,9},{9,8},{10,11... | collective-permute-start | bytes 1572872 | tf_op jit(solution)/shard_map/ppermute | solution.py:443
  43.1 27.1 %collective-permute-start.14 = (bf16[1024,512]{1,0:T(8,128)(2,1)}, bf16[1024,512]{1,0:T(8,128)(2,1)}, u32[]{:S(2)}, u32[]{:S(2)}) collective-permute-start(bf16[1024,512]{1,0:T(8,128)(2,1)} %get-tuple-element.462.refs_9_), channel_id=1, source_target_pairs={{0,24},{8,0},{16,8},{24,16},{1,25},{9,1},{17,9},{25,17},{2,26},{10... | collective-permute-start | bytes 3145736 | tf_op jit(solution)/shard_map/ppermute | solution.py:287
  46.7 26.8 %collective-permute-start.13 = (bf16[1024,512]{1,0:T(8,128)(2,1)}, bf16[1024,512]{1,0:T(8,128)(2,1)}, u32[]{:S(2)}, u32[]{:S(2)}) collective-permute-start(bf16[1024,512]{1,0:T(8,128)(2,1)} %get-tuple-element.462.refs_9_), channel_id=1, source_target_pairs={{0,8},{8,16},{16,24},{24,0},{1,9},{9,17},{17,25},{25,1},{2,10},{10... | collective-permute-start | bytes 3145736 | tf_op jit(solution)/shard_map/ppermute | solution.py:287
  48.2 38.0 %collective-permute-start.12 = (bf16[1024,512]{1,0:T(8,128)(2,1)}, bf16[1024,512]{1,0:T(8,128)(2,1)}, u32[]{:S(2)}, u32[]{:S(2)}) collective-permute-start(bf16[1024,512]{1,0:T(8,128)(2,1)} %get-tuple-element.461.refs_8_), channel_id=1, source_target_pairs={{0,6},{2,0},{4,2},{6,4},{1,7},{3,1},{5,3},{7,5},{8,14},{10,8},{12,... | collective-permute-start | bytes 3145736 | tf_op jit(solution)/shard_map/ppermute | solution.py:287
  50.4 35.9 %collective-permute-start.11 = (bf16[1024,512]{1,0:T(8,128)(2,1)}, bf16[1024,512]{1,0:T(8,128)(2,1)}, u32[]{:S(2)}, u32[]{:S(2)}) collective-permute-start(bf16[1024,512]{1,0:T(8,128)(2,1)} %get-tuple-element.461.refs_8_), channel_id=1, source_target_pairs={{0,2},{2,4},{4,6},{6,0},{1,3},{3,5},{5,7},{7,1},{8,10},{10,12},{12... | collective-permute-start | bytes 3145736 | tf_op jit(solution)/shard_map/ppermute | solution.py:287
  57.3 1.4 %copy-start = (f32[1024,512]{1,0:T(8,128)}, f32[1024,512]{1,0:T(8,128)S(1)}, u32[]{:S(2)}) copy-start(f32[1024,512]{1,0:T(8,128)S(1)} %shard_map.106.refs_10_) | copy-start | bytes 6291460
  64.6 1.1 copy-start.4
  65.7 25.8 %all-to-all-start.4 = ((bf16[4,144,1152]{2,1,0:T(8,128)(2,1)}), bf16[4,144,1152]{2,1,0:T(8,128)(2,1)S(1)}, u32[]{:S(2)}, u32[]{:S(2)}) async-start(bf16[4,144,1152]{2,1,0:T(8,128)(2,1)} %copy-done.4), calls=%async_computation.4 | async-start | bytes 2654208 | tf_op jit(solution)/shard_map/all_to_all | solution.py:23
  75.5 27.8 %collective-permute-start.18 = (bf16[512,512]{1,0:T(8,128)(2,1)}, bf16[512,512]{1,0:T(8,128)(2,1)}, u32[]{:S(2)}, u32[]{:S(2)}) collective-permute-start(bf16[512,512]{1,0:T(8,128)(2,1)} %get-tuple-element.477), channel_id=1, source_target_pairs={{0,8},{8,16},{16,24},{24,0},{1,9},{9,17},{17,25},{25,1},{2,10},{10... | collective-permute-start | bytes 1572872 | tf_op jit(solution)/shard_map/ppermute | solution.py:287
  75.5 27.8 %collective-permute-start.19 = (bf16[512,512]{1,0:T(8,128)(2,1)}, bf16[512,512]{1,0:T(8,128)(2,1)}, u32[]{:S(2)}, u32[]{:S(2)}) collective-permute-start(bf16[512,512]{1,0:T(8,128)(2,1)} %get-tuple-element.478), channel_id=1, source_target_pairs={{0,24},{8,0},{16,8},{24,16},{1,25},{9,1},{17,9},{25,17},{2,26},{10... | collective-permute-start | bytes 1572872 | tf_op jit(solution)/shard_map/ppermute | solution.py:287
  78.8 1.6 %copy-start.1 = (f32[1024,512]{1,0:T(8,128)S(1)}, f32[1024,512]{1,0:T(8,128)}, u32[]{:S(2)}) copy-start(f32[1024,512]{1,0:T(8,128)} %copy-done) | copy-start | bytes 6291460
  88.3 15.1 %collective-permute-start.16 = (bf16[512,512]{1,0:T(8,128)(2,1)}, bf16[512,512]{1,0:T(8,128)(2,1)}, u32[]{:S(2)}, u32[]{:S(2)}) collective-permute-start(bf16[512,512]{1,0:T(8,128)(2,1)} %get-tuple-element.475), channel_id=1, source_target_pairs={{0,2},{2,4},{4,6},{6,0},{1,3},{3,5},{5,7},{7,1},{8,10},{10,12},{12... | collective-permute-start | bytes 1572872 | tf_op jit(solution)/shard_map/ppermute | solution.py:287
  90.3 13.1 %collective-permute-start.17 = (bf16[512,512]{1,0:T(8,128)(2,1)}, bf16[512,512]{1,0:T(8,128)(2,1)}, u32[]{:S(2)}, u32[]{:S(2)}) collective-permute-start(bf16[512,512]{1,0:T(8,128)(2,1)} %get-tuple-element.476), channel_id=1, source_target_pairs={{0,6},{2,0},{4,2},{6,4},{1,7},{3,1},{5,3},{7,5},{8,14},{10,8},{12,... | collective-permute-start | bytes 1572872 | tf_op jit(solution)/shard_map/ppermute | solution.py:287
  91.7 0.7 copy-start.5
  92.4 10.9 %all-to-all-start.5 = ((bf16[4,304,128]{2,1,0:T(8,128)(2,1)}), bf16[4,304,128]{2,1,0:T(8,128)(2,1)S(1)}, u32[]{:S(2)}, u32[]{:S(2)}) async-start(bf16[4,304,128]{2,1,0:T(8,128)(2,1)} %copy-done.5), calls=%async_computation.5 | async-start | bytes 622592 | tf_op jit(solution)/shard_map/all_to_all | solution.py:23
  102.0 1.4 %copy-start.2 = (f32[1024,512]{1,0:T(8,128)}, f32[1024,512]{1,0:T(8,128)S(1)}, u32[]{:S(2)}) copy-start(f32[1024,512]{1,0:T(8,128)S(1)} %shard_map.110.refs_12_) | copy-start | bytes 6291460
  103.4 1.6 %copy-start.3 = (f32[1024,512]{1,0:T(8,128)S(1)}, f32[1024,512]{1,0:T(8,128)}, u32[]{:S(2)}) copy-start(f32[1024,512]{1,0:T(8,128)} %copy-done.2) | copy-start | bytes 6291460
  110.8 2.0 %collective-permute-start.20 = (bf16[512,512]{1,0:T(8,128)(2,1)S(1)}, bf16[512,512]{1,0:T(8,128)(2,1)S(1)}, u32[]{:S(2)}, u32[]{:S(2)}) collective-permute-start(bf16[512,512]{1,0:T(8,128)(2,1)S(1)} %get-tuple-element.481), channel_id=1, source_target_pairs={{0,1},{1,0},{2,3},{3,2},{4,5},{5,4},{6,7},{7,6},{8,9},{9,8},{10,11... | collective-permute-start | bytes 1572872 | tf_op jit(solution)/shard_map/ppermute | solution.py:475
  112.9 1.6 %copy-start.7 = (bf16[1024,512]{1,0:T(8,128)(2,1)S(1)}, bf16[1024,512]{1,0:T(8,128)(2,1)}, u32[]{:S(2)}) copy-start(bf16[1024,512]{1,0:T(8,128)(2,1)} %refs_12_.1) | copy-start | bytes 3145732
  112.9 1.6 %copy-start.10 = (f32[512,1]{1,0:T(8,128)S(1)}, f32[512,1]{1,0:T(8,128)}, u32[]{:S(2)}) copy-start(f32[512,1]{1,0:T(8,128)} %copy.25.tw) | copy-start | bytes 6148
  115.1 0.7 copy-start.6
  115.1 0.6 copy-start.9
